TPU v7x, 32 devices: a whole 2x2x4 slice. The times are simulated.
32 devices in a mesh: rows: 8 (over z, y), grp: 4 (over x, core).
Axes of the slice: x: 2, y: 2, z: 4, core: 2. Of those that a mesh axis runs over, the one named last changes fastest.
Arguments:
- features: bfloat16 [15456, 512], P('rows', 'grp'), may hold values from -40 to 40
- image_group: int32 [6], replicated, may hold values from 0 to 2, as said below
- switches: int32 [3864], P('rows'), may hold values from 0 to 3
- enc_weight: bfloat16 [3, 9, 512, 512], P(None, None, 'rows', 'grp'), may hold values from -0.09375 to 0.09375
- dec_weight: bfloat16 [3, 9, 512, 512], P(None, None, 'rows', 'grp'), may hold values from -0.09375 to 0.09375
- enc_gain: float32 [3, 512], P(None, 'grp'), may hold values from 0.25 to 1.75
- enc_bias: float32 [3, 512], P(None, 'grp'), may hold values from -2 to 2
- dec_gain: float32 [3, 512], P(None, 'grp'), may hold values from 0.25 to 1.75
- dec_bias: float32 [3, 512], P(None, 'grp'), may hold values from -2 to 2
- d_decoded: bfloat16 [15456, 512], P('rows', 'grp'), may hold values from -6 to 6
Outputs:
- decoded: bfloat16 [15456, 512], P('rows', 'grp')
- features_grad: bfloat16 [15456, 512], P('rows', 'grp')
- enc_weight_grad: float32 [3, 9, 512, 512], P(None, None, 'rows', 'grp')
- dec_weight_grad: float32 [3, 9, 512, 512], P(None, None, 'rows', 'grp')
- enc_gain_grad: float32 [3, 512], P(None, 'grp')
- enc_bias_grad: float32 [3, 512], P(None, 'grp')
- dec_gain_grad: float32 [3, 512], P(None, 'grp')
- dec_bias_grad: float32 [3, 512], P(None, 'grp')
Inputs may be any that keep to these rules, and one draw needn't show every extreme that they name: `image_group`: each of the three sizes names exactly 2 images.
All inputs are finite; a program needn't handle non-finite values.
Results may differ from a plain program's by a relative error of at most 0.033.
Values may be sent and summed in bfloat16 or wider, within the bound.
A program may use at most 320 MiB of HBM per device.

v0:
```python
import jax
import jax.numpy as jnp
from jax import lax
from jax.sharding import PartitionSpec as P

H1 = 15
W1 = 20
H2 = 18
W2 = 24
H3 = 30
W3 = 40
HALO = 164


EPSILON = 1e-05


def padded_2(block, sides, width):
    for axis, dim in sides:
        count = lax.axis_size(axis)
        forward = [(i, i + 1) for i in range(count - 1)]
        backward = [(target, source) for source, target in forward]
        low = lax.ppermute(
            lax.slice_in_dim(block, block.shape[dim] - width, None, axis=dim), axis, forward
        )
        high = lax.ppermute(lax.slice_in_dim(block, 0, width, axis=dim), axis, backward)
        block = jnp.concatenate([low, block, high], axis=dim)
    return block


def neighbours(image_group, first_window, window_count):
    choices_table = jnp.arange(3, dtype=jnp.int32)
    selected = (image_group[:, None] == choices_table[None, :]).astype(jnp.int32)
    heights = jnp.sum(selected * jnp.array([H1, H2, H3], jnp.int32)[None, :], axis=1)
    widths = jnp.sum(selected * jnp.array([W1, W2, W3], jnp.int32)[None, :], axis=1)
    window_areas = heights * widths
    image_ends = jnp.cumsum(window_areas)
    image_starts = image_ends - window_areas
    windows = first_window + jnp.arange(window_count, dtype=jnp.int32)
    membership = (
        (windows[:, None] >= image_starts[None, :]) & (windows[:, None] < image_ends[None, :])
    ).astype(jnp.int32)
    image_base = jnp.sum(membership * image_starts[None, :], axis=1)
    image_height = jnp.sum(membership * heights[None, :], axis=1)
    image_width = jnp.sum(membership * widths[None, :], axis=1)
    local_pos = windows - image_base
    pool_row = local_pos // image_width
    pool_column = local_pos % image_width
    quarter = jnp.arange(4, dtype=jnp.int32)
    pixel_row = (2 * pool_row[:, None] + quarter[None, :] // 2).reshape(-1)
    pixel_column = (2 * pool_column[:, None] + quarter[None, :] % 2).reshape(-1)
    pixel_height = jnp.repeat(2 * image_height, 4)
    pixel_width = jnp.repeat(2 * image_width, 4)
    pixel_base = jnp.repeat(image_base, 4)
    tap_list = []
    for row_step in (-1, 0, 1):
        for column_step in (-1, 0, 1):
            next_row = pixel_row + row_step
            next_column = pixel_column + column_step
            inside = (
                (next_row >= 0)
                & (next_row < pixel_height)
                & (next_column >= 0)
                & (next_column < pixel_width)
            )
            target = (
                4 * (pixel_base + next_row // 2 * (pixel_width // 2) + next_column // 2)
                + 2 * (next_row % 2)
                + next_column % 2
            )
            tap_list.append(jnp.where(inside, target, -1))
    return jnp.stack(tap_list)


def convolve(field_low, kernels, gather_index):
    padded = padded_2(field_low, (("rows", 0),), HALO)
    empty = jnp.zeros((field_low.shape[0], kernels.shape[2]), jnp.float32)
    carry = empty
    piece = lax.all_gather(padded, "grp", axis=1, tiled=True)
    for tap_number in range(9):
        taken = jnp.take(piece, gather_index[tap_number], axis=0, mode="fill", fill_value=0)
        kernel_rows = kernels[tap_number]
        carry = carry + jnp.dot(taken, kernel_rows, preferred_element_type=jnp.float32)
    return (carry, padded)


def normalize(conv_out, gain, shift_bias, pixel_total):
    sums, squares = lax.psum(
        (jnp.sum(conv_out, axis=0), jnp.sum(conv_out * conv_out, axis=0)), "rows"
    )
    average = sums / pixel_total
    inverse = lax.rsqrt(squares / pixel_total - average * average + EPSILON)
    normed = (conv_out - average) * inverse
    shifted = gain * normed + shift_bias
    return (jax.nn.silu(shifted), (normed, inverse, shifted))


def run_block(field_low, kernels, gains, shifts, gather_index, pixel_total):
    saved = []
    activation = None
    for layer_number in range(3):
        conv_out, padded = convolve(field_low, kernels[layer_number], gather_index)
        activation, stats = normalize(
            conv_out, gains[layer_number], shifts[layer_number], pixel_total
        )
        saved.append((padded,) + stats)
        field_low = activation.astype(jnp.bfloat16)
    return (activation, saved)


def layer_back(grad_act, saved_item, kernels, gain, gather_index, mirror_index, pixel_total):
    padded, normed, inverse, shifted = saved_item
    sigmoid_part = jax.nn.sigmoid(shifted)
    grad_shift = grad_act * sigmoid_part * (1.0 + shifted * (1.0 - sigmoid_part))
    bias_grad, gain_grad = lax.psum(
        (jnp.sum(grad_shift, axis=0), jnp.sum(grad_shift * normed, axis=0)), "rows"
    )
    grad_conv = (
        inverse * gain * (grad_shift - bias_grad / pixel_total - normed * gain_grad / pixel_total)
    )
    grad_low = grad_conv.astype(jnp.bfloat16)
    piece = lax.all_gather(padded, "grp", axis=1, tiled=True)
    tap_grads = []
    for weight_tap_number in range(9):
        weight_taken = jnp.take(
            piece, gather_index[weight_tap_number], axis=0, mode="fill", fill_value=0
        )
        tap_grads.append(
            jnp.einsum("pi,po->io", weight_taken, grad_low, preferred_element_type=jnp.float32)
        )
    kernel_grad = jnp.stack(tap_grads)
    grad_padded = padded_2(grad_low, (("rows", 0),), HALO)
    partial_sum = jnp.zeros((grad_low.shape[0], kernels.shape[1]), jnp.float32)
    for tap_number in range(9):
        taken = jnp.take(grad_padded, mirror_index[tap_number], axis=0, mode="fill", fill_value=0)
        partial_sum = partial_sum + jnp.einsum(
            "po,io->pi", taken, kernels[tap_number], preferred_element_type=jnp.float32
        )
    input_grad = lax.psum_scatter(
        partial_sum.astype(jnp.bfloat16), "grp", scatter_dimension=1, tiled=True
    ).astype(jnp.float32)
    return (input_grad, kernel_grad, gain_grad, bias_grad)


def block_back(grad_act, saved, kernels, gains, gather_index, mirror_index, pixel_total):
    kernel_list, gain_list, bias_list = ([None] * 3, [None] * 3, [None] * 3)
    for layer_number in (2, 1, 0):
        grad_act, kernel_list[layer_number], gain_list[layer_number], bias_list[layer_number] = (
            layer_back(
                grad_act,
                saved[layer_number],
                kernels[layer_number],
                gains[layer_number],
                gather_index,
                mirror_index,
                pixel_total,
            )
        )
    return (grad_act, jnp.stack(kernel_list), jnp.stack(gain_list), jnp.stack(bias_list))


def shards(
    features,
    image_group,
    switches,
    enc_weight,
    dec_weight,
    enc_gain,
    enc_bias,
    dec_gain,
    dec_bias,
    d_decoded,
):
    pixel_count = features.shape[0]
    window_count = pixel_count // 4
    pixel_total = float(pixel_count * lax.axis_size("rows"))
    first_window = lax.axis_index("rows") * window_count
    tap_index = neighbours(image_group, first_window, window_count)
    sentinel = pixel_count + 2 * HALO
    gather_index = jnp.where(tap_index < 0, sentinel, tap_index - (4 * first_window - HALO))
    mirror_index = gather_index[::-1]
    hits = (switches[:, None] == jnp.arange(4, dtype=jnp.int32)[None, :]).astype(jnp.float32)
    enc_full, dec_full = (
        lax.all_gather(enc_weight, "rows", axis=2, tiled=True),
        lax.all_gather(dec_weight, "rows", axis=2, tiled=True),
    )
    enc_last, enc_saved = run_block(
        features, enc_full, enc_gain, enc_bias, gather_index, pixel_total
    )
    blocks = enc_last.reshape(window_count, 4, -1)
    pooled = jnp.log(jnp.mean(jnp.exp(blocks), axis=1))
    unpooled = (pooled[:, None, :] * hits[:, :, None]).reshape(pixel_count, -1).astype(jnp.bfloat16)
    dec_last, dec_saved = run_block(
        unpooled, dec_full, dec_gain, dec_bias, gather_index, pixel_total
    )
    decoded = dec_last.astype(jnp.bfloat16)
    grad_unpooled, dec_kernel_grad, dec_gain_grad, dec_bias_grad = block_back(
        d_decoded.astype(jnp.float32),
        dec_saved,
        dec_full,
        dec_gain,
        gather_index,
        mirror_index,
        pixel_total,
    )
    grad_pooled = jnp.sum(grad_unpooled.reshape(window_count, 4, -1) * hits[:, :, None], axis=1)
    features_again, grad_tied = lax.optimization_barrier((features, grad_pooled))
    enc_last, enc_saved = run_block(
        features_again, enc_full, enc_gain, enc_bias, gather_index, pixel_total
    )
    grad_pooled = grad_tied
    blocks = enc_last.reshape(window_count, 4, -1)
    pooled = jnp.log(jnp.mean(jnp.exp(blocks), axis=1))
    softmax_share = jnp.exp(blocks - pooled[:, None, :]) * 0.25
    grad_last = (grad_pooled[:, None, :] * softmax_share).reshape(pixel_count, -1)
    grad_input, enc_kernel_grad, enc_gain_grad, enc_bias_grad = block_back(
        grad_last, enc_saved, enc_full, enc_gain, gather_index, mirror_index, pixel_total
    )
    enc_weight_grad, dec_weight_grad = (
        lax.psum_scatter(enc_kernel_grad, "rows", scatter_dimension=2, tiled=True),
        lax.psum_scatter(dec_kernel_grad, "rows", scatter_dimension=2, tiled=True),
    )
    return (
        decoded,
        grad_input.astype(jnp.bfloat16),
        enc_weight_grad,
        dec_weight_grad,
        enc_gain_grad,
        enc_bias_grad,
        dec_gain_grad,
        dec_bias_grad,
    )


def solution(mesh):
    in_specs = (
        P("rows", "grp"),
        P(),
        P("rows"),
        P(None, None, "rows", "grp"),
        P(None, None, "rows", "grp"),
        P(None, "grp"),
        P(None, "grp"),
        P(None, "grp"),
        P(None, "grp"),
        P("rows", "grp"),
    )
    out_specs = (
        P("rows", "grp"),
        P("rows", "grp"),
        P(None, None, "rows", "grp"),
        P(None, None, "rows", "grp"),
        P(None, "grp"),
        P(None, "grp"),
        P(None, "grp"),
        P(None, "grp"),
    )
    return jax.shard_map(shards, mesh=mesh, in_specs=in_specs, out_specs=out_specs, check_vma=False)
```

profile of v0, /device:TPU:9, one launch (start us, length us, event | category | flops | bytes accessed | tf_op | source)
XLA Modules:
  0.0 2693.4 jit_solution(6654409811752434208)
XLA Ops:
  26.1 21.5 all-gather.12.cloned.1.call-done
  47.6 11.8 gather_fusion.8
  59.5 9.1 gather_fusion.7
  95.9 9.2 gather_fusion.3
  114.2 9.1 gather_fusion.1
  149.2 14.9 all-reduce.14
  178.0 26.8 all-gather.16.cloned.1.call-done
  204.9 11.5 gather_fusion.17
  216.3 9.1 gather_fusion.16
  252.8 9.2 gather_fusion.12
  306.1 14.9 all-reduce.13
  335.8 26.0 all-gather.18.cloned.1.call-done
  361.8 11.5 gather_fusion.26
  373.3 9.1 gather_fusion.25
  409.8 9.2 gather_fusion.21
  428.0 9.1 gather_fusion.19
  463.1 14.9 all-reduce.12
  494.9 25.7 all-gather.20.cloned.1.call-done
  520.6 11.7 gather_fusion.35
  541.4 9.1 gather_fusion.33
  622.0 14.9 all-reduce.11
  650.9 26.8 all-gather.24.cloned.1.call-done
  677.7 11.4 gather_fusion.44
  689.1 9.2 gather_fusion.43
  778.9 14.9 all-reduce.10
  807.7 26.8 all-gather.26.cloned.1.call-done
  834.5 11.5 gather_fusion.53
  855.2 9.2 gather_fusion.51
  882.6 9.2 gather_fusion.48
  935.9 14.9 all-reduce.9
  952.4 13.6 all-reduce.8
  1070.3 9.3 add_convert_fusion.5
  1083.5 37.1 %reduce-scatter.25.cloned.1.call-done = bf16[128,1932]{1,0:T(8,128)(2,1)} async-done(((bf16[512,1932]{1,0:T(8,128)(2,1)}), bf16[128,1932]{1,0:T(8,128)(2,1)}) %reduce-scatter.25.cloned.1.call-update) | async-done | bytes 494608
  1122.5 14.9 all-reduce.7
  1237.0 9.3 add_convert_fusion.4
  1250.2 34.2 %reduce-scatter.27.cloned.1.call-done = bf16[128,1932]{1,0:T(8,128)(2,1)} async-done(((bf16[512,1932]{1,0:T(8,128)(2,1)}), bf16[128,1932]{1,0:T(8,128)(2,1)}) %reduce-scatter.27.cloned.1.call-update) | async-done | bytes 494608
  1286.4 14.9 all-reduce.6
  1400.9 9.3 add_convert_fusion.3
  1414.1 34.2 %reduce-scatter.29.cloned.1.call-done = bf16[128,1932]{1,0:T(8,128)(2,1)} async-done(((bf16[512,1932]{1,0:T(8,128)(2,1)}), bf16[128,1932]{1,0:T(8,128)(2,1)}) %reduce-scatter.29.cloned.1.call-update) | async-done | bytes 494608
  1463.6 25.2 all-gather.28.cloned.1.call-done
  1488.8 11.7 gather_fusion.89
  1500.5 9.2 gather_fusion.88
  1509.6 9.2 gather_fusion.87
  1590.3 14.9 all-reduce.5
  1619.3 26.8 all-gather.30.cloned.1.call-done
  1646.1 11.5 gather_fusion.98
  1703.2 9.2 gather_fusion.92
  1747.4 14.9 all-reduce.4
  1776.8 26.3 all-gather.32.cloned.1.call-done
  1803.1 11.5 gather_fusion.107
  1814.6 9.1 gather_fusion.106
  1832.8 9.1 gather_fusion.104
  1851.1 9.2 gather_fusion.102
  1904.4 14.9 all-reduce.3
  1926.3 13.7 all-reduce.2
  2042.4 9.3 add_convert_fusion.2
  2055.6 37.1 %reduce-scatter.31.cloned.1.call-done = bf16[128,1932]{1,0:T(8,128)(2,1)} async-done(((bf16[512,1932]{1,0:T(8,128)(2,1)}), bf16[128,1932]{1,0:T(8,128)(2,1)}) %reduce-scatter.31.cloned.1.call-update) | async-done | bytes 494608
  2094.7 14.9 all-reduce.1
  2209.6 9.3 add_convert_fusion.1
  2246.9 10.2 reduce-scatter.33.cloned.1.call-done
  2259.1 14.9 all-reduce
  2373.4 9.4 add_convert_fusion
  2469.4 84.0 %reduce-scatter.23.cloned.1.call-done = f32[3,9,64,128]{3,2,1,0:T(8,128)} async-done(((f32[3,9,512,128]{3,2,1,0:T(8,128)}), f32[3,9,64,128]{3,2,1,0:T(8,128)}) %reduce-scatter.23.cloned.1.call-update) | async-done | bytes 884752 | tf_op jit(solution)/shard_map/reduce_scatter | solution.py:221
  2553.4 133.3 %reduce-scatter.21.cloned.1.call-done = f32[3,9,64,128]{3,2,1,0:T(8,128)} async-done(((f32[3,9,512,128]{3,2,1,0:T(8,128)}), f32[3,9,64,128]{3,2,1,0:T(8,128)}) %reduce-scatter.21.cloned.1.call-update) | async-done | bytes 884752 | tf_op jit(solution)/shard_map/reduce_scatter | solution.py:220
  (1041 shorter events, 1527.6 us)
Async XLA Ops:
  7.2 40.4 %all-gather.12.cloned.1.call-start = ((), (), s32[]{:S(2)}) async-start(), calls=%async_computation.8 | async-start | bytes 2897920 | tf_op jit(solution)/shard_map/all_gather | solution.py:79
  8.1 5.3 collective-permute-start.1
  11.1 5.7 collective-permute-start
  21.3 111.2 %all-gather.14.cloned.1.call-start = ((), (), s32[]{:S(2)}) async-start(), calls=%async_computation.9 | async-start | bytes 3981312 | tf_op jit(solution)/shard_map/all_gather | solution.py:184
  22.1 182.8 %all-gather.16.cloned.1.call-start = ((), (), s32[]{:S(2)}) async-start(), calls=%async_computation.10 | async-start | bytes 2897920 | tf_op jit(solution)/shard_map/all_gather | solution.py:79
  26.0 138.1 %copy-start.189 = (f32[128]{0:T(128)}, f32[128]{0:T(128)S(1)}, u32[]{:S(2)}) copy-start(f32[128]{0:T(128)S(1)} %get-tuple-element.169) | copy-start | bytes 1540
  26.0 138.1 %copy-start.192 = (f32[128]{0:T(128)}, f32[128]{0:T(128)S(1)}, u32[]{:S(2)}) copy-start(f32[128]{0:T(128)S(1)} %get-tuple-element.201) | copy-start | bytes 1540
  26.0 295.0 %copy-start.195 = (f32[128]{0:T(128)}, f32[128]{0:T(128)S(1)}, u32[]{:S(2)}) copy-start(f32[128]{0:T(128)S(1)} %get-tuple-element.170) | copy-start | bytes 1540
  26.0 295.0 %copy-start.197 = (f32[128]{0:T(128)}, f32[128]{0:T(128)S(1)}, u32[]{:S(2)}) copy-start(f32[128]{0:T(128)S(1)} %get-tuple-element.200) | copy-start | bytes 1540
  164.4 5.3 collective-permute-start.3
  166.6 7.3 collective-permute-start.2
  178.0 183.8 %all-gather.18.cloned.1.call-start = ((), (), s32[]{:S(2)}) async-start(), calls=%async_computation.11 | async-start | bytes 2897920 | tf_op jit(solution)/shard_map/all_gather | solution.py:79
  321.4 5.3 collective-permute-start.5
  323.5 7.3 collective-permute-start.4
  334.9 185.7 %all-gather.20.cloned.1.call-start = ((), (), s32[]{:S(2)}) async-start(), calls=%async_computation.12 | async-start | bytes 2897920 | tf_op jit(solution)/shard_map/all_gather | solution.py:79
  480.2 5.3 collective-permute-start.7
  482.4 7.3 collective-permute-start.6
  493.7 111.5 %all-gather.22.cloned.1.call-start = ((), (), s32[]{:S(2)}) async-start(), calls=%async_computation.13 | async-start | bytes 3981312 | tf_op jit(solution)/shard_map/all_gather | solution.py:185
  494.3 183.4 %all-gather.24.cloned.1.call-start = ((), (), s32[]{:S(2)}) async-start(), calls=%async_computation.14 | async-start | bytes 2897920 | tf_op jit(solution)/shard_map/all_gather | solution.py:79
  494.9 142.0 %copy-start.199 = (f32[128]{0:T(128)}, f32[128]{0:T(128)S(1)}, u32[]{:S(2)}) copy-start(f32[128]{0:T(128)S(1)} %get-tuple-element.163) | copy-start | bytes 1540
  494.9 142.0 %copy-start.201 = (f32[128]{0:T(128)}, f32[128]{0:T(128)S(1)}, u32[]{:S(2)}) copy-start(f32[128]{0:T(128)S(1)} %get-tuple-element.204) | copy-start | bytes 1540
  636.9 52.2 %copy-start.207 = (f32[128]{0:T(128)}, f32[128]{0:T(128)S(1)}, u32[]{:S(2)}) copy-start(f32[128]{0:T(128)S(1)} %get-tuple-element.182) | copy-start | bytes 1540
  636.9 52.2 %copy-start.209 = (f32[128]{0:T(128)}, f32[128]{0:T(128)S(1)}, u32[]{:S(2)}) copy-start(f32[128]{0:T(128)S(1)} %get-tuple-element.183) | copy-start | bytes 1540
  637.3 5.3 collective-permute-start.9
  639.5 7.3 collective-permute-start.8
  650.8 183.7 %all-gather.26.cloned.1.call-start = ((), (), s32[]{:S(2)}) async-start(), calls=%async_computation.15 | async-start | bytes 2897920 | tf_op jit(solution)/shard_map/all_gather | solution.py:79
  794.1 5.3 collective-permute-start.11
  796.3 7.3 collective-permute-start.10
  807.7 313.0 %reduce-scatter.25.cloned.1.call-start = ((), (), s32[]{:S(2)}) async-start(), calls=%async_computation.21 | async-start | bytes 2621440
  968.6 8.2 collective-permute-start.13
  974.9 5.7 collective-permute-start.12
  1083.4 38.5 %copy-start.16 = (f32[1932,128]{1,0:T(8,128)S(1)}, f32[1932,128]{1,0:T(8,128)}, u32[]{:S(2)}) copy-start(f32[1932,128]{1,0:T(8,128)} %copy-done.15) | copy-start | bytes 2967556
  1083.5 201.0 %reduce-scatter.27.cloned.1.call-start = ((), (), s32[]{:S(2)}) async-start(), calls=%async_computation.22 | async-start | bytes 2621440
  1138.1 5.3 collective-permute-start.15
  1140.5 7.1 collective-permute-start.14
  1250.2 35.6 %copy-start.200 = (f32[128]{0:T(128)S(1)}, f32[128]{0:T(128)}, u32[]{:S(2)}) copy-start(f32[128]{0:T(128)} %copy-done.199) | copy-start | bytes 1540
  1250.2 35.7 %copy-start.202 = (f32[128]{0:T(128)S(1)}, f32[128]{0:T(128)}, u32[]{:S(2)}) copy-start(f32[128]{0:T(128)} %copy-done.201) | copy-start | bytes 1540
  1250.2 35.7 %copy-start.208 = (f32[128]{0:T(128)S(1)}, f32[128]{0:T(128)}, u32[]{:S(2)}) copy-start(f32[128]{0:T(128)} %copy-done.207) | copy-start | bytes 1540
  1250.2 35.7 %copy-start.210 = (f32[128]{0:T(128)S(1)}, f32[128]{0:T(128)}, u32[]{:S(2)}) copy-start(f32[128]{0:T(128)} %copy-done.209) | copy-start | bytes 1540
  1250.2 198.1 %reduce-scatter.29.cloned.1.call-start = ((), (), s32[]{:S(2)}) async-start(), calls=%async_computation.23 | async-start | bytes 2621440
  1302.0 5.3 collective-permute-start.17
  1304.4 7.0 collective-permute-start.16
  1414.0 36.0 %copy-start.34 = (f32[483,4]{1,0:T(8,128)S(1)}, f32[483,4]{1,0:T(8,128)}, u32[]{:S(2)}) copy-start(f32[483,4]{1,0:T(8,128)} %copy-done.33) | copy-start | bytes 23188
  1414.1 74.7 %all-gather.28.cloned.1.call-start = ((), (), s32[]{:S(2)}) async-start(), calls=%async_computation.16 | async-start | bytes 2897920 | tf_op jit(solution)/shard_map/all_gather | solution.py:79
  1450.7 5.3 collective-permute-start.19
  1453.8 5.7 collective-permute-start.18
  1463.5 182.6 %all-gather.30.cloned.1.call-start = ((), (), s32[]{:S(2)}) async-start(), calls=%async_computation.17 | async-start | bytes 2897920 | tf_op jit(solution)/shard_map/all_gather | solution.py:79
  1605.7 5.3 collective-permute-start.21
  1607.9 7.3 collective-permute-start.20
  1619.2 183.9 %all-gather.32.cloned.1.call-start = ((), (), s32[]{:S(2)}) async-start(), calls=%async_computation.18 | async-start | bytes 2897920 | tf_op jit(solution)/shard_map/all_gather | solution.py:79
  1762.7 5.3 collective-permute-start.23
  1764.9 7.3 collective-permute-start.22
  1776.2 316.5 %reduce-scatter.31.cloned.1.call-start = ((), (), s32[]{:S(2)}) async-start(), calls=%async_computation.24 | async-start | bytes 2621440
  1940.8 8.2 collective-permute-start.25
  1947.1 5.7 collective-permute-start.24
  2055.6 38.5 %copy-start.14 = (f32[1932,128]{1,0:T(8,128)S(1)}, f32[1932,128]{1,0:T(8,128)}, u32[]{:S(2)}) copy-start(f32[1932,128]{1,0:T(8,128)} %copy-done.13) | copy-start | bytes 2967556
  2055.6 201.6 %reduce-scatter.33.cloned.1.call-start = ((), (), s32[]{:S(2)}) async-start(), calls=%async_computation.25 | async-start | bytes 2621440
  2110.7 5.3 collective-permute-start.27
  2113.1 7.1 collective-permute-start.26
  2222.9 244.5 %reduce-scatter.35.cloned.1.call-start = ((), (), s32[]{:S(2)}) async-start(), calls=%async_computation.26 | async-start | bytes 2621440
  2274.7 7.1 collective-permute-start.29
  2277.0 7.0 collective-permute-start.28
  2386.6 166.8 %reduce-scatter.23.cloned.1.call-start = ((), (), s32[]{:S(2)}) async-start(), calls=%async_computation.20 | async-start | bytes 7962624 | tf_op jit(solution)/shard_map/reduce_scatter | solution.py:221
  2416.6 270.1 %reduce-scatter.21.cloned.1.call-start = ((), (), s32[]{:S(2)}) async-start(), calls=%async_computation.19 | async-start | bytes 7962624 | tf_op jit(solution)/shard_map/reduce_scatter | solution.py:220
  (232 other events, 1239.1 us)
Sparse Core Ops, SparseCore 0:
  21.4 26.1 all-gather.11
  49.8 63.2 all-gather.13
  178.1 26.7 all-gather.15
  335.0 26.7 all-gather.17
  493.9 26.7 all-gather.19
  522.7 63.2 all-gather.21
  650.9 26.7 all-gather.23
  807.8 26.7 all-gather.25
  1083.6 36.9 reduce-scatter.24
  1250.3 34.1 reduce-scatter.26
  1414.2 34.0 reduce-scatter.28
  1463.7 25.0 all-gather.27
  1619.4 26.7 all-gather.29
  1776.3 26.7 all-gather.31
  2055.7 36.9 reduce-scatter.30
  2223.0 34.0 reduce-scatter.32
  2386.7 34.1 reduce-scatter.34
  2425.0 128.3 reduce-scatter.22
  2558.1 128.5 reduce-scatter.20
where the time goes:
time: 2710 us; the launch traced here: 2690 us
  local copies, waits for them, and re-layouts  1270 us (47%)
  waiting for transfers between devices  662 us (24%)
  matrix products  403 us (15%)
  blocking collectives  221 us (8%)
  starting transfers between devices  86.2 us (3%)
  other arithmetic  30.4 us (1%)
    gather x81, local copies, waits for them, and re-layouts, convolve(): jnp.take(piece, gather_index[tap_number], axis=0, mode='fill', fill_value=0)  761 us
    gather x54, local copies, waits for them, and re-layouts, layer_back(): jnp.take(grad_padded, mirror_index[tap_number], axis=0, mode='fill', fill...  401 us
    all_gather x9, waiting for transfers between devices, convolve(): piece = lax.all_gather(padded, 'grp', axis=1, tiled=True)  232 us
    dot_general x54, matrix products, layer_back(): jnp.einsum('po,io->pi', taken, kernels[tap_number], preferred_element_typ...  183 us
    unnamed x25, waiting for transfers between devices  154 us
    dot_general x81, matrix products, convolve(): jnp.dot(taken, kernel_rows, preferred_element_type=jnp.float32)  149 us
    psum x9, blocking collectives, normalize(): lax.psum((jnp.sum(conv_out, axis=0), jnp.sum(conv_out * conv_out, axis=0)...  134 us
    reduce_scatter x1, waiting for transfers between devices, shards(): lax.psum_scatter(enc_kernel_grad, 'rows', scatter_dimension=2, tiled=True)  133 us
  transfers between devices with their start and end apart: 49, of which 31 were waited for; matrix products, arithmetic and copies ran while one was open for 10% of the time, Pallas kernels for 0%

commit v1 on v0

v1 whole, which is shorter than its diff:
```python
import functools

import jax
import jax.numpy as jnp
from jax import lax
from jax.experimental import pallas as pl
from jax.experimental.pallas import tpu as pltpu
from jax.sharding import PartitionSpec as P

SIZES = ((15, 20), (18, 24), (30, 40))
WIDTHS = tuple(w for _, w in SIZES)
EDGE = 48
EPSILON = 1e-05
MESH = pl.DeviceIdType.MESH
F32 = jnp.float32
BF16 = jnp.bfloat16
LANE = 128
(M_W0, M_W1, M_UP, M_DOWN, M_LEFT, M_RIGHT, M_VALID) = range(7)


def ceil_to(value, step):
    return -(-value // step) * step


def window_masks(image_group, first_window, count, padded):
    chosen = (image_group[:, None] == jnp.arange(3, dtype=jnp.int32)[None, :]).astype(jnp.int32)
    heights = jnp.sum(chosen * jnp.array([h for h, _ in SIZES], jnp.int32)[None, :], axis=1)
    widths = jnp.sum(chosen * jnp.array(WIDTHS, jnp.int32)[None, :], axis=1)
    areas = heights * widths
    ends = jnp.cumsum(areas)
    starts = ends - areas
    local = jnp.arange(padded + 2 * EDGE, dtype=jnp.int32) - EDGE
    windows = local + first_window
    member = ((windows[:, None] >= starts[None, :]) & (windows[:, None] < ends[None, :])).astype(jnp.int32)
    base = jnp.sum(member * starts[None, :], axis=1)
    height = jnp.sum(member * heights[None, :], axis=1)
    width = jnp.sum(member * widths[None, :], axis=1)
    inside = width > 0
    position = windows - base
    safe = jnp.maximum(width, 1)
    row = position // safe
    column = position - row * safe
    masks = [
        width == WIDTHS[0],
        width == WIDTHS[1],
        inside & (row > 0),
        inside & (row < height - 1),
        inside & (column > 0),
        inside & (column < width - 1),
        (local >= 0) & (local < count),
    ]
    table = jnp.stack([m.astype(F32) for m in masks], axis=1)
    return jnp.pad(table, ((0, 0), (0, LANE - len(masks))))


def to_planes(stream, count, padded):
    planes = jnp.transpose(stream.reshape(count, 4, stream.shape[1]), (1, 0, 2))
    return jnp.pad(planes, ((0, 0), (0, padded - count), (0, 0)))


def to_stream(planes, count):
    return jnp.transpose(planes[:, :count], (1, 0, 2)).reshape(4 * count, planes.shape[2])


def mask_of(mask_ref, which, low, count):
    return mask_ref[low : low + count, which : which + 1] > 0.5


def by_width(mask_ref, low, count, shifted):
    return jnp.where(
        mask_of(mask_ref, M_W0, low, count),
        shifted(WIDTHS[0]),
        jnp.where(mask_of(mask_ref, M_W1, low, count), shifted(WIDTHS[1]), shifted(WIDTHS[2])),
    )


def row_peers(rows):
    here = lax.axis_index("rows")
    there = lax.axis_index("grp")
    return [(lax.rem(here + k, rows), there) for k in range(1, rows)]


def grp_peers():
    here = lax.axis_index("rows")
    mine = lax.axis_index("grp")
    half, core = mine // 2, lax.rem(mine, 2)
    return (here, half * 2 + 1 - core), (here, (1 - half) * 2 + core)


def greet(peers):
    barrier = pltpu.get_barrier_semaphore()
    for peer in peers:
        pl.semaphore_signal(barrier, inc=1, device_id=peer, device_id_type=MESH)
    pl.semaphore_wait(barrier, len(peers))


def remote(src, dst, send, recv, peer):
    return pltpu.make_async_remote_copy(
        src_ref=src, dst_ref=dst, send_sem=send, recv_sem=recv, device_id=peer, device_id_type=MESH
    )


def exchange_sums(rows, own, buf, send, recv):
    peers = row_peers(rows)
    buf[0] = own
    copies = []
    for k, peer in enumerate(peers):
        copy = remote(buf.at[0], buf.at[k + 1], send.at[k], recv.at[k], peer)
        copy.start()
        copies.append(copy)
    for copy in copies:
        copy.wait()
    total = buf[0]
    for k in range(1, rows):
        total = total + buf[k]
    return total


def row_parts(padded, count):
    tail = (count - EDGE) // 16 * 16
    parts = [(0, EDGE), (tail, padded - tail)]
    inner = tail - EDGE
    start = EDGE
    steps = 3
    for k in range(steps):
        size = ceil_to(-(-(tail - start) // (steps - k)), 16)
        size = min(size, tail - start)
        parts.append((start, size))
        start += size
    return parts


def forward_kernel(
    rows, count, padded, pixels,
    v_ref, w_ref, gb_ref, mask_ref,
    next_ref, z_ref, stat_ref, full_ref,
    vbuf, yext, over, under, to_next, to_prev, from_prev, from_next, sums,
    core_s, core_r, x_s, x_r, fwd_s, fwd_r, halo_s, halo_r, sum_s, sum_r, out_sem,
):
    mine = lax.axis_index("grp")
    here = lax.axis_index("rows")
    half = mine // 2
    partner, across = grp_peers()
    greet([partner, across] + row_peers(rows))
    parts = row_parts(padded, count)

    own_lanes = pl.ds(pl.multiple_of(mine * LANE, LANE), LANE)
    far_lanes = pl.ds(pl.multiple_of(across[1] * LANE, LANE), LANE)
    x_copies = []
    for k, (low, size) in enumerate(parts):
        piece = pl.ds(low, size)
        copy = remote(
            v_ref.at[:, piece, :], vbuf.at[:, piece, own_lanes], x_s.at[k], x_r.at[k], across
        )
        copy.start()
        x_copies.append(copy)
    core_copy = remote(v_ref, vbuf.at[:, :, own_lanes], core_s, core_r, partner)
    core_copy.start()
    vbuf[:, :, own_lanes] = v_ref[...]
    yext[EDGE + padded :, :] = jnp.zeros((EDGE, yext.shape[1]), F32)
    core_copy.wait_recv()

    def add_products(low, size, base, touched):
        for q in range(4):
            a, b = q // 2, q % 2
            left = vbuf[q, low : low + size, pl.ds(base, 2 * LANE)]
            for step in range(3):
                right = w_ref[pl.ds(base, 2 * LANE), step * 3 * LANE : (step + 1) * 3 * LANE]
                product = jnp.dot(left, right, preferred_element_type=F32)
                for column in range(3):
                    spot = (a + step) * 4 + b + column
                    block = product[:, column * LANE : (column + 1) * LANE]
                    where = (slice(EDGE + low, EDGE + low + size), slice(spot * LANE, (spot + 1) * LANE))
                    if spot in touched:
                        yext[where] += block
                    else:
                        yext[where] = block
                        touched.add(spot)

    own_base = pl.multiple_of(half * 2 * LANE, 2 * LANE)
    far_base = pl.multiple_of((1 - half) * 2 * LANE, 2 * LANE)
    add_products(0, padded, own_base, set())

    full = set(range(16))
    forwards = []
    for k, (low, size) in enumerate(parts):
        piece = pl.ds(low, size)
        x_copies[k].wait_recv()
        far = vbuf.at[:, piece, far_lanes]
        copy = remote(far, far, fwd_s.at[k], fwd_r.at[k], partner)
        copy.start()
        forwards.append(copy)
    halos = []
    for k, (low, size) in enumerate(parts):
        forwards[k].wait_recv()
        add_products(low, size, far_base, full)
        if k == 1:
            last = EDGE + count - EDGE
            to_next[:, : 4 * LANE] = yext[last : last + EDGE, 12 * LANE :]
            to_next[:, 4 * LANE : 5 * LANE] = yext[last : last + EDGE, 7 * LANE : 8 * LANE]
            to_next[:, 5 * LANE :] = yext[last : last + EDGE, 11 * LANE : 12 * LANE]
            to_prev[:, : 4 * LANE] = yext[EDGE : 2 * EDGE, : 4 * LANE]
            to_prev[:, 4 * LANE : 5 * LANE] = yext[EDGE : 2 * EDGE, 4 * LANE : 5 * LANE]
            to_prev[:, 5 * LANE :] = yext[EDGE : 2 * EDGE, 8 * LANE : 9 * LANE]
            after = (lax.rem(here + 1, rows), mine)
            before = (lax.rem(here + rows - 1, rows), mine)
            halos = [
                remote(to_next, from_prev, halo_s.at[0], halo_r.at[0], after),
                remote(to_prev, from_next, halo_s.at[1], halo_r.at[1], before),
            ]
            for copy in halos:
                copy.start()
    out_copy = pltpu.make_async_copy(vbuf, full_ref, out_sem)
    out_copy.start()
    for copy in halos:
        copy.wait_recv()
    yext[:EDGE, 12 * LANE :] = from_prev[:, : 4 * LANE]
    yext[:EDGE, 7 * LANE : 8 * LANE] = from_prev[:, 4 * LANE : 5 * LANE]
    yext[:EDGE, 11 * LANE : 12 * LANE] = from_prev[:, 5 * LANE :]
    after_own = slice(EDGE + count, 2 * EDGE + count)
    yext[after_own, : 4 * LANE] = from_next[:, : 4 * LANE]
    yext[after_own, 4 * LANE : 5 * LANE] = from_next[:, 4 * LANE : 5 * LANE]
    yext[after_own, 8 * LANE : 9 * LANE] = from_next[:, 5 * LANE :]

    def at(low, size, spot):
        return yext[low : low + size, spot * LANE : (spot + 1) * LANE]

    low, size = 8, padded + 2 * EDGE - 16
    go_left = mask_of(mask_ref, M_LEFT, low, size)
    go_right = mask_of(mask_ref, M_RIGHT, low, size)
    for kept, first in ((over, 12), (under, 0)):
        kept[low : low + size, :LANE] = at(low, size, first + 1) + jnp.where(
            go_left, at(low - 1, size, first + 3), 0.0
        )
        kept[low : low + size, LANE:] = at(low, size, first + 2) + jnp.where(
            go_right, at(low + 1, size, first), 0.0
        )
    go_left = mask_of(mask_ref, M_LEFT, EDGE, padded)
    go_right = mask_of(mask_ref, M_RIGHT, EDGE, padded)
    valid = mask_of(mask_ref, M_VALID, EDGE, padded)
    total = jnp.zeros((1, LANE), F32)
    squares = jnp.zeros((1, LANE), F32)
    for q in range(4):
        a, b = q // 2, q % 2
        lanes = slice(b * LANE, (b + 1) * LANE)
        kept, sign = (over, -1) if a == 0 else (under, 1)
        rowwise = by_width(
            mask_ref, EDGE, padded,
            lambda w: kept[EDGE + sign * w : EDGE + sign * w + padded, lanes],
        )
        z = at(EDGE, padded, (a + 1) * 4 + b + 1)
        z = z + jnp.where(mask_of(mask_ref, (M_UP, M_DOWN)[a], EDGE, padded), rowwise, 0.0)
        if b == 0:
            z = z + jnp.where(go_left, at(EDGE - 1, padded, (a + 1) * 4 + 3), 0.0)
        else:
            z = z + jnp.where(go_right, at(EDGE + 1, padded, (a + 1) * 4), 0.0)
        z = jnp.where(valid, z, 0.0)
        z_ref[q] = z
        total = total + jnp.sum(z, axis=0, keepdims=True)
        squares = squares + jnp.sum(z * z, axis=0, keepdims=True)
    both = exchange_sums(
        rows, jnp.concatenate([total, squares, jnp.zeros((6, LANE), F32)], axis=0), sums, sum_s, sum_r
    )
    mean = both[0:1] / pixels
    inverse = lax.rsqrt(both[1:2] / pixels - mean * mean + EPSILON)
    stat_ref[...] = jnp.concatenate([mean, inverse, jnp.zeros((6, LANE), F32)], axis=0)
    for q in range(4):
        y = gb_ref[0:1] * ((z_ref[q] - mean) * inverse) + gb_ref[1:2]
        next_ref[q] = jnp.where(valid, y * jax.nn.sigmoid(y), 0.0).astype(BF16)
    core_copy.wait_send()
    for copy in x_copies + forwards + halos:
        copy.wait_send()
    out_copy.wait()


def backward_kernel(
    rows, count, padded, pixels,
    g_ref, z_ref, stat_ref, gb_ref, mask_ref, full_ref, w_ref,
    grad_ref, wgrad_ref, gbgrad_ref,
    gy, gext, above, below, patch, part, keep, core_out, core_in, x_out, x_in,
    to_next, to_prev, from_prev, from_next, sums,
    core_s, core_r, x_s, x_r, halo_s, halo_r, sum_s, sum_r,
):
    mine = lax.axis_index("grp")
    here = lax.axis_index("rows")
    half, core = mine // 2, lax.rem(mine, 2)
    partner, across = grp_peers()
    greet([partner, across] + row_peers(rows))
    mean, inverse = stat_ref[0:1], stat_ref[1:2]
    gain, shift = gb_ref[0:1], gb_ref[1:2]
    valid = mask_of(mask_ref, M_VALID, EDGE, padded)

    shift_sum = jnp.zeros((1, LANE), F32)
    gain_sum = jnp.zeros((1, LANE), F32)
    for q in range(4):
        normed = (z_ref[q] - mean) * inverse
        y = gain * normed + shift
        s = jax.nn.sigmoid(y)
        grad = g_ref[q] * s * (1.0 + y * (1.0 - s))
        grad = jnp.where(valid, grad, 0.0)
        gy[q] = grad
        shift_sum = shift_sum + jnp.sum(grad, axis=0, keepdims=True)
        gain_sum = gain_sum + jnp.sum(grad * normed, axis=0, keepdims=True)
    both = exchange_sums(
        rows, jnp.concatenate([shift_sum, gain_sum, jnp.zeros((6, LANE), F32)], axis=0), sums, sum_s, sum_r
    )
    gbgrad_ref[...] = both
    gext[EDGE + padded :, :] = jnp.zeros((EDGE, 4 * LANE), F32)
    for q in range(4):
        normed = (z_ref[q] - mean) * inverse
        gz = inverse * gain * (gy[q] - both[0:1] / pixels - normed * both[1:2] / pixels)
        gz = jnp.where(valid, gz, 0.0).astype(BF16).astype(F32)
        gext[EDGE : EDGE + padded, q * LANE : (q + 1) * LANE] = gz
    to_next[...] = gext[count : count + EDGE, :].astype(BF16)
    to_prev[...] = gext[EDGE : 2 * EDGE, :].astype(BF16)
    after = (lax.rem(here + 1, rows), mine)
    before = (lax.rem(here + rows - 1, rows), mine)
    halos = [
        remote(to_next, from_prev, halo_s.at[0], halo_r.at[0], after),
        remote(to_prev, from_next, halo_s.at[1], halo_r.at[1], before),
    ]
    for copy in halos:
        copy.start()
    for copy in halos:
        copy.wait()
    gext[:EDGE, :] = from_prev[...].astype(F32)
    gext[EDGE + count : 2 * EDGE + count, :] = from_next[...].astype(F32)

    low, size = EDGE - 8, padded + 16
    for kept, which, sign, lanes in (
        (above, M_UP, -1, slice(2 * LANE, 4 * LANE)),
        (below, M_DOWN, 1, slice(0, 2 * LANE)),
    ):
        rowwise = by_width(
            mask_ref, low, size, lambda w: gext[low + sign * w : low + sign * w + size, lanes]
        )
        kept[...] = jnp.where(mask_of(mask_ref, which, low, size), rowwise, 0.0)
    go_left = mask_of(mask_ref, M_LEFT, EDGE, padded)
    go_right = mask_of(mask_ref, M_RIGHT, EDGE, padded)
    for step, (kept, top, lane) in enumerate(
        ((above, 8, 0), (gext, EDGE, 0), (gext, EDGE, 2 * LANE), (below, 8, 0))
    ):
        even, odd = slice(lane, lane + LANE), slice(lane + LANE, lane + 2 * LANE)
        blocks = [
            jnp.where(go_left, kept[top - 1 : top - 1 + padded, odd], 0.0),
            kept[top : top + padded, even],
            kept[top : top + padded, odd],
            jnp.where(go_right, kept[top + 1 : top + 1 + padded, even], 0.0),
        ]
        for column, block in enumerate(blocks):
            spot = step * 4 + column
            patch[:, spot * LANE : (spot + 1) * LANE] = block.astype(BF16)

    def taps(q, step):
        a, b = q // 2, q % 2
        first = (a + step) * 4 + b
        return patch[:, first * LANE : (first + 3) * LANE]

    def input_grad(q, base):
        total = None
        for step in range(3):
            right = w_ref[pl.ds(base, 2 * LANE), step * 3 * LANE : (step + 1) * 3 * LANE]
            product = lax.dot_general(
                taps(q, step), right, (((1,), (1,)), ((), ())), preferred_element_type=F32
            )
            total = product if total is None else total + product
        part[...] = total

    own_lanes = pl.ds(pl.multiple_of(core * LANE, LANE), LANE)
    other_lanes = pl.ds(pl.multiple_of((1 - core) * LANE, LANE), LANE)
    own_base = pl.multiple_of(half * 2 * LANE, 2 * LANE)
    far_base = pl.multiple_of((1 - half) * 2 * LANE, 2 * LANE)
    core_copies, x_copies = [], []

    def send_across(q):
        core_copies[q].wait_recv()
        x_out[q] = (keep[q] + core_in[q].astype(F32)).astype(BF16)
        copy = remote(x_out.at[q], x_in.at[q], x_s.at[q], x_r.at[q], across)
        copy.start()
        x_copies.append(copy)

    for turn, base in enumerate((far_base, own_base)):
        for q in range(4):
            spot = turn * 4 + q
            input_grad(q, base)
            core_out[spot] = part[:, other_lanes].astype(BF16)
            keep[spot] = part[:, own_lanes]
            copy = remote(
                core_out.at[spot], core_in.at[spot], core_s.at[spot], core_r.at[spot], partner
            )
            copy.start()
            core_copies.append(copy)
            if turn == 0 and q > 0:
                send_across(q - 1)
        if turn == 0:
            send_across(3)

    for step in range(3):
        total = None
        for q in range(4):
            product = lax.dot_general(
                full_ref[q], taps(q, step), (((0,), (0,)), ((), ())), preferred_element_type=F32
            )
            total = product if total is None else total + product
        wgrad_ref[:, step * 3 * LANE : (step + 1) * 3 * LANE] = total.astype(BF16)

    for q in range(4):
        core_copies[4 + q].wait_recv()
        x_copies[q].wait_recv()
        grad_ref[q] = keep[4 + q] + core_in[4 + q].astype(F32) + x_in[q].astype(F32)
    for copy in core_copies + x_copies:
        copy.wait_send()


VM = pl.BlockSpec(memory_space=pltpu.VMEM)
HBM = pl.BlockSpec(memory_space=pl.ANY)
LIMIT = 56 * 1024 * 1024


def forward_layer(rows, count, padded, pixels, planes, weight, gain_shift, masks):
    channels = weight.shape[0]
    ext = padded + 2 * EDGE
    n_parts = len(row_parts(padded, count))
    dma = pltpu.SemaphoreType.DMA
    return pl.pallas_call(
        functools.partial(forward_kernel, rows, count, padded, pixels),
        name="layer_forward",
        out_shape=(
            jax.ShapeDtypeStruct((4, padded, LANE), BF16),
            jax.ShapeDtypeStruct((4, padded, LANE), F32),
            jax.ShapeDtypeStruct((8, LANE), F32),
            jax.ShapeDtypeStruct((4, padded, channels), BF16),
        ),
        in_specs=[VM] * 4,
        out_specs=(VM, VM, VM, HBM),
        scratch_shapes=[
            pltpu.VMEM((4, padded, channels), BF16),
            pltpu.VMEM((ext, 16 * LANE), F32),
            pltpu.VMEM((ext, 2 * LANE), F32),
            pltpu.VMEM((ext, 2 * LANE), F32),
        ]
        + [pltpu.VMEM((EDGE, 6 * LANE), F32)] * 4
        + [pltpu.VMEM((rows, 8, LANE), F32)]
        + [dma, dma]
        + [dma((n_parts,))] * 4
        + [dma((2,))] * 2
        + [dma((rows - 1,))] * 2
        + [dma],
        compiler_params=pltpu.CompilerParams(
            collective_id=0, has_side_effects=True, vmem_limit_bytes=LIMIT
        ),
        cost_estimate=pl.CostEstimate(
            flops=2 * 36 * padded * channels * LANE, bytes_accessed=8 * 2**20, transcendentals=0
        ),
    )(planes, weight, gain_shift, masks)


def backward_layer(rows, count, padded, pixels, grad, z, stat, gain_shift, masks, full, weight):
    channels = weight.shape[0]
    ext = padded + 2 * EDGE
    dma = pltpu.SemaphoreType.DMA
    return pl.pallas_call(
        functools.partial(backward_kernel, rows, count, padded, pixels),
        name="layer_backward",
        out_shape=(
            jax.ShapeDtypeStruct((4, padded, LANE), F32),
            jax.ShapeDtypeStruct((channels, 9 * LANE), BF16),
            jax.ShapeDtypeStruct((8, LANE), F32),
        ),
        in_specs=[VM] * 7,
        out_specs=(VM, VM, VM),
        scratch_shapes=[
            pltpu.VMEM((4, padded, LANE), F32),
            pltpu.VMEM((ext, 4 * LANE), F32),
            pltpu.VMEM((padded + 16, 2 * LANE), F32),
            pltpu.VMEM((padded + 16, 2 * LANE), F32),
            pltpu.VMEM((padded, 16 * LANE), BF16),
            pltpu.VMEM((padded, 2 * LANE), F32),
            pltpu.VMEM((8, padded, LANE), F32),
            pltpu.VMEM((8, padded, LANE), BF16),
            pltpu.VMEM((8, padded, LANE), BF16),
            pltpu.VMEM((4, padded, LANE), BF16),
            pltpu.VMEM((4, padded, LANE), BF16),
        ]
        + [pltpu.VMEM((EDGE, 4 * LANE), BF16)] * 4
        + [pltpu.VMEM((rows, 8, LANE), F32)]
        + [dma((8,))] * 2
        + [dma((4,))] * 2
        + [dma((2,))] * 2
        + [dma((rows - 1,))] * 2,
        compiler_params=pltpu.CompilerParams(
            collective_id=1, has_side_effects=True, vmem_limit_bytes=LIMIT
        ),
        cost_estimate=pl.CostEstimate(
            flops=4 * 36 * padded * channels * LANE, bytes_accessed=8 * 2**20, transcendentals=0
        ),
    )(grad, z, stat, gain_shift, masks, full, weight)


def shards(
    features, image_group, switches, enc_weight, dec_weight,
    enc_gain, enc_bias, dec_gain, dec_bias, d_decoded,
):
    rows = lax.axis_size("rows")
    count = features.shape[0] // 4
    padded = ceil_to(count, 16)
    pixels = float(features.shape[0] * rows)
    masks = window_masks(image_group, lax.axis_index("rows") * count, count, padded)

    def whole_weight(weight):
        flat = jnp.transpose(weight[::-1], (1, 0, 2)).reshape(weight.shape[1], -1)
        return lax.all_gather(flat, "rows", axis=0, tiled=True)

    def pair(gain, shift):
        return jnp.pad(jnp.stack([gain, shift]), ((0, 6), (0, 0)))

    weights = [whole_weight(w[l]) for w in (enc_weight, dec_weight) for l in range(3)]
    pairs = [pair(g[l], s[l]) for g, s in ((enc_gain, enc_bias), (dec_gain, dec_bias)) for l in range(3)]
    hits = switches[None, :] == jnp.arange(4, dtype=jnp.int32)[:, None]
    hits = jnp.pad(hits.astype(F32), ((0, 0), (0, padded - count)))[:, :, None]

    saved = []
    planes = to_planes(features, count, padded)
    pooled = blocks = None
    for layer in range(6):
        planes, z, stat, full = forward_layer(
            rows, count, padded, pixels, planes, weights[layer], pairs[layer], masks
        )
        saved.append((z, stat, full))
        if layer == 2:
            y = pairs[2][0] * ((z - stat[0]) * stat[1]) + pairs[2][1]
            blocks = jax.nn.silu(y)
            pooled = jnp.log(jnp.mean(jnp.exp(blocks), axis=0))
            planes = (pooled[None] * hits).astype(BF16)
    decoded = to_stream(planes, count)

    grad = to_planes(d_decoded, count, padded).astype(F32)
    weight_grads, pair_grads = [None] * 6, [None] * 6
    for layer in range(5, -1, -1):
        z, stat, full = saved[layer]
        grad, weight_grad, pair_grads[layer] = backward_layer(
            rows, count, padded, pixels, grad, z, stat, pairs[layer], masks, full, weights[layer]
        )
        mine = lax.psum_scatter(weight_grad, "rows", scatter_dimension=0, tiled=True).astype(F32)
        mine = jnp.transpose(mine.reshape(mine.shape[0], 9, -1)[:, ::-1], (1, 0, 2))
        weight_grads[layer] = mine
        if layer == 3:
            grad_pooled = jnp.sum(grad * hits, axis=0)
            grad = grad_pooled[None] * jnp.exp(blocks - pooled[None]) * 0.25
    return (
        decoded,
        to_stream(grad.astype(BF16), count),
        jnp.stack(weight_grads[:3]),
        jnp.stack(weight_grads[3:]),
        jnp.stack([p[1] for p in pair_grads[:3]]),
        jnp.stack([p[0] for p in pair_grads[:3]]),
        jnp.stack([p[1] for p in pair_grads[3:]]),
        jnp.stack([p[0] for p in pair_grads[3:]]),
    )


def solution(mesh):
    wide = P("rows", "grp")
    kernels = P(None, None, "rows", "grp")
    vector = P(None, "grp")
    return jax.shard_map(
        shards,
        mesh=mesh,
        in_specs=(wide, P(), P("rows"), kernels, kernels, vector, vector, vector, vector, wide),
        out_specs=(wide, wide, kernels, kernels, vector, vector, vector, vector),
        check_vma=False,
    )
```

time: 2710 us -> 746 us (0.28)
  local copies, waits for them, and re-layouts: 1270 us -> 25.6 us
  matrix products: 403 us -> 0 us
  Pallas kernels: 0 us -> 363 us
  waiting for transfers between devices: 662 us -> 313 us
  blocking collectives: 221 us -> 0 us
  starting transfers between devices: 86.2 us -> 1.6 us
    gather x135 -> x0, local copies, waits for them, and re-layouts: 1160 us -> none  [the longest x81 761 us: convolve(): jnp.take(piece, gather_index[tap_number], axis=0, mode='fill', fill_value=0)]
    dot_general x189 -> x0, matrix products: 403 us -> none  [the longest x54 183 us: layer_back(): jnp.einsum('po,io->pi', taken, kernels[tap_number], preferred_element_typ...]
    pallas_call x0 -> x12, Pallas kernels: none -> 363 us  [the longest x6 195 us: backward_layer(): pl.pallas_call(functools.partial(backward_kernel, rows, count, padded, pi...]
    psum x15 -> x0, blocking collectives: 221 us -> none  [the longest x9 134 us: normalize(): lax.psum((jnp.sum(conv_out, axis=0), jnp.sum(conv_out * conv_out, axis=0)...]
    unnamed x25 -> x12, waiting for transfers between devices: 154 us -> 0.2 us
    all_gather x11 -> x6, waiting for transfers between devices: 232 us -> 102 us  [whole_weight(): return lax.all_gather(flat, 'rows', axis=0, tiled=True)]
    ppermute x30 -> x0, starting transfers between devices: 85 us -> none  [the longest x15 43.3 us: padded_2(): lax.ppermute(lax.slice_in_dim(block, 0, width, axis=dim), axis, backward)]
    ppermute x30 -> x0, waiting for transfers between devices: 58.3 us -> none  [the longest x15 58.3 us: padded_2(): lax.ppermute(lax.slice_in_dim(block, block.shape[dim] - width, None, axis...]
  transfers between devices with their start and end apart: 49 -> 12, of which waited for: 31 -> 10; matrix products, arithmetic and copies ran while one was open for 10% -> 5% of each run, Pallas kernels for 0% -> 41%
where the time goes in v1:
time: 746 us; the launch traced here: 733 us
  Pallas kernels  363 us (49%)
  waiting for transfers between devices  313 us (42%)
  local copies, waits for them, and re-layouts  25.6 us (3%)
  between operations  14.9 us (2%)
  other arithmetic  14.5 us (2%)
    reduce_scatter x6, waiting for transfers between devices, shards(): lax.psum_scatter(weight_grad, 'rows', scatter_dimension=0, tiled=True)  211 us
    pallas_call x6, Pallas kernels, backward_layer(): pl.pallas_call(functools.partial(backward_kernel, rows, count, padded, pi...  195 us
    pallas_call x6, Pallas kernels, forward_layer(): pl.pallas_call(functools.partial(forward_kernel, rows, count, padded, pix...  168 us
    all_gather x6, waiting for transfers between devices, whole_weight(): return lax.all_gather(flat, 'rows', axis=0, tiled=True)  102 us
  transfers between devices with their start and end apart: 12, of which 10 were waited for; matrix products, arithmetic and copies ran while one was open for 5% of the time, Pallas kernels for 41%

profile of v1, /device:TPU:9, one launch (start us, length us, event | category | flops | bytes accessed | tf_op | source)
XLA Modules:
  0.0 732.9 jit_solution(12007766293504962146)
XLA Ops:
  7.2 1.1 slice_bitcast_fusion.4
  8.4 0.7 copy_bitcast_fusion.7
  9.2 0.7 copy_bitcast_fusion.6
  9.9 0.7 copy_bitcast_fusion.5
  10.7 0.7 copy_bitcast_fusion.4
  11.5 0.7 copy_bitcast_fusion.3
  12.2 0.7 copy_bitcast_fusion.2
  14.1 0.8 pad_convert_fusion.1.mask_ref
  15.7 1.0 pad_convert_fusion.g_ref
  16.7 0.6 select_maximum_fusion.gb_ref
  17.3 0.6 select_maximum_fusion.2.gb_ref
  17.9 0.6 select_maximum_fusion.1.gb_ref
  18.5 0.6 select_maximum_fusion.3.gb_ref
  19.1 0.6 select_maximum_fusion.4.gb_ref
  19.7 0.6 select_maximum_fusion.5.gb_ref
  20.3 0.8 pad.39.v_ref
  21.1 30.5 %all-gather.7.cloned.1.call-done.w_ref = bf16[512,1152]{1,0:T(8,128)(2,1)} async-done(((bf16[64,1152]{1,0:T(8,128)(2,1)}), bf16[512,1152]{1,0:T(8,128)(2,1)}) %all-gather.7.cloned.1.call-update) | async-done | bytes 1179664 | tf_op jit(solution)/shard_map/all_gather | solution.py:512
  51.6 28.2 %layer_forward.6 = (bf16[4,496,128]{2,1,0:T(8,128)(2,1)}, f32[4,496,128]{2,1,0:T(8,128)}, f32[8,128]{1,0:T(8,128)}, bf16[4,496,512]{2,1,0:T(8,128)(2,1)}) custom-call(bf16[4,496,128]{2,1,0:T(8,128)(2,1)} %pad.39.v_ref, bf16[512,1152]{1,0:T(8,128)(2,1)} %all-gather.7.cloned.1.call-done.w_ref, f32[8,128]{1,0:T(8,128)} %select_maximum_fusion.5.gb_ref, ...), custom_call_target="tpu_custom_call" | custom-call | flops 2340421632 | bytes 8388608 | tf_op jit(solution)/shard_map/layer_forward/pallas_call | solution.py:425
  79.8 16.0 %all-gather.9.cloned.1.call-done.w_ref = bf16[512,1152]{1,0:T(8,128)(2,1)} async-done(((bf16[64,1152]{1,0:T(8,128)(2,1)}), bf16[512,1152]{1,0:T(8,128)(2,1)}) %all-gather.9.cloned.1.call-update) | async-done | bytes 1179664 | tf_op jit(solution)/shard_map/all_gather | solution.py:512
  95.8 28.1 %layer_forward.7 = (bf16[4,496,128]{2,1,0:T(8,128)(2,1)}, f32[4,496,128]{2,1,0:T(8,128)}, f32[8,128]{1,0:T(8,128)}, bf16[4,496,512]{2,1,0:T(8,128)(2,1)}) custom-call(bf16[4,496,128]{2,1,0:T(8,128)(2,1)} %get-tuple-element.49.v_ref, bf16[512,1152]{1,0:T(8,128)(2,1)} %all-gather.9.cloned.1.call-done.w_ref, f32[8,128]{1,0:T(8,128)} %select_maximum_fusion.4.gb_ref, ...), custom_call_target="tpu_custom_call" | custom-call | flops 2340421632 | bytes 8388608 | tf_op jit(solution)/shard_map/layer_forward/pallas_call | solution.py:425
  123.9 14.8 %all-gather.11.cloned.1.call-done.w_ref = bf16[512,1152]{1,0:T(8,128)(2,1)} async-done(((bf16[64,1152]{1,0:T(8,128)(2,1)}), bf16[512,1152]{1,0:T(8,128)(2,1)}) %all-gather.11.cloned.1.call-update) | async-done | bytes 1179664 | tf_op jit(solution)/shard_map/all_gather | solution.py:512
  138.7 28.0 %layer_forward.8 = (bf16[4,496,128]{2,1,0:T(8,128)(2,1)}, f32[4,496,128]{2,1,0:T(8,128)}, f32[8,128]{1,0:T(8,128)}, bf16[4,496,512]{2,1,0:T(8,128)(2,1)}) custom-call(bf16[4,496,128]{2,1,0:T(8,128)(2,1)} %get-tuple-element.50.v_ref, bf16[512,1152]{1,0:T(8,128)(2,1)} %all-gather.11.cloned.1.call-done.w_ref, f32[8,128]{1,0:T(8,128)} %select_maximum_fusion.3.gb_ref, ...), custom_call_target="tpu_custom_call" | custom-call | flops 2340421632 | bytes 8388608 | tf_op jit(solution)/shard_map/layer_forward/pallas_call | solution.py:425
  166.7 0.8 slice_bitcast_fusion.8
  167.4 1.7 exponential_reduce_fusion
  169.2 1.1 multiply_convert_fusion.v_ref
  170.3 10.9 %all-gather.13.cloned.1.call-done.w_ref = bf16[512,1152]{1,0:T(8,128)(2,1)} async-done(((bf16[64,1152]{1,0:T(8,128)(2,1)}), bf16[512,1152]{1,0:T(8,128)(2,1)}) %all-gather.13.cloned.1.call-update) | async-done | bytes 1179664 | tf_op jit(solution)/shard_map/all_gather | solution.py:512
  181.2 28.0 %layer_forward.9 = (bf16[4,496,128]{2,1,0:T(8,128)(2,1)}, f32[4,496,128]{2,1,0:T(8,128)}, f32[8,128]{1,0:T(8,128)}, bf16[4,496,512]{2,1,0:T(8,128)(2,1)}) custom-call(bf16[4,496,128]{2,1,0:T(8,128)(2,1)} %multiply_convert_fusion.v_ref, bf16[512,1152]{1,0:T(8,128)(2,1)} %all-gather.13.cloned.1.call-done.w_ref, f32[8,128]{1,0:T(8,128)} %select_maximum_fusion.2.gb_ref, ...), custom_call_target="tpu_custom_call" | custom-call | flops 2340421632 | bytes 8388608 | tf_op jit(solution)/shard_map/layer_forward/pallas_call | solution.py:425
  209.2 15.2 %all-gather.15.cloned.1.call-done.w_ref = bf16[512,1152]{1,0:T(8,128)(2,1)} async-done(((bf16[64,1152]{1,0:T(8,128)(2,1)}), bf16[512,1152]{1,0:T(8,128)(2,1)}) %all-gather.15.cloned.1.call-update) | async-done | bytes 1179664 | tf_op jit(solution)/shard_map/all_gather | solution.py:512
  224.4 28.0 %layer_forward.10 = (bf16[4,496,128]{2,1,0:T(8,128)(2,1)}, f32[4,496,128]{2,1,0:T(8,128)}, f32[8,128]{1,0:T(8,128)}, bf16[4,496,512]{2,1,0:T(8,128)(2,1)}) custom-call(bf16[4,496,128]{2,1,0:T(8,128)(2,1)} %get-tuple-element.53.v_ref, bf16[512,1152]{1,0:T(8,128)(2,1)} %all-gather.15.cloned.1.call-done.w_ref, f32[8,128]{1,0:T(8,128)} %select_maximum_fusion.1.gb_ref, ...), custom_call_target="tpu_custom_call" | custom-call | flops 2340421632 | bytes 8388608 | tf_op jit(solution)/shard_map/layer_forward/pallas_call | solution.py:425
  252.4 14.5 %all-gather.17.cloned.1.call-done.w_ref = bf16[512,1152]{1,0:T(8,128)(2,1)} async-done(((bf16[64,1152]{1,0:T(8,128)(2,1)}), bf16[512,1152]{1,0:T(8,128)(2,1)}) %all-gather.17.cloned.1.call-update) | async-done | bytes 1179664 | tf_op jit(solution)/shard_map/all_gather | solution.py:512
  267.0 28.1 %layer_forward.11 = (bf16[4,496,128]{2,1,0:T(8,128)(2,1)}, f32[4,496,128]{2,1,0:T(8,128)}, f32[8,128]{1,0:T(8,128)}, bf16[4,496,512]{2,1,0:T(8,128)(2,1)}) custom-call(bf16[4,496,128]{2,1,0:T(8,128)(2,1)} %get-tuple-element.54.v_ref, bf16[512,1152]{1,0:T(8,128)(2,1)} %all-gather.17.cloned.1.call-done.w_ref, f32[8,128]{1,0:T(8,128)} %select_maximum_fusion.gb_ref, ...), custom_call_target="tpu_custom_call" | custom-call | flops 2340421632 | bytes 8388608 | tf_op jit(solution)/shard_map/layer_forward/pallas_call | solution.py:425
  295.0 33.3 %layer_backward.6 = (f32[4,496,128]{2,1,0:T(8,128)}, bf16[512,1152]{1,0:T(8,128)(2,1)}, f32[8,128]{1,0:T(8,128)}) custom-call(f32[4,496,128]{2,1,0:T(8,128)} %pad_convert_fusion.g_ref, f32[4,496,128]{2,1,0:T(8,128)} %get-tuple-element.56.z_ref, f32[8,128]{1,0:T(8,128)} %get-tuple-element.57.stat_ref, f32[8,128]{1,0:T(8,128)} %select_maximum_fusion.gb_ref, ...), custom_call_target="tpu_custom_call" | custom-call | flops 4680843264 | bytes 8388608 | tf_op jit(solution)/shard_map/layer_backward/pallas_call | solution.py:462
  328.5 32.8 %layer_backward.7 = (f32[4,496,128]{2,1,0:T(8,128)}, bf16[512,1152]{1,0:T(8,128)(2,1)}, f32[8,128]{1,0:T(8,128)}) custom-call(f32[4,496,128]{2,1,0:T(8,128)} %get-tuple-element.59.g_ref, f32[4,496,128]{2,1,0:T(8,128)} %get-tuple-element.60.z_ref, f32[8,128]{1,0:T(8,128)} %get-tuple-element.61.stat_ref, f32[8,128]{1,0:T(8,128)} %select_maximum_fusion.1.gb_ref, ...), custom_call_target="tpu_custom_call" | custom-call | flops 4680843264 | bytes 8388608 | tf_op jit(solution)/shard_map/layer_backward/pallas_call | solution.py:462
  361.5 31.7 %layer_backward.8 = (f32[4,496,128]{2,1,0:T(8,128)}, bf16[512,1152]{1,0:T(8,128)(2,1)}, f32[8,128]{1,0:T(8,128)}) custom-call(f32[4,496,128]{2,1,0:T(8,128)} %get-tuple-element.63.g_ref, f32[4,496,128]{2,1,0:T(8,128)} %get-tuple-element.64.z_ref, f32[8,128]{1,0:T(8,128)} %get-tuple-element.65.stat_ref, f32[8,128]{1,0:T(8,128)} %select_maximum_fusion.2.gb_ref, ...), custom_call_target="tpu_custom_call" | custom-call | flops 4680843264 | bytes 8388608 | tf_op jit(solution)/shard_map/layer_backward/pallas_call | solution.py:462
  393.6 1.6 multiply_reduce_fusion
  395.1 1.5 multiply_multiply_fusion.g_ref
  396.7 32.3 %layer_backward.9 = (f32[4,496,128]{2,1,0:T(8,128)}, bf16[512,1152]{1,0:T(8,128)(2,1)}, f32[8,128]{1,0:T(8,128)}) custom-call(f32[4,496,128]{2,1,0:T(8,128)} %multiply_multiply_fusion.g_ref, f32[4,496,128]{2,1,0:T(8,128)} %get-tuple-element.51.z_ref, f32[8,128]{1,0:T(8,128)} %get-tuple-element.52.stat_ref, f32[8,128]{1,0:T(8,128)} %select_maximum_fusion.3.gb_ref, ...), custom_call_target="tpu_custom_call" | custom-call | flops 4680843264 | bytes 8388608 | tf_op jit(solution)/shard_map/layer_backward/pallas_call | solution.py:462
  429.5 31.8 %layer_backward.10 = (f32[4,496,128]{2,1,0:T(8,128)}, bf16[512,1152]{1,0:T(8,128)(2,1)}, f32[8,128]{1,0:T(8,128)}) custom-call(f32[4,496,128]{2,1,0:T(8,128)} %get-tuple-element.69.g_ref, f32[4,496,128]{2,1,0:T(8,128)} %get-tuple-element.70.z_ref, f32[8,128]{1,0:T(8,128)} %get-tuple-element.71.stat_ref, f32[8,128]{1,0:T(8,128)} %select_maximum_fusion.4.gb_ref, ...), custom_call_target="tpu_custom_call" | custom-call | flops 4680843264 | bytes 8388608 | tf_op jit(solution)/shard_map/layer_backward/pallas_call | solution.py:462
  461.5 33.0 %layer_backward.11 = (f32[4,496,128]{2,1,0:T(8,128)}, bf16[512,1152]{1,0:T(8,128)(2,1)}, f32[8,128]{1,0:T(8,128)}) custom-call(f32[4,496,128]{2,1,0:T(8,128)} %get-tuple-element.73.g_ref, f32[4,496,128]{2,1,0:T(8,128)} %get-tuple-element.74.z_ref, f32[8,128]{1,0:T(8,128)} %get-tuple-element.75.stat_ref, f32[8,128]{1,0:T(8,128)} %select_maximum_fusion.5.gb_ref, ...), custom_call_target="tpu_custom_call" | custom-call | flops 4680843264 | bytes 8388608 | tf_op jit(solution)/shard_map/layer_backward/pallas_call | solution.py:462
  494.8 1.1 reshape.326
  495.8 1.3 fusion
  497.3 1.1 reshape.328
  498.4 0.8 fusion.1
  499.1 0.8 fusion.2
  499.9 0.8 fusion.3
  500.7 0.6 pad_maximum_fusion.5
  501.3 0.6 pad_maximum_fusion.4
  501.8 0.8 fusion.4
  502.6 0.8 fusion.5
  503.4 0.8 fusion.6
  504.1 0.6 pad_maximum_fusion.3
  504.7 0.6 pad_maximum_fusion.2
  505.3 1.0 reshape.352
  506.5 1.0 reshape.350
  507.7 16.9 %reduce-scatter.13.cloned.1.call-done = bf16[64,1152]{1,0:T(8,128)(2,1)} async-done(((bf16[512,1152]{1,0:T(8,128)(2,1)}), bf16[64,1152]{1,0:T(8,128)(2,1)}) %reduce-scatter.13.cloned.1.call-update) | async-done | bytes 147472 | tf_op jit(solution)/shard_map/reduce_scatter | solution.py:544
  524.5 1.0 reshape.348
  525.8 1.2 copy.82
  527.0 63.8 %reduce-scatter.11.cloned.1.call-done = bf16[64,1152]{1,0:T(8,128)(2,1)} async-done(((bf16[512,1152]{1,0:T(8,128)(2,1)}), bf16[64,1152]{1,0:T(8,128)(2,1)}) %reduce-scatter.11.cloned.1.call-update) | async-done | bytes 147472 | tf_op jit(solution)/shard_map/reduce_scatter | solution.py:544
  590.8 1.0 reshape.346
  592.0 65.2 %reduce-scatter.9.cloned.1.call-done = bf16[64,1152]{1,0:T(8,128)(2,1)} async-done(((bf16[512,1152]{1,0:T(8,128)(2,1)}), bf16[64,1152]{1,0:T(8,128)(2,1)}) %reduce-scatter.9.cloned.1.call-update) | async-done | bytes 147472 | tf_op jit(solution)/shard_map/reduce_scatter | solution.py:544
  657.2 1.0 reshape.344
  658.4 65.1 %reduce-scatter.7.cloned.1.call-done = bf16[64,1152]{1,0:T(8,128)(2,1)} async-done(((bf16[512,1152]{1,0:T(8,128)(2,1)}), bf16[64,1152]{1,0:T(8,128)(2,1)}) %reduce-scatter.7.cloned.1.call-update) | async-done | bytes 147472 | tf_op jit(solution)/shard_map/reduce_scatter | solution.py:544
  723.5 1.0 reshape.342
  724.7 1.2 copy.81
  (88 shorter events, 5.4 us)
Async XLA Ops:
  7.2 3.5 copy-start.4
  7.2 44.4 %all-gather.7.cloned.1.call-start = ((), (), s32[]{:S(2)}) async-start(), calls=%async_computation.6 | async-start | bytes 1327104 | tf_op jit(solution)/shard_map/all_gather | solution.py:512
  9.1 3.9 copy-start.10
  9.1 3.9 copy-start.11
  9.1 3.9 copy-start.12
  9.1 86.7 %all-gather.9.cloned.1.call-start = ((), (), s32[]{:S(2)}) async-start(), calls=%async_computation.7 | async-start | bytes 1327104 | tf_op jit(solution)/shard_map/all_gather | solution.py:512
  9.1 4.2 copy-start.5
  9.9 128.8 %all-gather.11.cloned.1.call-start = ((), (), s32[]{:S(2)}) async-start(), calls=%async_computation.8 | async-start | bytes 1327104 | tf_op jit(solution)/shard_map/all_gather | solution.py:512
  10.6 4.2 copy-start.1
  10.6 170.6 %all-gather.13.cloned.1.call-start = ((), (), s32[]{:S(2)}) async-start(), calls=%async_computation.9 | async-start | bytes 1327104 | tf_op jit(solution)/shard_map/all_gather | solution.py:512
  11.4 213.0 %all-gather.15.cloned.1.call-start = ((), (), s32[]{:S(2)}) async-start(), calls=%async_computation.10 | async-start | bytes 1327104 | tf_op jit(solution)/shard_map/all_gather | solution.py:512
  12.2 3.0 copy-start.2
  12.2 254.8 %all-gather.17.cloned.1.call-start = ((), (), s32[]{:S(2)}) async-start(), calls=%async_computation.11 | async-start | bytes 1327104 | tf_op jit(solution)/shard_map/all_gather | solution.py:512
  12.9 492.4 %reduce-scatter.17.cloned.1.call-start = ((), (), s32[]{:S(2)}) async-start(), calls=%async_computation.17 | async-start | bytes 1327104 | tf_op jit(solution)/shard_map/reduce_scatter | solution.py:544
  15.2 1.5 copy-start.8
  15.2 1.5 copy-start.9
  15.3 3.3 copy-start.6
  15.3 3.2 copy-start.7
  328.4 178.1 %reduce-scatter.15.cloned.1.call-start = ((), (), s32[]{:S(2)}) async-start(), calls=%async_computation.16 | async-start | bytes 1327104 | tf_op jit(solution)/shard_map/reduce_scatter | solution.py:544
  361.3 163.3 %reduce-scatter.13.cloned.1.call-start = ((), (), s32[]{:S(2)}) async-start(), calls=%async_computation.15 | async-start | bytes 1327104 | tf_op jit(solution)/shard_map/reduce_scatter | solution.py:544
  393.2 1.9 copy-start
  393.3 197.6 %reduce-scatter.11.cloned.1.call-start = ((), (), s32[]{:S(2)}) async-start(), calls=%async_computation.14 | async-start | bytes 1327104 | tf_op jit(solution)/shard_map/reduce_scatter | solution.py:544
  429.0 228.2 %reduce-scatter.9.cloned.1.call-start = ((), (), s32[]{:S(2)}) async-start(), calls=%async_computation.13 | async-start | bytes 1327104 | tf_op jit(solution)/shard_map/reduce_scatter | solution.py:544
  461.3 262.2 %reduce-scatter.7.cloned.1.call-start = ((), (), s32[]{:S(2)}) async-start(), calls=%async_computation.12 | async-start | bytes 1327104 | tf_op jit(solution)/shard_map/reduce_scatter | solution.py:544
  461.5 33.0 %copy-start.3 = (bf16[4,496,128]{2,1,0:T(8,128)(2,1)S(1)}, bf16[4,496,128]{2,1,0:T(8,128)(2,1)}, u32[]{:S(2)}) copy-start(bf16[4,496,128]{2,1,0:T(8,128)(2,1)} %get-tuple-element.55) | copy-start | bytes 1523716
Sparse Core Ops, SparseCore 0:
  10.8 40.7 all-gather.6
  54.3 41.3 all-gather.8
  98.0 40.6 all-gather.10
  140.7 40.4 all-gather.12
  183.3 41.1 all-gather.14
  226.5 40.4 all-gather.16
  328.5 62.6 reduce-scatter.16
  394.6 63.4 reduce-scatter.14
  461.5 62.9 reduce-scatter.12
  527.8 62.9 reduce-scatter.10
  594.2 62.9 reduce-scatter.8
  660.4 62.9 reduce-scatter.6

commit v2 on v1

v2 whole, which is shorter than its diff:
```python
import functools

import jax
import jax.numpy as jnp
from jax import lax
from jax.experimental import pallas as pl
from jax.experimental.pallas import tpu as pltpu
from jax.sharding import PartitionSpec as P

SIZES = ((15, 20), (18, 24), (30, 40))
WIDTHS = tuple(w for _, w in SIZES)
EDGE = 48
EPSILON = 1e-05
MESH = pl.DeviceIdType.MESH
F32 = jnp.float32
BF16 = jnp.bfloat16
LANE = 128
(M_W0, M_W1, M_UP, M_DOWN, M_LEFT, M_RIGHT, M_VALID) = range(7)


def ceil_to(value, step):
    return -(-value // step) * step


def window_masks(image_group, first_window, count, padded):
    chosen = (image_group[:, None] == jnp.arange(3, dtype=jnp.int32)[None, :]).astype(jnp.int32)
    heights = jnp.sum(chosen * jnp.array([h for h, _ in SIZES], jnp.int32)[None, :], axis=1)
    widths = jnp.sum(chosen * jnp.array(WIDTHS, jnp.int32)[None, :], axis=1)
    areas = heights * widths
    ends = jnp.cumsum(areas)
    starts = ends - areas
    local = jnp.arange(padded + 2 * EDGE, dtype=jnp.int32) - EDGE
    windows = local + first_window
    member = ((windows[:, None] >= starts[None, :]) & (windows[:, None] < ends[None, :])).astype(jnp.int32)
    base = jnp.sum(member * starts[None, :], axis=1)
    height = jnp.sum(member * heights[None, :], axis=1)
    width = jnp.sum(member * widths[None, :], axis=1)
    inside = width > 0
    position = windows - base
    safe = jnp.maximum(width, 1)
    row = position // safe
    column = position - row * safe
    masks = [
        width == WIDTHS[0],
        width == WIDTHS[1],
        inside & (row > 0),
        inside & (row < height - 1),
        inside & (column > 0),
        inside & (column < width - 1),
        (local >= 0) & (local < count),
    ]
    table = jnp.stack([m.astype(F32) for m in masks], axis=1)
    return jnp.pad(table, ((0, 0), (0, LANE - len(masks))))


def to_planes(stream, count, padded):
    planes = jnp.transpose(stream.reshape(count, 4, stream.shape[1]), (1, 0, 2))
    return jnp.pad(planes, ((0, 0), (0, padded - count), (0, 0)))


def to_stream(planes, count):
    return jnp.transpose(planes[:, :count], (1, 0, 2)).reshape(4 * count, planes.shape[2])


def mask_of(mask_ref, which, low, count):
    return mask_ref[low : low + count, which : which + 1] > 0.5


def by_width(mask_ref, low, count, shifted):
    return jnp.where(
        mask_of(mask_ref, M_W0, low, count),
        shifted(WIDTHS[0]),
        jnp.where(mask_of(mask_ref, M_W1, low, count), shifted(WIDTHS[1]), shifted(WIDTHS[2])),
    )


def row_peers(rows):
    here = lax.axis_index("rows")
    there = lax.axis_index("grp")
    return [(lax.rem(here + k, rows), there) for k in range(1, rows)]


def grp_peers():
    here = lax.axis_index("rows")
    mine = lax.axis_index("grp")
    half, core = mine // 2, lax.rem(mine, 2)
    return (here, half * 2 + 1 - core), (here, (1 - half) * 2 + core)


def greet(peers):
    barrier = pltpu.get_barrier_semaphore()
    for peer in peers:
        pl.semaphore_signal(barrier, inc=1, device_id=peer, device_id_type=MESH)
    pl.semaphore_wait(barrier, len(peers))


def remote(src, dst, send, recv, peer):
    return pltpu.make_async_remote_copy(
        src_ref=src, dst_ref=dst, send_sem=send, recv_sem=recv, device_id=peer, device_id_type=MESH
    )


def exchange_sums(rows, own, buf, send, recv):
    buf[0] = own
    copies = []
    for k, peer in enumerate(row_peers(rows)):
        copy = remote(buf.at[0], buf.at[k + 1], send.at[k], recv.at[k], peer)
        copy.start()
        copies.append(copy)
    for copy in copies:
        copy.wait()
    total = buf[0]
    for k in range(1, rows):
        total = total + buf[k]
    return total


def row_parts(padded, count):
    tail = (count - EDGE) // 16 * 16
    parts = [(0, EDGE), (tail, padded - tail)]
    start, steps = EDGE, 3
    for k in range(steps):
        size = min(ceil_to(-(-(tail - start) // (steps - k)), 16), tail - start)
        parts.append((start, size))
        start += size
    return parts


def lanes_of(block):
    return pl.ds(pl.multiple_of(block * LANE, LANE), LANE)


class Gather:
    def __init__(self, rows, shard, buf, send, recv, pass_send, pass_recv):
        self.shard, self.buf = shard, buf
        self.far = rows // 2
        here, there = lax.axis_index("rows"), lax.axis_index("grp")
        self.high, self.low = here // 2, lax.rem(here, 2)
        self.there = there
        self.send, self.recv, self.pass_send, self.pass_recv = send, recv, pass_send, pass_recv

    def rows_of(self, step, low):
        block = lax.rem(self.high + step, self.far) * 2 + low
        return pl.ds(pl.multiple_of(block * self.shard, 16), self.shard)

    def spread(self, layer, step):
        own = self.buf.at[layer, self.rows_of(0, self.low), :]
        peer = (lax.rem(self.high + step, self.far) * 2 + self.low, self.there)
        k = step - 1
        return remote(own, own, self.send.at[layer, k], self.recv.at[layer, k], peer)

    def across(self, layer, step):
        piece = self.buf.at[layer, self.rows_of(self.far - step, self.low), :]
        peer = (self.high * 2 + 1 - self.low, self.there)
        return remote(piece, piece, self.pass_send.at[layer, step], self.pass_recv.at[layer, step], peer)

    def start(self, layer, own):
        self.buf[layer, self.rows_of(0, self.low), :] = own
        for step in range(1, self.far):
            self.spread(layer, step).start()
        self.across(layer, 0).start()

    def forward(self, layer, step):
        self.spread(layer, step).wait_recv()
        self.across(layer, step).start()

    def wait(self, layer):
        for step in range(self.far):
            self.across(layer, step).wait_recv()

    def drain(self, layer):
        for step in range(1, self.far):
            self.spread(layer, step).wait_send()
        for step in range(self.far):
            self.across(layer, step).wait_send()


class Scatter:
    def __init__(self, rows, shard, grads, first, second, third, out, send, recv, far_send, far_recv):
        self.shard, self.grads, self.first, self.second, self.third = shard, grads, first, second, third
        self.out, self.far = out, rows // 2
        here, self.there = lax.axis_index("rows"), lax.axis_index("grp")
        self.high, self.low = here // 2, lax.rem(here, 2)
        self.send, self.recv, self.far_send, self.far_recv = send, recv, far_send, far_recv

    def rows_of(self, step, low):
        block = lax.rem(self.high + step, self.far) * 2 + low
        return pl.ds(pl.multiple_of(block * self.shard, 16), self.shard)

    def across(self, slot, step):
        peer = (self.high * 2 + 1 - self.low, self.there)
        return remote(
            self.grads.at[slot, self.rows_of(step, 1 - self.low), :], self.first.at[slot, step],
            self.send.at[slot, step], self.recv.at[slot, step], peer,
        )

    def spread(self, slot, step):
        peer = (lax.rem(self.high + step, self.far) * 2 + self.low, self.there)
        k = step - 1
        return remote(
            self.second.at[slot, k], self.third.at[slot, k],
            self.far_send.at[slot, k], self.far_recv.at[slot, k], peer,
        )

    def order(self):
        return list(range(1, self.far)) + [0]

    def start(self, slot):
        for step in self.order():
            self.across(slot, step).start()

    def forward(self, slot, step):
        self.across(slot, step).wait_recv()
        total = self.grads[slot, self.rows_of(step, self.low), :].astype(F32) + self.first[slot, step].astype(F32)
        if step == 0:
            self.out[slot] = total
        else:
            self.second[slot, step - 1] = total.astype(BF16)
            self.spread(slot, step).start()

    def finish(self, slot):
        total = self.out[slot]
        for step in range(1, self.far):
            self.spread(slot, step).wait_recv()
            total = total + self.third[slot, step - 1].astype(F32)
        self.out[slot] = total

    def drain(self, slot):
        for step in range(self.far):
            self.across(slot, step).wait_send()
        for step in range(1, self.far):
            self.spread(slot, step).wait_send()


def each(count, body):
    lax.fori_loop(0, count, lambda i, carry: (body(i), carry)[1], 0)


def forward_kernel(
    inside, layers, rows, count, padded, pixels,
    v_ref, w_ref, gb_ref, mask_ref,
    next_ref, stat_ref, z_out, full_out, w_out,
    vbuf, wbuf, zbuf, yext, over, under, to_next, to_prev, from_prev, from_next, sums,
    core_s, core_r, x_s, x_r, fwd_s, fwd_r, halo_s, halo_r, sum_s, sum_r, out_sem,
    w_s, w_r, wp_s, wp_r,
):
    mine, here = lax.axis_index("grp"), lax.axis_index("rows")
    half = mine // 2
    partner, across = grp_peers()
    parts = row_parts(padded, count)
    own_lanes, far_lanes = lanes_of(mine), lanes_of(across[1])
    own_base = pl.multiple_of(half * 2 * LANE, 2 * LANE)
    far_base = pl.multiple_of((1 - half) * 2 * LANE, 2 * LANE)
    gather = Gather(rows, w_ref.shape[1], wbuf, w_s, w_r, wp_s, wp_r)

    def slab(layer, k, lanes):
        low, size = parts[k]
        return vbuf.at[layer, :, pl.ds(low, size), lanes]

    def to_core(layer, k):
        piece = slab(layer, k, own_lanes)
        return remote(piece, piece, core_s.at[layer, k], core_r.at[layer, k], partner)

    def to_far(layer, k):
        piece = slab(layer, k, own_lanes)
        return remote(piece, piece, x_s.at[layer, k], x_r.at[layer, k], across)

    def pass_on(layer, k):
        piece = slab(layer, k, far_lanes)
        return remote(piece, piece, fwd_s.at[layer, k], fwd_r.at[layer, k], partner)

    def load(layer):
        return pltpu.make_async_copy(w_ref.at[layer], wbuf.at[layer], w_s.at[layer, 0])

    def saves(layer):
        pairs = [(vbuf.at[layer], full_out.at[layer]), (zbuf.at[layer], z_out.at[layer])]
        if inside:
            pairs.append((wbuf.at[layer], w_out.at[layer]))
        return [pltpu.make_async_copy(src, dst, out_sem.at[layer, k]) for k, (src, dst) in enumerate(pairs)]

    after = (lax.rem(here + 1, rows), mine)
    before = (lax.rem(here + rows - 1, rows), mine)
    down = remote(to_next, from_prev, halo_s.at[0], halo_r.at[0], after)
    up = remote(to_prev, from_next, halo_s.at[1], halo_r.at[1], before)

    def add_products(layer, low, size, base, touched):
        for q in range(4):
            a, b = q // 2, q % 2
            left = vbuf[layer, q, low : low + size, pl.ds(base, 2 * LANE)]
            for step in range(3):
                right = wbuf[layer, pl.ds(base, 2 * LANE), step * 3 * LANE : (step + 1) * 3 * LANE]
                product = jnp.dot(left, right, preferred_element_type=F32)
                for column in range(3):
                    spot = (a + step) * 4 + b + column
                    block = product[:, column * LANE : (column + 1) * LANE]
                    where = (slice(EDGE + low, EDGE + low + size), slice(spot * LANE, (spot + 1) * LANE))
                    if spot in touched:
                        yext[where] += block
                    else:
                        yext[where] = block
                        touched.add(spot)

    def at(low, size, spot):
        return yext[low : low + size, spot * LANE : (spot + 1) * LANE]

    greet([partner, across] + row_peers(rows))
    vbuf[0, :, :, own_lanes] = v_ref[...]
    for k in range(len(parts)):
        to_far(0, k).start()
        to_core(0, k).start()
    if inside:
        gather.start(0, w_ref[0])
    else:
        load(0).start()
    yext[:EDGE, :] = jnp.zeros((EDGE, yext.shape[1]), F32)
    yext[EDGE + padded :, :] = jnp.zeros((EDGE, yext.shape[1]), F32)
    if inside:
        for step in range(1, rows // 2):
            gather.forward(0, step)

    def layer_step(layer):
        more = layer + 1 < layers
        if inside:
            gather.wait(layer)
            saves(layer)[2].start()

            @pl.when(more)
            def _():
                gather.start(layer + 1, w_ref[layer + 1])
        else:
            load(layer).wait()

            @pl.when(more)
            def _():
                load(layer + 1).start()

        for k in range(len(parts)):
            to_core(layer, k).wait_recv()
        add_products(layer, 0, padded, own_base, set())

        def far_products(k):
            pass_on(layer, k).wait_recv()
            low, size = parts[k]
            add_products(layer, low, size, far_base, set(range(16)))
            if k != 1:
                return
            to_next[:, : 4 * LANE] = yext[count : count + EDGE, 12 * LANE :]
            to_next[:, 4 * LANE : 5 * LANE] = at(count, EDGE, 7)
            to_next[:, 5 * LANE :] = at(count, EDGE, 11)
            to_prev[:, : 4 * LANE] = yext[EDGE : 2 * EDGE, : 4 * LANE]
            to_prev[:, 4 * LANE : 5 * LANE] = at(EDGE, EDGE, 4)
            to_prev[:, 5 * LANE :] = at(EDGE, EDGE, 8)

            @pl.when(here + 1 < rows)
            def _():
                down.start()

            @pl.when(here > 0)
            def _():
                up.start()

        for k in range(len(parts)):
            to_far(layer, k).wait_recv()
            pass_on(layer, k).start()
            if k > 0:
                far_products(k - 1)
            step = k - (len(parts) - (rows // 2))
            if inside and step >= 1:

                @pl.when(more)
                def _():
                    gather.forward(layer + 1, step)
        far_products(len(parts) - 1)
        saves(layer)[0].start()

        @pl.when(here > 0)
        def _():
            down.wait_recv()
            up.wait_send()
            yext[:EDGE, 12 * LANE :] = from_prev[:, : 4 * LANE]
            yext[:EDGE, 7 * LANE : 8 * LANE] = from_prev[:, 4 * LANE : 5 * LANE]
            yext[:EDGE, 11 * LANE : 12 * LANE] = from_prev[:, 5 * LANE :]

        @pl.when(here + 1 < rows)
        def _():
            up.wait_recv()
            down.wait_send()
            beyond = slice(EDGE + count, 2 * EDGE + count)
            yext[beyond, : 4 * LANE] = from_next[:, : 4 * LANE]
            yext[beyond, 4 * LANE : 5 * LANE] = from_next[:, 4 * LANE : 5 * LANE]
            yext[beyond, 8 * LANE : 9 * LANE] = from_next[:, 5 * LANE :]

        low, size = 8, padded + 2 * EDGE - 16
        go_left = mask_of(mask_ref, M_LEFT, low, size)
        go_right = mask_of(mask_ref, M_RIGHT, low, size)
        for kept, first in ((over, 12), (under, 0)):
            kept[low : low + size, :LANE] = at(low, size, first + 1) + jnp.where(
                go_left, at(low - 1, size, first + 3), 0.0
            )
            kept[low : low + size, LANE:] = at(low, size, first + 2) + jnp.where(
                go_right, at(low + 1, size, first), 0.0
            )
        go_left = mask_of(mask_ref, M_LEFT, EDGE, padded)
        go_right = mask_of(mask_ref, M_RIGHT, EDGE, padded)
        valid = mask_of(mask_ref, M_VALID, EDGE, padded)
        total = jnp.zeros((1, LANE), F32)
        squares = jnp.zeros((1, LANE), F32)
        for q in range(4):
            a, b = q // 2, q % 2
            lanes = slice(b * LANE, (b + 1) * LANE)
            kept, sign = (over, -1) if a == 0 else (under, 1)
            rowwise = by_width(
                mask_ref, EDGE, padded,
                lambda w: kept[EDGE + sign * w : EDGE + sign * w + padded, lanes],
            )
            z = at(EDGE, padded, (a + 1) * 4 + b + 1)
            z = z + jnp.where(mask_of(mask_ref, (M_UP, M_DOWN)[a], EDGE, padded), rowwise, 0.0)
            if b == 0:
                z = z + jnp.where(go_left, at(EDGE - 1, padded, (a + 1) * 4 + 3), 0.0)
            else:
                z = z + jnp.where(go_right, at(EDGE + 1, padded, (a + 1) * 4), 0.0)
            z = jnp.where(valid, z, 0.0)
            zbuf[layer, q] = z
            total = total + jnp.sum(z, axis=0, keepdims=True)
            squares = squares + jnp.sum(z * z, axis=0, keepdims=True)
        saves(layer)[1].start()
        both = exchange_sums(
            rows, jnp.concatenate([total, squares, jnp.zeros((6, LANE), F32)], axis=0),
            sums.at[layer], sum_s.at[layer], sum_r.at[layer],
        )
        mean = both[0:1] / pixels
        inverse = lax.rsqrt(both[1:2] / pixels - mean * mean + EPSILON)
        stat_ref[layer] = jnp.concatenate([mean, inverse, jnp.zeros((6, LANE), F32)], axis=0)

        def activation(k, q):
            low, size = parts[k]
            y = gb_ref[layer, 0:1] * ((zbuf[layer, q, low : low + size] - mean) * inverse) + gb_ref[layer, 1:2]
            keep = mask_of(mask_ref, M_VALID, EDGE + low, size)
            return jnp.where(keep, y * jax.nn.sigmoid(y), 0.0).astype(BF16)

        @pl.when(more)
        def _():
            for k, (low, size) in enumerate(parts):
                for q in range(4):
                    vbuf[layer + 1, q, low : low + size, own_lanes] = activation(k, q)
                to_far(layer + 1, k).start()
                to_core(layer + 1, k).start()

        @pl.when(layer + 1 == layers)
        def _():
            for k, (low, size) in enumerate(parts):
                for q in range(4):
                    next_ref[q, low : low + size] = activation(k, q)

    each(layers, layer_step)

    def drain(layer):
        for k in range(len(parts)):
            to_far(layer, k).wait_send()
            to_core(layer, k).wait_send()
            pass_on(layer, k).wait_send()
        if inside:
            gather.drain(layer)
        for copy in saves(layer):
            copy.wait()

    each(layers, drain)


def backward_kernel(
    inside, pending, flush, layers, rows, count, padded, pixels, *refs
):
    refs = list(refs)
    g_ref, stat_ref, gb_ref, mask_ref, z_in, full_in, w_in = refs[:7]
    del refs[:7]
    dk_in = refs.pop(0) if pending else None
    grad_ref, gbgrad_ref = refs.pop(0), refs.pop(0)
    wgrad_ref = refs.pop(0) if inside else None
    dk_out = None if flush else refs.pop(0)
    (
        zbuf, fbuf, wbuf, dk, gy, gext, above, below, patch, part, keep, core_out, core_in, x_out, x_in,
        to_next, to_prev, from_prev, from_next, sums,
        core_s, core_r, x_s, x_r, halo_s, halo_r, sum_s, sum_r, load_sem, out_sem,
    ) = refs[:30]
    mine, here = lax.axis_index("grp"), lax.axis_index("rows")
    half, core = mine // 2, lax.rem(mine, 2)
    partner, across = grp_peers()
    own_lanes, other_lanes = lanes_of(core), lanes_of(1 - core)
    own_base = pl.multiple_of(half * 2 * LANE, 2 * LANE)
    far_base = pl.multiple_of((1 - half) * 2 * LANE, 2 * LANE)
    scatter = None
    if inside:
        first, second, third, s1, r1, s2, r2 = refs[30:]
        scatter = Scatter(rows, dk.shape[1] // rows, dk, first, second, third, wgrad_ref, s1, r1, s2, r2)

    def loads(layer):
        pairs = [(z_in, zbuf), (w_in, wbuf), (full_in, fbuf)]
        return [
            pltpu.make_async_copy(src.at[layer], dst.at[layer], load_sem.at[layer, k])
            for k, (src, dst) in enumerate(pairs)
        ]

    def dk_load():
        return pltpu.make_async_copy(dk_in, dk.at[0], out_sem)

    for layer in range(layers - 1, -1, -1):
        for copy in loads(layer):
            copy.start()
    if pending:
        dk_load().start()
    after = (lax.rem(here + 1, rows), mine)
    before = (lax.rem(here + rows - 1, rows), mine)
    down = remote(to_next, from_prev, halo_s.at[0], halo_r.at[0], after)
    up = remote(to_prev, from_next, halo_s.at[1], halo_r.at[1], before)
    grad_ref[...] = g_ref[...]
    gext[:EDGE, :] = jnp.zeros((EDGE, 4 * LANE), F32)
    gext[EDGE + padded :, :] = jnp.zeros((EDGE, 4 * LANE), F32)
    greet([partner, across] + row_peers(rows))
    if pending:
        dk_load().wait()

    def taps(q, step):
        first = (q // 2 + step) * 4 + q % 2
        return patch[:, first * LANE : (first + 3) * LANE]

    def layer_step(turn):
        layer = layers - 1 - turn
        side = lax.rem(turn, 2)
        last = turn + 1 == layers
        scattering = (turn >= 0) if pending else (turn > 0)
        mean, inverse = stat_ref[layer, 0:1], stat_ref[layer, 1:2]
        gain, shift = gb_ref[layer, 0:1], gb_ref[layer, 1:2]
        valid = mask_of(mask_ref, M_VALID, EDGE, padded)
        loads(layer)[0].wait()
        shift_sum = jnp.zeros((1, LANE), F32)
        gain_sum = jnp.zeros((1, LANE), F32)
        for q in range(4):
            normed = (zbuf[layer, q] - mean) * inverse
            y = gain * normed + shift
            s = jax.nn.sigmoid(y)
            grad = jnp.where(valid, grad_ref[q] * s * (1.0 + y * (1.0 - s)), 0.0)
            gy[q] = grad
            shift_sum = shift_sum + jnp.sum(grad, axis=0, keepdims=True)
            gain_sum = gain_sum + jnp.sum(grad * normed, axis=0, keepdims=True)
        both = exchange_sums(
            rows, jnp.concatenate([shift_sum, gain_sum, jnp.zeros((6, LANE), F32)], axis=0),
            sums.at[turn], sum_s.at[turn], sum_r.at[turn],
        )
        gbgrad_ref[layer] = both
        for q in range(4):
            normed = (zbuf[layer, q] - mean) * inverse
            gz = inverse * gain * (gy[q] - both[0:1] / pixels - normed * both[1:2] / pixels)
            gz = jnp.where(valid, gz, 0.0).astype(BF16).astype(F32)
            gext[EDGE : EDGE + padded, q * LANE : (q + 1) * LANE] = gz
        to_next[...] = gext[count : count + EDGE, :].astype(BF16)
        to_prev[...] = gext[EDGE : 2 * EDGE, :].astype(BF16)

        @pl.when(here + 1 < rows)
        def _():
            down.start()

        @pl.when(here > 0)
        def _():
            up.start()

        if inside:

            @pl.when(scattering)
            def _():
                scatter.start(turn)

        @pl.when(here > 0)
        def _():
            down.wait_recv()
            up.wait_send()
            gext[:EDGE, :] = from_prev[...].astype(F32)

        @pl.when(here + 1 < rows)
        def _():
            up.wait_recv()
            down.wait_send()
            gext[EDGE + count : 2 * EDGE + count, :] = from_next[...].astype(F32)

        low, size = EDGE - 8, padded + 16
        for kept, which, sign, lanes in (
            (above, M_UP, -1, slice(2 * LANE, 4 * LANE)),
            (below, M_DOWN, 1, slice(0, 2 * LANE)),
        ):
            rowwise = by_width(
                mask_ref, low, size, lambda w: gext[low + sign * w : low + sign * w + size, lanes]
            )
            kept[...] = jnp.where(mask_of(mask_ref, which, low, size), rowwise, 0.0)
        go_left = mask_of(mask_ref, M_LEFT, EDGE, padded)
        go_right = mask_of(mask_ref, M_RIGHT, EDGE, padded)
        for step, (kept, top, lane) in enumerate(
            ((above, 8, 0), (gext, EDGE, 0), (gext, EDGE, 2 * LANE), (below, 8, 0))
        ):
            even, odd = slice(lane, lane + LANE), slice(lane + LANE, lane + 2 * LANE)
            blocks = [
                jnp.where(go_left, kept[top - 1 : top - 1 + padded, odd], 0.0),
                kept[top : top + padded, even],
                kept[top : top + padded, odd],
                jnp.where(go_right, kept[top + 1 : top + 1 + padded, even], 0.0),
            ]
            for column, block in enumerate(blocks):
                spot = step * 4 + column
                patch[:, spot * LANE : (spot + 1) * LANE] = block.astype(BF16)

        def kernel_grad(step):
            total = None
            for q in range(4):
                product = lax.dot_general(
                    fbuf[layer, q], taps(q, step), (((0,), (0,)), ((), ())), preferred_element_type=F32
                )
                total = product if total is None else total + product
            dk[turn + 1, :, step * 3 * LANE : (step + 1) * 3 * LANE] = total.astype(BF16)

        loads(layer)[1].wait()
        loads(layer)[2].wait()
        if flush:

            @pl.when(last)
            def _():
                for step in range(3):
                    kernel_grad(step)
                if inside:
                    scatter.start(layers)

        def input_grad(q, base):
            total = None
            for step in range(3):
                right = wbuf[layer, pl.ds(base, 2 * LANE), step * 3 * LANE : (step + 1) * 3 * LANE]
                product = lax.dot_general(
                    taps(q, step), right, (((1,), (1,)), ((), ())), preferred_element_type=F32
                )
                total = product if total is None else total + product
            part[...] = total

        def to_core(spot):
            return remote(
                core_out.at[side, spot], core_in.at[side, spot],
                core_s.at[side, spot], core_r.at[side, spot], partner,
            )

        def to_far(q):
            return remote(x_out.at[side, q], x_in.at[side, q], x_s.at[side, q], x_r.at[side, q], across)

        def send_across(q):
            to_core(q).wait_recv()
            x_out[side, q] = (keep[q] + core_in[side, q].astype(F32)).astype(BF16)
            to_far(q).start()

        for which, base in enumerate((far_base, own_base)):
            for q in range(4):
                spot = which * 4 + q
                input_grad(q, base)
                core_out[side, spot] = part[:, other_lanes].astype(BF16)
                keep[spot] = part[:, own_lanes]
                to_core(spot).start()
                if which == 0 and q > 0:
                    send_across(q - 1)
            if which == 0:
                send_across(3)

        @pl.when(jnp.logical_not(last) if flush else turn >= 0)
        def _():
            for step in range(3):
                kernel_grad(step)

        if inside:

            @pl.when(scattering)
            def _():
                for step in scatter.order():
                    scatter.forward(turn, step)
        for q in range(4):
            to_core(4 + q).wait_recv()
            to_far(q).wait_recv()
            grad_ref[q] = keep[4 + q] + core_in[side, 4 + q].astype(F32) + x_in[side, q].astype(F32)
        for spot in range(8):
            to_core(spot).wait_send()
        for q in range(4):
            to_far(q).wait_send()
        if inside:

            @pl.when(scattering)
            def _():
                scatter.finish(turn)
                scatter.drain(turn)

    each(layers, layer_step)
    if inside and flush:
        for step in scatter.order():
            scatter.forward(layers, step)
        scatter.finish(layers)
        scatter.drain(layers)
    if not flush:
        copy = pltpu.make_async_copy(dk.at[layers] if inside else dk, dk_out, out_sem)
        copy.start()
        copy.wait()


VM = pl.BlockSpec(memory_space=pltpu.VMEM)
HBM = pl.BlockSpec(memory_space=pl.ANY)
LIMIT = 56 * 1024 * 1024
DMA = pltpu.SemaphoreType.DMA


def forward_block(inside, rows, count, padded, pixels, planes, weight, gain_shift, masks):
    layers, channels, taps = weight.shape[0], 4 * LANE, weight.shape[2]
    ext = padded + 2 * EDGE
    n_parts = len(row_parts(padded, count))
    far = rows // 2
    out = pl.pallas_call(
        functools.partial(forward_kernel, inside, layers, rows, count, padded, pixels),
        name="forward_block",
        out_shape=(
            jax.ShapeDtypeStruct((4, padded, LANE), BF16),
            jax.ShapeDtypeStruct((layers, 8, LANE), F32),
            jax.ShapeDtypeStruct((layers, 4, padded, LANE), F32),
            jax.ShapeDtypeStruct((layers, 4, padded, channels), BF16),
            jax.ShapeDtypeStruct((layers, channels, taps) if inside else (1, 16, LANE), BF16),
        ),
        in_specs=[VM, VM if inside else HBM, VM, VM],
        out_specs=(VM, VM, HBM, HBM, HBM),
        scratch_shapes=[
            pltpu.VMEM((layers, 4, padded, channels), BF16),
            pltpu.VMEM((layers, channels, taps), BF16),
            pltpu.VMEM((layers, 4, padded, LANE), F32),
            pltpu.VMEM((ext, 16 * LANE), F32),
            pltpu.VMEM((ext, 2 * LANE), F32),
            pltpu.VMEM((ext, 2 * LANE), F32),
        ]
        + [pltpu.VMEM((EDGE, 6 * LANE), F32)] * 4
        + [pltpu.VMEM((layers, rows, 8, LANE), F32)]
        + [DMA((layers, n_parts))] * 6
        + [DMA((2,))] * 2
        + [DMA((layers, rows - 1))] * 2
        + [DMA((layers, 3))]
        + [DMA((layers, far - 1))] * 2
        + [DMA((layers, far))] * 2,
        compiler_params=pltpu.CompilerParams(
            collective_id=0, has_side_effects=True, vmem_limit_bytes=LIMIT
        ),
    )(planes, weight, gain_shift, masks)
    return out[:4] + ((out[4] if inside else weight),)


def backward_block(
    inside, flush, rows, count, padded, pixels, grad, z, stat, gain_shift, masks, full, weight, dk
):
    layers, channels, taps = weight.shape
    ext = padded + 2 * EDGE
    pending = dk is not None
    shard = channels // rows
    far = rows // 2
    outs = [
        (jax.ShapeDtypeStruct((4, padded, LANE), F32), VM),
        (jax.ShapeDtypeStruct((layers, 8, LANE), F32), VM),
    ]
    if inside:
        outs.append((jax.ShapeDtypeStruct((layers + 1, shard, taps), F32), VM))
    if not flush:
        outs.append(
            (jax.ShapeDtypeStruct((channels, taps) if inside else (layers + 1, channels, taps), BF16), HBM)
        )
    scratch = [
        pltpu.VMEM((layers, 4, padded, LANE), F32),
        pltpu.VMEM((layers, 4, padded, channels), BF16),
        pltpu.VMEM((layers, channels, taps), BF16),
        pltpu.VMEM((layers + 1, channels, taps), BF16),
        pltpu.VMEM((4, padded, LANE), F32),
        pltpu.VMEM((ext, 4 * LANE), F32),
        pltpu.VMEM((padded + 16, 2 * LANE), F32),
        pltpu.VMEM((padded + 16, 2 * LANE), F32),
        pltpu.VMEM((padded, 16 * LANE), BF16),
        pltpu.VMEM((padded, 2 * LANE), F32),
        pltpu.VMEM((8, padded, LANE), F32),
        pltpu.VMEM((2, 8, padded, LANE), BF16),
        pltpu.VMEM((2, 8, padded, LANE), BF16),
        pltpu.VMEM((2, 4, padded, LANE), BF16),
        pltpu.VMEM((2, 4, padded, LANE), BF16),
    ]
    scratch += [pltpu.VMEM((EDGE, 4 * LANE), BF16)] * 4
    scratch += [pltpu.VMEM((layers, rows, 8, LANE), F32)]
    scratch += [DMA((2, 8))] * 2 + [DMA((2, 4))] * 2 + [DMA((2,))] * 2 + [DMA((layers, rows - 1))] * 2
    scratch += [DMA((layers, 3)), DMA]
    if inside:
        scratch += [
            pltpu.VMEM((layers + 1, far, shard, taps), BF16),
            pltpu.VMEM((layers + 1, far - 1, shard, taps), BF16),
            pltpu.VMEM((layers + 1, far - 1, shard, taps), BF16),
        ]
        scratch += [DMA((layers + 1, far))] * 2 + [DMA((layers + 1, far - 1))] * 2
    args = [grad, stat, gain_shift, masks, z, full, weight] + ([dk] if pending else [])
    return pl.pallas_call(
        functools.partial(backward_kernel, inside, pending, flush, layers, rows, count, padded, pixels),
        name="backward_block",
        out_shape=tuple(o for o, _ in outs),
        in_specs=[VM] * 4 + [HBM] * (len(args) - 4),
        out_specs=tuple(s for _, s in outs),
        scratch_shapes=scratch,
        compiler_params=pltpu.CompilerParams(
            collective_id=2 if flush else 1, has_side_effects=True, vmem_limit_bytes=LIMIT
        ),
    )(*args)


def shards(
    features, image_group, switches, enc_weight, dec_weight,
    enc_gain, enc_bias, dec_gain, dec_bias, d_decoded,
):
    rows = lax.axis_size("rows")
    count = features.shape[0] // 4
    padded = ceil_to(count, 16)
    pixels = float(features.shape[0] * rows)
    shard = enc_weight.shape[2]
    inside = shard % 16 == 0
    sizes = (rows, count, padded, pixels)
    masks = window_masks(image_group, lax.axis_index("rows") * count, count, padded)

    def flat_weight(weight):
        flat = jnp.transpose(weight[:, ::-1], (0, 2, 1, 3)).reshape(weight.shape[0], shard, -1)
        return flat if inside else lax.all_gather(flat, "rows", axis=1, tiled=True)

    def pair(gain, shift):
        return jnp.pad(jnp.stack([gain, shift], axis=1), ((0, 0), (0, 6), (0, 0)))

    enc_pair, dec_pair = pair(enc_gain, enc_bias), pair(dec_gain, dec_bias)
    hits = switches[None, :] == jnp.arange(4, dtype=jnp.int32)[:, None]
    hits = jnp.pad(hits.astype(F32), ((0, 0), (0, padded - count)))[:, :, None]

    _, enc_stat, enc_z, enc_full, enc_w = forward_block(
        inside, *sizes, to_planes(features, count, padded), flat_weight(enc_weight), enc_pair, masks
    )
    y = enc_pair[2, 0] * ((enc_z[2] - enc_stat[2, 0]) * enc_stat[2, 1]) + enc_pair[2, 1]
    blocks = jax.nn.silu(y)
    pooled = jnp.log(jnp.mean(jnp.exp(blocks), axis=0))
    planes = (pooled[None] * hits).astype(BF16)
    planes, dec_stat, dec_z, dec_full, dec_w = forward_block(
        inside, *sizes, planes, flat_weight(dec_weight), dec_pair, masks
    )
    decoded = to_stream(planes, count)

    grad = to_planes(d_decoded, count, padded).astype(F32)
    dec_out = backward_block(
        inside, False, *sizes, grad, dec_z, dec_stat, dec_pair, masks, dec_full, dec_w, None
    )
    grad_pooled = jnp.sum(dec_out[0] * hits, axis=0)
    grad = grad_pooled[None] * jnp.exp(blocks - pooled[None]) * 0.25
    enc_out = backward_block(
        inside, inside, *sizes, grad, enc_z, enc_stat, enc_pair, masks, enc_full, enc_w,
        dec_out[-1] if inside else None,
    )
    if inside:
        dec_parts = jnp.stack([enc_out[2][0], dec_out[2][2], dec_out[2][1]])
        enc_parts = jnp.stack([enc_out[2][3], enc_out[2][2], enc_out[2][1]])
    else:
        dec_parts, enc_parts = (
            lax.psum_scatter(out[-1][:0:-1], "rows", scatter_dimension=1, tiled=True).astype(F32)
            for out in (dec_out, enc_out)
        )

    def whole_taps(parts):
        return jnp.transpose(parts.reshape(3, shard, 9, -1)[:, :, ::-1], (0, 2, 1, 3))

    return (
        decoded,
        to_stream(enc_out[0].astype(BF16), count),
        whole_taps(enc_parts),
        whole_taps(dec_parts),
        enc_out[1][:, 1],
        enc_out[1][:, 0],
        dec_out[1][:, 1],
        dec_out[1][:, 0],
    )


def solution(mesh):
    wide = P("rows", "grp")
    kernels = P(None, None, "rows", "grp")
    vector = P(None, "grp")
    return jax.shard_map(
        shards,
        mesh=mesh,
        in_specs=(wide, P(), P("rows"), kernels, kernels, vector, vector, vector, vector, wide),
        out_specs=(wide, wide, kernels, kernels, vector, vector, vector, vector),
        check_vma=False,
    )
```

time: 746 us -> 481 us (0.64)
  waiting for transfers between devices: 313 us -> 0 us
  Pallas kernels: 363 us -> 434 us
  between operations: 14.9 us -> 1.41 us
    reduce_scatter x6 -> x0, waiting for transfers between devices: 211 us -> none  [shards(): lax.psum_scatter(weight_grad, 'rows', scatter_dimension=0, tiled=True)]
    all_gather x6 -> x0, waiting for transfers between devices: 102 us -> none  [whole_weight(): return lax.all_gather(flat, 'rows', axis=0, tiled=True)]
    pallas_call x12 -> x4, Pallas kernels: 363 us -> 434 us  [the longest x2 248 us: backward_block(): pl.pallas_call(functools.partial(backward_kernel, inside, pending, flush,...]
  transfers between devices with their start and end apart: 12 -> 0, of which waited for: 10 -> 0; matrix products, arithmetic and copies ran while one was open for 5% -> 0% of each run, Pallas kernels for 41% -> 0%
where the time goes in v2:
time: 481 us; the launch traced here: 472 us
  Pallas kernels  434 us (90%)
  local copies, waits for them, and re-layouts  24.5 us (5%)
  other arithmetic  12.3 us (3%)
    pallas_call x2, Pallas kernels, backward_block(): pl.pallas_call(functools.partial(backward_kernel, inside, pending, flush,...  248 us
    pallas_call x2, Pallas kernels, forward_block(): pl.pallas_call(functools.partial(forward_kernel, inside, layers, rows, co...  186 us

profile of v2, /device:TPU:9, one launch (start us, length us, event | category | flops | bytes accessed | tf_op | source)
XLA Modules:
  0.0 471.9 jit_solution(578449371862582474)
XLA Ops:
  0.6 0.0 copy-start.5
  0.6 0.0 copy-start.3
  0.7 0.9 select_reduce_fusion.4
  1.5 0.2 reduce-window.7
  1.7 0.7 slice_bitcast_fusion.1
  2.4 0.7 stack.39
  3.1 0.7 stack.40
  3.8 0.7 stack.35
  4.5 0.7 stack.36
  5.1 0.7 iota_compare_fusion.1
  5.9 0.1 select_reduce_fusion
  6.0 0.3 reshape_and_fusion
  6.4 0.6 select_maximum_fusion.1.gb_ref.refs_2_
  7.0 0.6 select_maximum_fusion.gb_ref.refs_2_
  7.6 0.2 copy.56
  7.8 0.8 pad_convert_fusion.1.mask_ref.refs_3_
  8.5 1.8 copy_bitcast_fusion.3.w_ref
  10.4 0.0 copy-done.5
  10.4 0.8 copy_bitcast_fusion.2.w_ref
  11.2 0.0 copy-done.3
  11.2 0.3 reshape.276
  11.5 0.1 copy.78
  11.6 0.8 pad.27.v_ref
  12.4 0.0 copy-done.4
  12.4 0.3 reshape.281
  12.7 0.1 copy.77
  12.8 1.0 pad_convert_fusion.refs_0_
  13.8 93.6 %forward_block.2 = (bf16[4,496,128]{2,1,0:T(8,128)(2,1)}, f32[3,8,128]{2,1,0:T(8,128)}, f32[3,4,496,128]{3,2,1,0:T(8,128)}, bf16[3,4,496,512]{3,2,1,0:T(8,128)(2,1)}, bf16[3,512,1152]{2,1,0:T(8,128)(2,1)}) custom-call(bf16[4,496,128]{2,1,0:T(8,128)(2,1)} %pad.27.v_ref, bf16[3,64,1152]{2,1,0:T(8,128)(2,1)} %copy_bitcast_fusion.3.w_ref, ...), custom_call_target="tpu_custom_call" | custom-call | tf_op jit(solution)/shard_map/forward_block/pallas_call | solution.py:714
  107.5 0.8 slice_bitcast_fusion.3
  108.2 1.7 exponential_reduce_fusion
  110.0 1.1 multiply_convert_fusion.v_ref
  111.1 92.0 %forward_block.3 = (bf16[4,496,128]{2,1,0:T(8,128)(2,1)}, f32[3,8,128]{2,1,0:T(8,128)}, f32[3,4,496,128]{3,2,1,0:T(8,128)}, bf16[3,4,496,512]{3,2,1,0:T(8,128)(2,1)}, bf16[3,512,1152]{2,1,0:T(8,128)(2,1)}) custom-call(bf16[4,496,128]{2,1,0:T(8,128)(2,1)} %multiply_convert_fusion.v_ref, bf16[3,64,1152]{2,1,0:T(8,128)(2,1)} %copy_bitcast_fusion.2.w_ref, ...), custom_call_target="tpu_custom_call" | custom-call | tf_op jit(solution)/shard_map/forward_block/pallas_call | solution.py:714
  203.1 1.1 slice_bitcast_fusion
  204.2 0.2 copy.58
  204.4 1.1 reshape.280
  205.4 110.4 %backward_block.2 = (f32[4,496,128]{2,1,0:T(8,128)}, f32[3,8,128]{2,1,0:T(8,128)}, f32[4,64,1152]{2,1,0:T(8,128)}, bf16[512,1152]{1,0:T(8,128)(2,1)}) custom-call(f32[4,496,128]{2,1,0:T(8,128)} %pad_convert_fusion.refs_0_, f32[3,8,128]{2,1,0:T(8,128)} %get-tuple-element.27.refs_1_, f32[3,8,128]{2,1,0:T(8,128)} %select_maximum_fusion.gb_ref.refs_2_, ...), custom_call_target="tpu_custom_call" | custom-call | tf_op jit(solution)/shard_map/backward_block/pallas_call | solution.py:796
  315.8 1.6 multiply_reduce_fusion
  317.3 0.8 fusion.6
  318.1 0.6 copy.79
  318.7 0.6 copy.80
  319.3 2.6 multiply_multiply_fusion.refs_0_
  321.9 137.7 %backward_block.3 = (f32[4,496,128]{2,1,0:T(8,128)}, f32[3,8,128]{2,1,0:T(8,128)}, f32[4,64,1152]{2,1,0:T(8,128)}) custom-call(f32[4,496,128]{2,1,0:T(8,128)} %multiply_multiply_fusion.refs_0_, f32[3,8,128]{2,1,0:T(8,128)} %get-tuple-element.25.refs_1_, f32[3,8,128]{2,1,0:T(8,128)} %select_maximum_fusion.1.gb_ref.refs_2_, ...), custom_call_target="tpu_custom_call" | custom-call | tf_op jit(solution)/shard_map/backward_block/pallas_call | solution.py:796
  459.6 1.3 fusion.3
  460.9 0.0 copy-start.2
  460.9 0.2 copy.60
  461.1 1.1 reshape.282
  462.2 0.8 fusion.7
  463.0 0.6 copy.81
  463.6 0.6 copy.82
  464.1 1.1 fusion.5
  465.2 0.0 copy-done.2
  465.2 0.9 fusion.4
  466.1 0.1 pad_maximum_fusion.1
  466.2 0.2 reshape.284
  466.4 1.2 rev.15
  467.6 0.0 copy-start
  467.6 0.0 copy-start.1
  467.6 1.2 copy.62
  468.8 0.0 copy-done
  468.8 0.0 copy-done.1
  468.8 0.1 pad_maximum_fusion
  468.8 0.2 reshape.283
  469.0 1.2 rev.14
  470.2 1.2 copy.61
  (13 shorter events, 0.2 us)
Async XLA Ops:
  0.6 9.7 %copy-start.5 = (bf16[3,9,64,128]{3,2,1,0:T(8,128)(2,1)S(1)}, bf16[3,9,64,128]{3,2,1,0:T(8,128)(2,1)}, u32[]{:S(2)}) copy-start(bf16[3,9,64,128]{3,2,1,0:T(8,128)(2,1)} %param.16) | copy-start | bytes 1327108
  0.6 10.5 %copy-start.3 = (bf16[1932,128]{1,0:T(8,128)(2,1)S(1)}, bf16[1932,128]{1,0:T(8,128)(2,1)}, u32[]{:S(2)}) copy-start(bf16[1932,128]{1,0:T(8,128)(2,1)} %param.12) | copy-start | bytes 1483780
  11.2 1.2 copy-start.4
  460.9 4.3 copy-start.2
  467.6 1.2 copy-start
  467.6 1.2 copy-start.1

commit v3 on v2

--- a/solution.py
+++ b/solution.py
@@ -15,14 +15,15 @@
 F32 = jnp.float32
 BF16 = jnp.bfloat16
 LANE = 128
-(M_W0, M_W1, M_UP, M_DOWN, M_LEFT, M_RIGHT, M_VALID) = range(7)
+(M_W0, M_W1, M_UP, M_DOWN, M_LEFT, M_RIGHT, M_VALID, M_HIT) = range(8)
+POOL = 2
 
 
 def ceil_to(value, step):
     return -(-value // step) * step
 
 
-def window_masks(image_group, first_window, count, padded):
+def window_masks(image_group, switches, first_window, count, padded):
     chosen = (image_group[:, None] == jnp.arange(3, dtype=jnp.int32)[None, :]).astype(jnp.int32)
     heights = jnp.sum(chosen * jnp.array([h for h, _ in SIZES], jnp.int32)[None, :], axis=1)
     widths = jnp.sum(chosen * jnp.array(WIDTHS, jnp.int32)[None, :], axis=1)
@@ -49,6 +50,8 @@
         inside & (column < width - 1),
         (local >= 0) & (local < count),
     ]
+    kept = jnp.pad(switches, (EDGE, padded - count + EDGE), constant_values=-1)
+    masks += [kept == q for q in range(4)]
     table = jnp.stack([m.astype(F32) for m in masks], axis=1)
     return jnp.pad(table, ((0, 0), (0, LANE - len(masks))))
 
@@ -74,10 +77,16 @@
     )
 
 
+def smooth_max(blocks):
+    total = sum(jnp.exp(block) for block in blocks)
+    return jnp.log(total * 0.25)
+
+
 def row_peers(rows):
     here = lax.axis_index("rows")
     there = lax.axis_index("grp")
-    return [(lax.rem(here + k, rows), there) for k in range(1, rows)]
+    order = sorted(range(1, rows), key=lambda k: -min(k, rows - k))
+    return [(lax.rem(here + k, rows), there) for k in order]
 
 
 def grp_peers():
@@ -187,14 +196,16 @@
         block = lax.rem(self.high + step, self.far) * 2 + low
         return pl.ds(pl.multiple_of(block * self.shard, 16), self.shard)
 
-    def across(self, slot, step):
+    def across(self, turn, step):
+        slot = lax.rem(turn, 2)
         peer = (self.high * 2 + 1 - self.low, self.there)
         return remote(
             self.grads.at[slot, self.rows_of(step, 1 - self.low), :], self.first.at[slot, step],
             self.send.at[slot, step], self.recv.at[slot, step], peer,
         )
 
-    def spread(self, slot, step):
+    def spread(self, turn, step):
+        slot = lax.rem(turn, 2)
         peer = (lax.rem(self.high + step, self.far) * 2 + self.low, self.there)
         k = step - 1
         return remote(
@@ -205,31 +216,34 @@
     def order(self):
         return list(range(1, self.far)) + [0]
 
-    def start(self, slot):
+    def start(self, turn):
         for step in self.order():
-            self.across(slot, step).start()
-
-    def forward(self, slot, step):
-        self.across(slot, step).wait_recv()
-        total = self.grads[slot, self.rows_of(step, self.low), :].astype(F32) + self.first[slot, step].astype(F32)
+            self.across(turn, step).start()
+
+    def forward(self, turn, step, layer):
+        slot = lax.rem(turn, 2)
+        self.across(turn, step).wait_recv()
+        own = self.grads[slot, self.rows_of(step, self.low), :]
+        total = own.astype(F32) + self.first[slot, step].astype(F32)
         if step == 0:
-            self.out[slot] = total
+            self.out[layer] = total
         else:
             self.second[slot, step - 1] = total.astype(BF16)
-            self.spread(slot, step).start()
-
-    def finish(self, slot):
-        total = self.out[slot]
+            self.spread(turn, step).start()
+
+    def finish(self, turn, layer):
+        slot = lax.rem(turn, 2)
+        total = self.out[layer]
         for step in range(1, self.far):
-            self.spread(slot, step).wait_recv()
+            self.spread(turn, step).wait_recv()
             total = total + self.third[slot, step - 1].astype(F32)
-        self.out[slot] = total
-
-    def drain(self, slot):
+        self.out[layer] = total
+
+    def drain(self, turn):
         for step in range(self.far):
-            self.across(slot, step).wait_send()
+            self.across(turn, step).wait_send()
         for step in range(1, self.far):
-            self.spread(slot, step).wait_send()
+            self.spread(turn, step).wait_send()
 
 
 def each(count, body):
@@ -272,11 +286,10 @@
     def load(layer):
         return pltpu.make_async_copy(w_ref.at[layer], wbuf.at[layer], w_s.at[layer, 0])
 
-    def saves(layer):
-        pairs = [(vbuf.at[layer], full_out.at[layer]), (zbuf.at[layer], z_out.at[layer])]
-        if inside:
-            pairs.append((wbuf.at[layer], w_out.at[layer]))
-        return [pltpu.make_async_copy(src, dst, out_sem.at[layer, k]) for k, (src, dst) in enumerate(pairs)]
+    def save(layer, which):
+        pairs = [(vbuf, full_out), (zbuf, z_out), (wbuf, w_out)]
+        src, dst = pairs[which]
+        return pltpu.make_async_copy(src.at[layer], dst.at[layer], out_sem.at[layer, which])
 
     after = (lax.rem(here + 1, rows), mine)
     before = (lax.rem(here + rows - 1, rows), mine)
@@ -322,7 +335,7 @@
         more = layer + 1 < layers
         if inside:
             gather.wait(layer)
-            saves(layer)[2].start()
+            save(layer, 2).start()
 
             @pl.when(more)
             def _():
@@ -337,6 +350,12 @@
         for k in range(len(parts)):
             to_core(layer, k).wait_recv()
         add_products(layer, 0, padded, own_base, set())
+
+        def gather_forward(first, end):
+            @pl.when(more)
+            def _():
+                for step in range(first, end):
+                    gather.forward(layer + 1, step)
 
         def far_products(k):
             pass_on(layer, k).wait_recv()
@@ -344,12 +363,10 @@
             add_products(layer, low, size, far_base, set(range(16)))
             if k != 1:
                 return
-            to_next[:, : 4 * LANE] = yext[count : count + EDGE, 12 * LANE :]
-            to_next[:, 4 * LANE : 5 * LANE] = at(count, EDGE, 7)
-            to_next[:, 5 * LANE :] = at(count, EDGE, 11)
-            to_prev[:, : 4 * LANE] = yext[EDGE : 2 * EDGE, : 4 * LANE]
-            to_prev[:, 4 * LANE : 5 * LANE] = at(EDGE, EDGE, 4)
-            to_prev[:, 5 * LANE :] = at(EDGE, EDGE, 8)
+            for lane, spot in enumerate((12, 13, 14, 15, 7, 11)):
+                to_next[:, lane * LANE : (lane + 1) * LANE] = at(count, EDGE, spot).astype(BF16)
+            for lane, spot in enumerate((0, 1, 2, 3, 4, 8)):
+                to_prev[:, lane * LANE : (lane + 1) * LANE] = at(EDGE, EDGE, spot).astype(BF16)
 
             @pl.when(here + 1 < rows)
             def _():
@@ -364,31 +381,28 @@
             pass_on(layer, k).start()
             if k > 0:
                 far_products(k - 1)
-            step = k - (len(parts) - (rows // 2))
-            if inside and step >= 1:
-
-                @pl.when(more)
-                def _():
-                    gather.forward(layer + 1, step)
+            if inside and k == 2:
+                gather_forward(1, 2)
         far_products(len(parts) - 1)
-        saves(layer)[0].start()
+        save(layer, 0).start()
+        if inside:
+            gather_forward(2, 3)
 
         @pl.when(here > 0)
         def _():
             down.wait_recv()
             up.wait_send()
-            yext[:EDGE, 12 * LANE :] = from_prev[:, : 4 * LANE]
-            yext[:EDGE, 7 * LANE : 8 * LANE] = from_prev[:, 4 * LANE : 5 * LANE]
-            yext[:EDGE, 11 * LANE : 12 * LANE] = from_prev[:, 5 * LANE :]
+            for lane, spot in enumerate((12, 13, 14, 15, 7, 11)):
+                received = from_prev[:, lane * LANE : (lane + 1) * LANE].astype(F32)
+                yext[:EDGE, spot * LANE : (spot + 1) * LANE] = received
 
         @pl.when(here + 1 < rows)
         def _():
             up.wait_recv()
             down.wait_send()
-            beyond = slice(EDGE + count, 2 * EDGE + count)
-            yext[beyond, : 4 * LANE] = from_next[:, : 4 * LANE]
-            yext[beyond, 4 * LANE : 5 * LANE] = from_next[:, 4 * LANE : 5 * LANE]
-            yext[beyond, 8 * LANE : 9 * LANE] = from_next[:, 5 * LANE :]
+            for lane, spot in enumerate((0, 1, 2, 3, 4, 8)):
+                received = from_next[:, lane * LANE : (lane + 1) * LANE].astype(F32)
+                yext[EDGE + count : 2 * EDGE + count, spot * LANE : (spot + 1) * LANE] = received
 
         low, size = 8, padded + 2 * EDGE - 16
         go_left = mask_of(mask_ref, M_LEFT, low, size)
@@ -423,11 +437,13 @@
             zbuf[layer, q] = z
             total = total + jnp.sum(z, axis=0, keepdims=True)
             squares = squares + jnp.sum(z * z, axis=0, keepdims=True)
-        saves(layer)[1].start()
+        save(layer, 1).start()
         both = exchange_sums(
             rows, jnp.concatenate([total, squares, jnp.zeros((6, LANE), F32)], axis=0),
             sums.at[layer], sum_s.at[layer], sum_r.at[layer],
         )
+        if inside:
+            gather_forward(3, rows // 2)
         mean = both[0:1] / pixels
         inverse = lax.rsqrt(both[1:2] / pixels - mean * mean + EPSILON)
         stat_ref[layer] = jnp.concatenate([mean, inverse, jnp.zeros((6, LANE), F32)], axis=0)
@@ -435,22 +451,40 @@
         def activation(k, q):
             low, size = parts[k]
             y = gb_ref[layer, 0:1] * ((zbuf[layer, q, low : low + size] - mean) * inverse) + gb_ref[layer, 1:2]
-            keep = mask_of(mask_ref, M_VALID, EDGE + low, size)
-            return jnp.where(keep, y * jax.nn.sigmoid(y), 0.0).astype(BF16)
-
-        @pl.when(more)
-        def _():
+            return y * jax.nn.sigmoid(y)
+
+        def kept(k, which):
+            low, size = parts[k]
+            return mask_of(mask_ref, which, EDGE + low, size)
+
+        def pass_to_next(of_part):
             for k, (low, size) in enumerate(parts):
+                blocks = of_part(k)
                 for q in range(4):
-                    vbuf[layer + 1, q, low : low + size, own_lanes] = activation(k, q)
+                    vbuf[layer + 1, q, low : low + size, own_lanes] = blocks[q].astype(BF16)
                 to_far(layer + 1, k).start()
                 to_core(layer + 1, k).start()
 
+        def plain(k):
+            return [jnp.where(kept(k, M_VALID), activation(k, q), 0.0) for q in range(4)]
+
+        def unpooled(k):
+            pooled = smooth_max([activation(k, q) for q in range(4)])
+            return [jnp.where(kept(k, M_HIT + q), pooled, 0.0) for q in range(4)]
+
+        @pl.when(jnp.logical_and(more, layer != POOL))
+        def _():
+            pass_to_next(plain)
+
+        @pl.when(layer == POOL)
+        def _():
+            pass_to_next(unpooled)
+
         @pl.when(layer + 1 == layers)
         def _():
             for k, (low, size) in enumerate(parts):
-                for q in range(4):
-                    next_ref[q, low : low + size] = activation(k, q)
+                for q, block in enumerate(plain(k)):
+                    next_ref[q, low : low + size] = block.astype(BF16)
 
     each(layers, layer_step)
 
@@ -461,63 +495,49 @@
             pass_on(layer, k).wait_send()
         if inside:
             gather.drain(layer)
-        for copy in saves(layer):
-            copy.wait()
+        for which in range(3 if inside else 2):
+            save(layer, which).wait()
 
     each(layers, drain)
 
 
-def backward_kernel(
-    inside, pending, flush, layers, rows, count, padded, pixels, *refs
-):
+def backward_kernel(inside, layers, rows, count, padded, pixels, *refs):
     refs = list(refs)
     g_ref, stat_ref, gb_ref, mask_ref, z_in, full_in, w_in = refs[:7]
-    del refs[:7]
-    dk_in = refs.pop(0) if pending else None
-    grad_ref, gbgrad_ref = refs.pop(0), refs.pop(0)
-    wgrad_ref = refs.pop(0) if inside else None
-    dk_out = None if flush else refs.pop(0)
+    grad_ref, gbgrad_ref, wgrad_ref = refs[7:10]
     (
         zbuf, fbuf, wbuf, dk, gy, gext, above, below, patch, part, keep, core_out, core_in, x_out, x_in,
         to_next, to_prev, from_prev, from_next, sums,
         core_s, core_r, x_s, x_r, halo_s, halo_r, sum_s, sum_r, load_sem, out_sem,
-    ) = refs[:30]
+    ) = refs[10:40]
     mine, here = lax.axis_index("grp"), lax.axis_index("rows")
     half, core = mine // 2, lax.rem(mine, 2)
     partner, across = grp_peers()
     own_lanes, other_lanes = lanes_of(core), lanes_of(1 - core)
     own_base = pl.multiple_of(half * 2 * LANE, 2 * LANE)
     far_base = pl.multiple_of((1 - half) * 2 * LANE, 2 * LANE)
-    scatter = None
     if inside:
-        first, second, third, s1, r1, s2, r2 = refs[30:]
+        first, second, third, s1, r1, s2, r2 = refs[40:]
         scatter = Scatter(rows, dk.shape[1] // rows, dk, first, second, third, wgrad_ref, s1, r1, s2, r2)
 
-    def loads(layer):
-        pairs = [(z_in, zbuf), (w_in, wbuf), (full_in, fbuf)]
-        return [
-            pltpu.make_async_copy(src.at[layer], dst.at[layer], load_sem.at[layer, k])
-            for k, (src, dst) in enumerate(pairs)
-        ]
-
-    def dk_load():
-        return pltpu.make_async_copy(dk_in, dk.at[0], out_sem)
-
-    for layer in range(layers - 1, -1, -1):
-        for copy in loads(layer):
-            copy.start()
-    if pending:
-        dk_load().start()
+    def load(turn, which):
+        src, dst = ((z_in, zbuf), (w_in, wbuf), (full_in, fbuf))[which]
+        side = lax.rem(turn, 2)
+        return pltpu.make_async_copy(src.at[layers - 1 - turn], dst.at[side], load_sem.at[side, which])
+
+    def save(turn):
+        side = lax.rem(turn, 2)
+        return pltpu.make_async_copy(dk.at[side], wgrad_ref.at[layers - 1 - turn], out_sem.at[side])
+
+    for turn in range(2):
+        for which in range(3):
+            load(turn, which).start()
     after = (lax.rem(here + 1, rows), mine)
     before = (lax.rem(here + rows - 1, rows), mine)
-    down = remote(to_next, from_prev, halo_s.at[0], halo_r.at[0], after)
-    up = remote(to_prev, from_next, halo_s.at[1], halo_r.at[1], before)
     grad_ref[...] = g_ref[...]
     gext[:EDGE, :] = jnp.zeros((EDGE, 4 * LANE), F32)
     gext[EDGE + padded :, :] = jnp.zeros((EDGE, 4 * LANE), F32)
     greet([partner, across] + row_peers(rows))
-    if pending:
-        dk_load().wait()
 
     def taps(q, step):
         first = (q // 2 + step) * 4 + q % 2
@@ -527,59 +547,103 @@
         layer = layers - 1 - turn
         side = lax.rem(turn, 2)
         last = turn + 1 == layers
-        scattering = (turn >= 0) if pending else (turn > 0)
         mean, inverse = stat_ref[layer, 0:1], stat_ref[layer, 1:2]
         gain, shift = gb_ref[layer, 0:1], gb_ref[layer, 1:2]
         valid = mask_of(mask_ref, M_VALID, EDGE, padded)
-        loads(layer)[0].wait()
+        load(turn, 0).wait()
+        down = remote(to_next, from_prev.at[side], halo_s.at[0], halo_r.at[side, 0], after)
+        up = remote(to_prev, from_next.at[side], halo_s.at[1], halo_r.at[side, 1], before)
+
+        def shifted(q):
+            normed = (zbuf[side, q] - mean) * inverse
+            return normed, gain * normed + shift
+
+        @pl.when(layer == POOL)
+        def _():
+            pooled_grad = jnp.zeros((padded, LANE), F32)
+            for q in range(4):
+                pooled_grad = jnp.where(mask_of(mask_ref, M_HIT + q, EDGE, padded), grad_ref[q], pooled_grad)
+            blocks = []
+            for q in range(4):
+                _, y = shifted(q)
+                gy[q] = y * jax.nn.sigmoid(y)
+            pooled = smooth_max([gy[q] for q in range(4)])
+            for q in range(4):
+                grad_ref[q] = pooled_grad * (jnp.exp(gy[q] - pooled) * 0.25)
+
         shift_sum = jnp.zeros((1, LANE), F32)
         gain_sum = jnp.zeros((1, LANE), F32)
         for q in range(4):
-            normed = (zbuf[layer, q] - mean) * inverse
-            y = gain * normed + shift
+            normed, y = shifted(q)
             s = jax.nn.sigmoid(y)
             grad = jnp.where(valid, grad_ref[q] * s * (1.0 + y * (1.0 - s)), 0.0)
             gy[q] = grad
             shift_sum = shift_sum + jnp.sum(grad, axis=0, keepdims=True)
             gain_sum = gain_sum + jnp.sum(grad * normed, axis=0, keepdims=True)
+
+        def spread(buf, low, planes):
+            for lane, q in enumerate(planes):
+                piece = slice(low, low + EDGE)
+                normed = (zbuf[side, q, piece] - mean) * inverse
+                buf[:, 2 * lane * LANE : (2 * lane + 1) * LANE] = gy[q, piece].astype(BF16)
+                buf[:, (2 * lane + 1) * LANE : (2 * lane + 2) * LANE] = normed.astype(BF16)
+
+        spread(to_next, count - EDGE, (2, 3, 1))
+        spread(to_prev, 0, (0, 1, 2))
+
+        @pl.when(here + 1 < rows)
+        def _():
+            down.start()
+
+        @pl.when(here > 0)
+        def _():
+            up.start()
+
+        if inside:
+
+            @pl.when(turn > 1)
+            def _():
+                scatter.finish(turn - 2, layer + 2)
+                scatter.drain(turn - 2)
+
         both = exchange_sums(
             rows, jnp.concatenate([shift_sum, gain_sum, jnp.zeros((6, LANE), F32)], axis=0),
-            sums.at[turn], sum_s.at[turn], sum_r.at[turn],
+            sums.at[side], sum_s.at[side], sum_r.at[side],
         )
         gbgrad_ref[layer] = both
+        if inside:
+
+            @pl.when(turn > 0)
+            def _():
+                scatter.start(turn - 1)
+
+        def conv_grad(grad, normed):
+            out = inverse * gain * (grad - both[0:1] / pixels - normed * both[1:2] / pixels)
+            return out.astype(BF16).astype(F32)
+
         for q in range(4):
-            normed = (zbuf[layer, q] - mean) * inverse
-            gz = inverse * gain * (gy[q] - both[0:1] / pixels - normed * both[1:2] / pixels)
-            gz = jnp.where(valid, gz, 0.0).astype(BF16).astype(F32)
-            gext[EDGE : EDGE + padded, q * LANE : (q + 1) * LANE] = gz
-        to_next[...] = gext[count : count + EDGE, :].astype(BF16)
-        to_prev[...] = gext[EDGE : 2 * EDGE, :].astype(BF16)
-
-        @pl.when(here + 1 < rows)
-        def _():
-            down.start()
-
-        @pl.when(here > 0)
-        def _():
-            up.start()
-
-        if inside:
-
-            @pl.when(scattering)
-            def _():
-                scatter.start(turn)
+            normed, _ = shifted(q)
+            gext[EDGE : EDGE + padded, q * LANE : (q + 1) * LANE] = jnp.where(
+                valid, conv_grad(gy[q], normed), 0.0
+            )
+
+        def receive(buf, low, planes):
+            for lane, q in enumerate(planes):
+                grad = buf[side, :, 2 * lane * LANE : (2 * lane + 1) * LANE].astype(F32)
+                normed = buf[side, :, (2 * lane + 1) * LANE : (2 * lane + 2) * LANE].astype(F32)
+                gext[low : low + EDGE, q * LANE : (q + 1) * LANE] = conv_grad(grad, normed)
 
         @pl.when(here > 0)
         def _():
             down.wait_recv()
             up.wait_send()
-            gext[:EDGE, :] = from_prev[...].astype(F32)
+            receive(from_prev, 0, (2, 3, 1))
 
         @pl.when(here + 1 < rows)
         def _():
             up.wait_recv()
             down.wait_send()
-            gext[EDGE + count : 2 * EDGE + count, :] = from_next[...].astype(F32)
+            receive(from_next, EDGE + count, (0, 1, 2))
 
         low, size = EDGE - 8, padded + 16
         for kept, which, sign, lanes in (
@@ -606,30 +670,36 @@
                 spot = step * 4 + column
                 patch[:, spot * LANE : (spot + 1) * LANE] = block.astype(BF16)
 
-        def kernel_grad(step):
-            total = None
-            for q in range(4):
-                product = lax.dot_general(
-                    fbuf[layer, q], taps(q, step), (((0,), (0,)), ((), ())), preferred_element_type=F32
-                )
-                total = product if total is None else total + product
-            dk[turn + 1, :, step * 3 * LANE : (step + 1) * 3 * LANE] = total.astype(BF16)
-
-        loads(layer)[1].wait()
-        loads(layer)[2].wait()
-        if flush:
-
-            @pl.when(last)
+        def kernel_grad():
+            for step in range(3):
+                total = None
+                for q in range(4):
+                    product = lax.dot_general(
+                        fbuf[side, q], taps(q, step), (((0,), (0,)), ((), ())), preferred_element_type=F32
+                    )
+                    total = product if total is None else total + product
+                dk[side, :, step * 3 * LANE : (step + 1) * 3 * LANE] = total.astype(BF16)
+            if not inside:
+                save(turn).start()
+
+        load(turn, 1).wait()
+        load(turn, 2).wait()
+        if not inside:
+
+            @pl.when(turn > 1)
             def _():
-                for step in range(3):
-                    kernel_grad(step)
-                if inside:
-                    scatter.start(layers)
+                save(turn - 2).wait()
+
+        @pl.when(last)
+        def _():
+            kernel_grad()
+            if inside:
+                scatter.start(turn)
 
         def input_grad(q, base):
             total = None
             for step in range(3):
-                right = wbuf[layer, pl.ds(base, 2 * LANE), step * 3 * LANE : (step + 1) * 3 * LANE]
+                right = wbuf[side, pl.ds(base, 2 * LANE), step * 3 * LANE : (step + 1) * 3 * LANE]
                 product = lax.dot_general(
                     taps(q, step), right, (((1,), (1,)), ((), ())), preferred_element_type=F32
                 )
@@ -650,29 +720,29 @@
             x_out[side, q] = (keep[q] + core_in[side, q].astype(F32)).astype(BF16)
             to_far(q).start()
 
-        for which, base in enumerate((far_base, own_base)):
-            for q in range(4):
-                spot = which * 4 + q
-                input_grad(q, base)
-                core_out[side, spot] = part[:, other_lanes].astype(BF16)
-                keep[spot] = part[:, own_lanes]
-                to_core(spot).start()
-                if which == 0 and q > 0:
-                    send_across(q - 1)
-            if which == 0:
-                send_across(3)
-
-        @pl.when(jnp.logical_not(last) if flush else turn >= 0)
-        def _():
-            for step in range(3):
-                kernel_grad(step)
+        for spot in range(8):
+            input_grad(spot % 4, far_base if spot < 4 else own_base)
+            core_out[side, spot] = part[:, other_lanes].astype(BF16)
+            keep[spot] = part[:, own_lanes]
+            to_core(spot).start()
+            if 2 <= spot < 6:
+                send_across(spot - 2)
+
+        @pl.when(jnp.logical_not(last))
+        def _():
+            kernel_grad()
+
+        @pl.when(turn + 2 < layers)
+        def _():
+            for which in range(3):
+                load(turn + 2, which).start()
 
         if inside:
 
-            @pl.when(scattering)
+            @pl.when(turn > 0)
             def _():
                 for step in scatter.order():
-                    scatter.forward(turn, step)
+                    scatter.forward(turn - 1, step, layer + 1)
         for q in range(4):
             to_core(4 + q).wait_recv()
             to_far(q).wait_recv()
@@ -681,23 +751,17 @@
             to_core(spot).wait_send()
         for q in range(4):
             to_far(q).wait_send()
-        if inside:
-
-            @pl.when(scattering)
-            def _():
-                scatter.finish(turn)
-                scatter.drain(turn)
 
     each(layers, layer_step)
-    if inside and flush:
+    if inside:
         for step in scatter.order():
-            scatter.forward(layers, step)
-        scatter.finish(layers)
-        scatter.drain(layers)
-    if not flush:
-        copy = pltpu.make_async_copy(dk.at[layers] if inside else dk, dk_out, out_sem)
-        copy.start()
-        copy.wait()
+            scatter.forward(layers - 1, step, 0)
+        for turn in (layers - 2, layers - 1):
+            scatter.finish(turn, layers - 1 - turn)
+            scatter.drain(turn)
+    else:
+        for turn in (layers - 2, layers - 1):
+            save(turn).wait()
 
 
 VM = pl.BlockSpec(memory_space=pltpu.VMEM)
@@ -731,7 +795,7 @@
             pltpu.VMEM((ext, 2 * LANE), F32),
             pltpu.VMEM((ext, 2 * LANE), F32),
         ]
-        + [pltpu.VMEM((EDGE, 6 * LANE), F32)] * 4
+        + [pltpu.VMEM((EDGE, 6 * LANE), BF16)] * 4
         + [pltpu.VMEM((layers, rows, 8, LANE), F32)]
         + [DMA((layers, n_parts))] * 6
         + [DMA((2,))] * 2
@@ -746,29 +810,16 @@
     return out[:4] + ((out[4] if inside else weight),)
 
 
-def backward_block(
-    inside, flush, rows, count, padded, pixels, grad, z, stat, gain_shift, masks, full, weight, dk
-):
+def backward_block(inside, rows, count, padded, pixels, grad, z, stat, gain_shift, masks, full, weight):
     layers, channels, taps = weight.shape
     ext = padded + 2 * EDGE
-    pending = dk is not None
     shard = channels // rows
     far = rows // 2
-    outs = [
-        (jax.ShapeDtypeStruct((4, padded, LANE), F32), VM),
-        (jax.ShapeDtypeStruct((layers, 8, LANE), F32), VM),
-    ]
-    if inside:
-        outs.append((jax.ShapeDtypeStruct((layers + 1, shard, taps), F32), VM))
-    if not flush:
-        outs.append(
-            (jax.ShapeDtypeStruct((channels, taps) if inside else (layers + 1, channels, taps), BF16), HBM)
-        )
     scratch = [
-        pltpu.VMEM((layers, 4, padded, LANE), F32),
-        pltpu.VMEM((layers, 4, padded, channels), BF16),
-        pltpu.VMEM((layers, channels, taps), BF16),
-        pltpu.VMEM((layers + 1, channels, taps), BF16),
+        pltpu.VMEM((2, 4, padded, LANE), F32),
+        pltpu.VMEM((2, 4, padded, channels), BF16),
+        pltpu.VMEM((2, channels, taps), BF16),
+        pltpu.VMEM((2, channels, taps), BF16),
         pltpu.VMEM((4, padded, LANE), F32),
         pltpu.VMEM((ext, 4 * LANE), F32),
         pltpu.VMEM((padded + 16, 2 * LANE), F32),
@@ -781,29 +832,34 @@
         pltpu.VMEM((2, 4, padded, LANE), BF16),
         pltpu.VMEM((2, 4, padded, LANE), BF16),
     ]
-    scratch += [pltpu.VMEM((EDGE, 4 * LANE), BF16)] * 4
-    scratch += [pltpu.VMEM((layers, rows, 8, LANE), F32)]
-    scratch += [DMA((2, 8))] * 2 + [DMA((2, 4))] * 2 + [DMA((2,))] * 2 + [DMA((layers, rows - 1))] * 2
-    scratch += [DMA((layers, 3)), DMA]
+    scratch += [pltpu.VMEM((EDGE, 6 * LANE), BF16)] * 2 + [pltpu.VMEM((2, EDGE, 6 * LANE), BF16)] * 2
+    scratch += [pltpu.VMEM((2, rows, 8, LANE), F32)]
+    scratch += [DMA((2, 8))] * 2 + [DMA((2, 4))] * 2 + [DMA((2,)), DMA((2, 2))] + [DMA((2, rows - 1))] * 2
+    scratch += [DMA((2, 3)), DMA((2,))]
     if inside:
         scratch += [
-            pltpu.VMEM((layers + 1, far, shard, taps), BF16),
-            pltpu.VMEM((layers + 1, far - 1, shard, taps), BF16),
-            pltpu.VMEM((layers + 1, far - 1, shard, taps), BF16),
+            pltpu.VMEM((2, far, shard, taps), BF16),
+            pltpu.VMEM((2, far - 1, shard, taps), BF16),
+            pltpu.VMEM((2, far - 1, shard, taps), BF16),
         ]
-        scratch += [DMA((layers + 1, far))] * 2 + [DMA((layers + 1, far - 1))] * 2
-    args = [grad, stat, gain_shift, masks, z, full, weight] + ([dk] if pending else [])
+        scratch += [DMA((2, far))] * 2 + [DMA((2, far - 1))] * 2
     return pl.pallas_call(
-        functools.partial(backward_kernel, inside, pending, flush, layers, rows, count, padded, pixels),
+        functools.partial(backward_kernel, inside, layers, rows, count, padded, pixels),
         name="backward_block",
-        out_shape=tuple(o for o, _ in outs),
-        in_specs=[VM] * 4 + [HBM] * (len(args) - 4),
-        out_specs=tuple(s for _, s in outs),
+        out_shape=(
+            jax.ShapeDtypeStruct((4, padded, LANE), F32),
+            jax.ShapeDtypeStruct((layers, 8, LANE), F32),
+            jax.ShapeDtypeStruct((layers, shard, taps), F32)
+            if inside
+            else jax.ShapeDtypeStruct((layers, channels, taps), BF16),
+        ),
+        in_specs=[VM] * 4 + [HBM] * 3,
+        out_specs=(VM, VM, VM if inside else HBM),
         scratch_shapes=scratch,
         compiler_params=pltpu.CompilerParams(
-            collective_id=2 if flush else 1, has_side_effects=True, vmem_limit_bytes=LIMIT
+            collective_id=1, has_side_effects=True, vmem_limit_bytes=LIMIT
         ),
-    )(*args)
+    )(grad, stat, gain_shift, masks, z, full, weight)
 
 
 def shards(
@@ -817,62 +873,35 @@
     shard = enc_weight.shape[2]
     inside = shard % 16 == 0
     sizes = (rows, count, padded, pixels)
-    masks = window_masks(image_group, lax.axis_index("rows") * count, count, padded)
-
-    def flat_weight(weight):
-        flat = jnp.transpose(weight[:, ::-1], (0, 2, 1, 3)).reshape(weight.shape[0], shard, -1)
-        return flat if inside else lax.all_gather(flat, "rows", axis=1, tiled=True)
-
-    def pair(gain, shift):
-        return jnp.pad(jnp.stack([gain, shift], axis=1), ((0, 0), (0, 6), (0, 0)))
-
-    enc_pair, dec_pair = pair(enc_gain, enc_bias), pair(dec_gain, dec_bias)
-    hits = switches[None, :] == jnp.arange(4, dtype=jnp.int32)[:, None]
-    hits = jnp.pad(hits.astype(F32), ((0, 0), (0, padded - count)))[:, :, None]
-
-    _, enc_stat, enc_z, enc_full, enc_w = forward_block(
-        inside, *sizes, to_planes(features, count, padded), flat_weight(enc_weight), enc_pair, masks
+    masks = window_masks(image_group, switches, lax.axis_index("rows") * count, count, padded)
+
+    both = jnp.concatenate([enc_weight, dec_weight])
+    flat = jnp.transpose(both[:, ::-1], (0, 2, 1, 3)).reshape(both.shape[0], shard, -1)
+    if not inside:
+        flat = lax.all_gather(flat, "rows", axis=1, tiled=True)
+    pairs = jnp.stack([jnp.concatenate([enc_gain, dec_gain]), jnp.concatenate([enc_bias, dec_bias])], axis=1)
+    pairs = jnp.pad(pairs, ((0, 0), (0, 6), (0, 0)))
+
+    planes, stat, z, full, weight = forward_block(
+        inside, *sizes, to_planes(features, count, padded), flat, pairs, masks
     )
-    y = enc_pair[2, 0] * ((enc_z[2] - enc_stat[2, 0]) * enc_stat[2, 1]) + enc_pair[2, 1]
-    blocks = jax.nn.silu(y)
-    pooled = jnp.log(jnp.mean(jnp.exp(blocks), axis=0))
-    planes = (pooled[None] * hits).astype(BF16)
-    planes, dec_stat, dec_z, dec_full, dec_w = forward_block(
-        inside, *sizes, planes, flat_weight(dec_weight), dec_pair, masks
+    grad = to_planes(d_decoded, count, padded).astype(F32)
+    grad, pair_grads, weight_grads = backward_block(
+        inside, *sizes, grad, z, stat, pairs, masks, full, weight
     )
-    decoded = to_stream(planes, count)
-
-    grad = to_planes(d_decoded, count, padded).astype(F32)
-    dec_out = backward_block(
-        inside, False, *sizes, grad, dec_z, dec_stat, dec_pair, masks, dec_full, dec_w, None
-    )
-    grad_pooled = jnp.sum(dec_out[0] * hits, axis=0)
-    grad = grad_pooled[None] * jnp.exp(blocks - pooled[None]) * 0.25
-    enc_out = backward_block(
-        inside, inside, *sizes, grad, enc_z, enc_stat, enc_pair, masks, enc_full, enc_w,
-        dec_out[-1] if inside else None,
-    )
-    if inside:
-        dec_parts = jnp.stack([enc_out[2][0], dec_out[2][2], dec_out[2][1]])
-        enc_parts = jnp.stack([enc_out[2][3], enc_out[2][2], enc_out[2][1]])
-    else:
-        dec_parts, enc_parts = (
-            lax.psum_scatter(out[-1][:0:-1], "rows", scatter_dimension=1, tiled=True).astype(F32)
-            for out in (dec_out, enc_out)
-        )
-
-    def whole_taps(parts):
-        return jnp.transpose(parts.reshape(3, shard, 9, -1)[:, :, ::-1], (0, 2, 1, 3))
-
+    if not inside:
+        weight_grads = lax.psum_scatter(weight_grads, "rows", scatter_dimension=1, tiled=True).astype(F32)
+    layers = weight_grads.shape[0]
+    weight_grads = jnp.transpose(weight_grads.reshape(layers, shard, 9, -1)[:, :, ::-1], (0, 2, 1, 3))
     return (
-        decoded,
-        to_stream(enc_out[0].astype(BF16), count),
-        whole_taps(enc_parts),
-        whole_taps(dec_parts),
-        enc_out[1][:, 1],
-        enc_out[1][:, 0],
-        dec_out[1][:, 1],
-        dec_out[1][:, 0],
+        to_stream(planes, count),
+        to_stream(grad.astype(BF16), count),
+        weight_grads[:3],
+        weight_grads[3:],
+        pair_grads[:3, 1],
+        pair_grads[:3, 0],
+        pair_grads[3:, 1],
+        pair_grads[3:, 0],
     )
 
 

time: 481 us -> 395 us (0.82); the launches traced: 472 us -> 395 us
  Pallas kernels: 434 us -> 366 us
  other arithmetic: 12.3 us -> 6.07 us
    pallas_call x2 -> x1, Pallas kernels: 248 us -> 204 us  [backward_block(): pl.pallas_call(functools.partial(backward_kernel, inside, layers, rows, c...]
    pallas_call x2 -> x1, Pallas kernels: 186 us -> 162 us  [forward_block(): pl.pallas_call(functools.partial(forward_kernel, inside, layers, rows, co...]
where the time goes in v3:
time: 395 us
  Pallas kernels  366 us (93%)
  local copies, waits for them, and re-layouts  21.5 us (5%)
  other arithmetic  6.07 us (2%)
    pallas_call x1, Pallas kernels, backward_block(): pl.pallas_call(functools.partial(backward_kernel, inside, layers, rows, c...  204 us
    pallas_call x1, Pallas kernels, forward_block(): pl.pallas_call(functools.partial(forward_kernel, inside, layers, rows, co...  162 us

profile of v3, /device:TPU:9, one launch (start us, length us, event | category | flops | bytes accessed | tf_op | source)
XLA Modules:
  0.0 394.8 jit_solution(2875196848243116774)
XLA Ops:
  0.6 0.0 copy-start.1
  0.6 0.8 select_reduce_fusion.4
  1.5 0.2 reduce-window.7
  1.7 0.7 pad_maximum_fusion.1
  2.4 0.7 pad_maximum_fusion.2
  3.1 0.8 pad_compare_fusion
  3.9 0.1 select_reduce_fusion
  4.1 0.3 reshape_and_fusion
  4.4 0.1 stack.43
  4.5 0.6 select_maximum_fusion.gb_ref.refs_2_
  5.1 0.2 copy.56
  5.3 0.8 pad_convert_fusion.1.mask_ref.refs_3_
  6.1 0.0 copy-start.2
  6.1 0.0 copy-start.3
  6.1 1.4 reshape.259
  7.5 0.1 copy.75
  7.6 0.8 pad.21.v_ref
  8.4 0.0 copy-done.1
  8.4 0.3 reshape.263
  8.7 0.1 copy.74
  8.8 1.0 pad_convert_fusion.refs_0_
  9.8 0.0 copy-done.2
  9.8 0.0 copy-done.3
  9.8 0.1 pad_maximum_fusion
  9.9 1.0 copy_bitcast_fusion.w_ref
  10.9 162.1 %forward_block.1 = (bf16[4,496,128]{2,1,0:T(8,128)(2,1)}, f32[6,8,128]{2,1,0:T(8,128)}, f32[6,4,496,128]{3,2,1,0:T(8,128)}, bf16[6,4,496,512]{3,2,1,0:T(8,128)(2,1)}, bf16[6,512,1152]{2,1,0:T(8,128)(2,1)}) custom-call(bf16[4,496,128]{2,1,0:T(8,128)(2,1)} %pad.21.v_ref, bf16[6,64,1152]{2,1,0:T(8,128)(2,1)} %copy_bitcast_fusion.w_ref, ...), custom_call_target="tpu_custom_call" | custom-call | tf_op jit(solution)/shard_map/forward_block/pallas_call | solution.py:778
  173.0 1.1 slice_bitcast_fusion
  174.1 0.2 copy.57
  174.3 1.1 reshape.262
  175.3 204.3 %backward_block.1 = (f32[4,496,128]{2,1,0:T(8,128)}, f32[6,8,128]{2,1,0:T(8,128)}, f32[6,64,1152]{2,1,0:T(8,128)}) custom-call(f32[4,496,128]{2,1,0:T(8,128)} %pad_convert_fusion.refs_0_, f32[6,8,128]{2,1,0:T(8,128)} %get-tuple-element.17.refs_1_, f32[6,8,128]{2,1,0:T(8,128)} %select_maximum_fusion.gb_ref.refs_2_, ...), custom_call_target="tpu_custom_call" | custom-call | tf_op jit(solution)/shard_map/backward_block/pallas_call | solution.py:846
  379.7 0.0 copy-start
  379.7 1.4 fusion
  381.1 0.2 copy.59
  381.3 1.1 reshape.264
  382.4 0.8 fusion.2
  383.2 0.6 copy.76
  383.7 0.6 copy.77
  384.3 0.6 copy.78
  384.9 0.6 copy.79
  385.5 0.0 copy-done
  385.5 1.8 reshape.265
  387.3 4.7 %rev.7 = f32[6,64,9,128]{3,2,1,0:T(8,128)S(1)} reverse(f32[6,64,9,128]{3,2,1,0:T(8,128)} %reshape.265), dimensions={2} | reverse | bytes 3538944 | tf_op jit(solution)/shard_map/rev | solution.py:895
  392.1 0.4 fusion.1
  392.4 1.2 copy.61
  393.6 1.2 copy.60
  (15 shorter events, 0.1 us)
Async XLA Ops:
  0.6 7.8 %copy-start.1 = (bf16[1932,128]{1,0:T(8,128)(2,1)S(1)}, bf16[1932,128]{1,0:T(8,128)(2,1)}, u32[]{:S(2)}) copy-start(bf16[1932,128]{1,0:T(8,128)(2,1)} %param.21) | copy-start | bytes 1483780
  6.1 3.7 copy-start.2
  6.1 3.7 copy-start.3
  379.7 5.8 %copy-start = (f32[6,64,1152]{2,1,0:T(8,128)S(1)}, f32[6,64,1152]{2,1,0:T(8,128)}, u32[]{:S(2)}) copy-start(f32[6,64,1152]{2,1,0:T(8,128)} %get-tuple-element.22) | copy-start | bytes 5308420

commit v4 on v3

--- a/solution.py
+++ b/solution.py
@@ -23,24 +23,31 @@
     return -(-value // step) * step
 
 
-def window_masks(image_group, switches, first_window, count, padded):
-    chosen = (image_group[:, None] == jnp.arange(3, dtype=jnp.int32)[None, :]).astype(jnp.int32)
-    heights = jnp.sum(chosen * jnp.array([h for h, _ in SIZES], jnp.int32)[None, :], axis=1)
-    widths = jnp.sum(chosen * jnp.array(WIDTHS, jnp.int32)[None, :], axis=1)
-    areas = heights * widths
-    ends = jnp.cumsum(areas)
-    starts = ends - areas
-    local = jnp.arange(padded + 2 * EDGE, dtype=jnp.int32) - EDGE
+def fill_masks(group_ref, first_window, count, padded, switch_ref, mask_ref):
+    shape = (padded + 2 * EDGE, 1)
+    local = lax.broadcasted_iota(jnp.int32, shape, 0) - EDGE
     windows = local + first_window
-    member = ((windows[:, None] >= starts[None, :]) & (windows[:, None] < ends[None, :])).astype(jnp.int32)
-    base = jnp.sum(member * starts[None, :], axis=1)
-    height = jnp.sum(member * heights[None, :], axis=1)
-    width = jnp.sum(member * widths[None, :], axis=1)
+
+    start = jnp.int32(0)
+    base = height = width = jnp.zeros(shape, jnp.int32)
+    for image in range(group_ref.shape[0]):
+        group = group_ref[image]
+        tall, wide = (
+            jnp.where(group == 0, SIZES[0][k], jnp.where(group == 1, SIZES[1][k], SIZES[2][k])) for k in range(2)
+        )
+        end = start + tall * wide
+        member = (windows >= start) & (windows < end)
+        base, height, width = (
+            jnp.where(member, new, old) for new, old in ((start, base), (tall, height), (wide, width))
+        )
+        start = end
     inside = width > 0
     position = windows - base
-    safe = jnp.maximum(width, 1)
-    row = position // safe
-    column = position - row * safe
+    row = jnp.zeros(shape, jnp.int32)
+    for tall, wide in SIZES:
+        quotient = jnp.floor((position.astype(F32) + 0.5) * (1.0 / wide)).astype(jnp.int32)
+        row = jnp.where(width == wide, quotient, row)
+    column = position - row * width
     masks = [
         width == WIDTHS[0],
         width == WIDTHS[1],
@@ -50,19 +57,24 @@
         inside & (column < width - 1),
         (local >= 0) & (local < count),
     ]
-    kept = jnp.pad(switches, (EDGE, padded - count + EDGE), constant_values=-1)
-    masks += [kept == q for q in range(4)]
-    table = jnp.stack([m.astype(F32) for m in masks], axis=1)
-    return jnp.pad(table, ((0, 0), (0, LANE - len(masks))))
-
-
-def to_planes(stream, count, padded):
-    planes = jnp.transpose(stream.reshape(count, 4, stream.shape[1]), (1, 0, 2))
-    return jnp.pad(planes, ((0, 0), (0, padded - count), (0, 0)))
-
-
-def to_stream(planes, count):
-    return jnp.transpose(planes[:, :count], (1, 0, 2)).reshape(4 * count, planes.shape[2])
+    lane = lax.broadcasted_iota(jnp.int32, (shape[0], LANE), 1)
+    table = (lane - M_HIT == switch_ref[...]).astype(F32)
+    for k, mask in enumerate(masks):
+        table = jnp.where((lane == k) & mask, 1.0, table)
+    mask_ref[...] = table
+
+
+def split_planes(stream_ref, wide_ref, count):
+    wide_ref[: 4 * count] = stream_ref[...].astype(F32)
+    wide_ref[4 * count :] = jnp.zeros((wide_ref.shape[0] - 4 * count, LANE), F32)
+
+
+def plane(wide_ref, q):
+    return wide_ref[pl.ds(q, wide_ref.shape[0] // 4, stride=4), :]
+
+
+def set_plane(wide_ref, q, low, block):
+    wide_ref[pl.ds(4 * low + q, block.shape[0], stride=4), :] = block
 
 
 def mask_of(mask_ref, which, low, count):
@@ -109,14 +121,20 @@
     )
 
 
-def exchange_sums(rows, own, buf, send, recv):
+def sums_copies(rows, buf, send, recv):
+    return [
+        remote(buf.at[0], buf.at[k + 1], send.at[k], recv.at[k], peer) for k, peer in enumerate(row_peers(rows))
+    ]
+
+
+def send_sums(rows, own, buf, send, recv):
     buf[0] = own
-    copies = []
-    for k, peer in enumerate(row_peers(rows)):
-        copy = remote(buf.at[0], buf.at[k + 1], send.at[k], recv.at[k], peer)
+    for copy in sums_copies(rows, buf, send, recv):
         copy.start()
-        copies.append(copy)
-    for copy in copies:
+
+
+def add_sums(rows, buf, send, recv):
+    for copy in sums_copies(rows, buf, send, recv):
         copy.wait()
     total = buf[0]
     for k in range(1, rows):
@@ -152,42 +170,46 @@
         block = lax.rem(self.high + step, self.far) * 2 + low
         return pl.ds(pl.multiple_of(block * self.shard, 16), self.shard)
 
-    def spread(self, layer, step):
-        own = self.buf.at[layer, self.rows_of(0, self.low), :]
+    def block(self, layer, step, piece):
+        lanes = slice(None) if piece is None else slice(piece * 3 * LANE, (piece + 1) * 3 * LANE)
+        slot = layer if piece is None else piece
+        return self.buf.at[layer, self.rows_of(step, self.low), lanes], slot
+
+    def spread(self, layer, step, piece=None):
+        own, slot = self.block(layer, 0, piece)
         peer = (lax.rem(self.high + step, self.far) * 2 + self.low, self.there)
         k = step - 1
-        return remote(own, own, self.send.at[layer, k], self.recv.at[layer, k], peer)
-
-    def across(self, layer, step):
-        piece = self.buf.at[layer, self.rows_of(self.far - step, self.low), :]
+        return remote(own, own, self.send.at[slot, k], self.recv.at[slot, k], peer)
+
+    def across(self, layer, step, piece=None):
+        part, slot = self.block(layer, self.far - step, piece)
         peer = (self.high * 2 + 1 - self.low, self.there)
-        return remote(piece, piece, self.pass_send.at[layer, step], self.pass_recv.at[layer, step], peer)
-
-    def start(self, layer, own):
-        self.buf[layer, self.rows_of(0, self.low), :] = own
+        return remote(part, part, self.pass_send.at[slot, step], self.pass_recv.at[slot, step], peer)
+
+    def start(self, layer, piece=None):
         for step in range(1, self.far):
-            self.spread(layer, step).start()
-        self.across(layer, 0).start()
-
-    def forward(self, layer, step):
-        self.spread(layer, step).wait_recv()
-        self.across(layer, step).start()
-
-    def wait(self, layer):
+            self.spread(layer, step, piece).start()
+        self.across(layer, 0, piece).start()
+
+    def forward(self, layer, step, piece=None):
+        self.spread(layer, step, piece).wait_recv()
+        self.across(layer, step, piece).start()
+
+    def wait(self, layer, piece=None):
         for step in range(self.far):
-            self.across(layer, step).wait_recv()
-
-    def drain(self, layer):
+            self.across(layer, step, piece).wait_recv()
+
+    def drain(self, layer, piece=None):
         for step in range(1, self.far):
-            self.spread(layer, step).wait_send()
+            self.spread(layer, step, piece).wait_send()
         for step in range(self.far):
-            self.across(layer, step).wait_send()
+            self.across(layer, step, piece).wait_send()
 
 
 class Scatter:
-    def __init__(self, rows, shard, grads, first, second, third, out, send, recv, far_send, far_recv):
+    def __init__(self, rows, shard, grads, first, second, third, total, outs, send, recv, far_send, far_recv):
         self.shard, self.grads, self.first, self.second, self.third = shard, grads, first, second, third
-        self.out, self.far = out, rows // 2
+        self.total, self.outs, self.far = total, outs, rows // 2
         here, self.there = lax.axis_index("rows"), lax.axis_index("grp")
         self.high, self.low = here // 2, lax.rem(here, 2)
         self.send, self.recv, self.far_send, self.far_recv = send, recv, far_send, far_recv
@@ -197,7 +219,7 @@
         return pl.ds(pl.multiple_of(block * self.shard, 16), self.shard)
 
     def across(self, turn, step):
-        slot = lax.rem(turn, 2)
+        slot = lax.rem(turn, 3)
         peer = (self.high * 2 + 1 - self.low, self.there)
         return remote(
             self.grads.at[slot, self.rows_of(step, 1 - self.low), :], self.first.at[slot, step],
@@ -205,7 +227,7 @@
         )
 
     def spread(self, turn, step):
-        slot = lax.rem(turn, 2)
+        slot = lax.rem(turn, 3)
         peer = (lax.rem(self.high + step, self.far) * 2 + self.low, self.there)
         k = step - 1
         return remote(
@@ -220,24 +242,36 @@
         for step in self.order():
             self.across(turn, step).start()
 
-    def forward(self, turn, step, layer):
-        slot = lax.rem(turn, 2)
+    def forward(self, turn, step):
+        slot = lax.rem(turn, 3)
         self.across(turn, step).wait_recv()
         own = self.grads[slot, self.rows_of(step, self.low), :]
         total = own.astype(F32) + self.first[slot, step].astype(F32)
         if step == 0:
-            self.out[layer] = total
+            self.total[slot] = total
         else:
             self.second[slot, step - 1] = total.astype(BF16)
             self.spread(turn, step).start()
 
     def finish(self, turn, layer):
-        slot = lax.rem(turn, 2)
-        total = self.out[layer]
+        slot = lax.rem(turn, 3)
+        total = self.total[slot]
         for step in range(1, self.far):
             self.spread(turn, step).wait_recv()
             total = total + self.third[slot, step - 1].astype(F32)
-        self.out[layer] = total
+        depth = self.outs[0].shape[0]
+
+        def put(out, index):
+            for block in range(9):
+                out[index, 8 - block] = total[:, block * LANE : (block + 1) * LANE]
+
+        @pl.when(layer < depth)
+        def _():
+            put(self.outs[0], layer)
+
+        @pl.when(layer >= depth)
+        def _():
+            put(self.outs[1], layer - depth)
 
     def drain(self, turn):
         for step in range(self.far):
@@ -251,13 +285,15 @@
 
 
 def forward_kernel(
-    inside, layers, rows, count, padded, pixels,
-    v_ref, w_ref, gb_ref, mask_ref,
-    next_ref, stat_ref, z_out, full_out, w_out,
-    vbuf, wbuf, zbuf, yext, over, under, to_next, to_prev, from_prev, from_next, sums,
-    core_s, core_r, x_s, x_r, fwd_s, fwd_r, halo_s, halo_r, sum_s, sum_r, out_sem,
-    w_s, w_r, wp_s, wp_r,
+    inside, layers, rows, count, padded, pixels, group_ref, switch_ref, v_ref, gb_ref, *refs
 ):
+    w_refs, refs = refs[: 1 + inside], refs[1 + inside :]
+    (
+        next_ref, stat_ref, mask_ref, z_out, full_out, w_out,
+        vbuf, wbuf, zbuf, yext, over, under, wide, to_next, to_prev, from_prev, from_next, sums,
+        core_s, core_r, x_s, x_r, fwd_s, fwd_r, halo_s, halo_r, sum_s, sum_r, out_sem,
+        w_s, w_r, wp_s, wp_r, first_s, first_r, first_ps, first_pr,
+    ) = refs
     mine, here = lax.axis_index("grp"), lax.axis_index("rows")
     half = mine // 2
     partner, across = grp_peers()
@@ -265,7 +301,9 @@
     own_lanes, far_lanes = lanes_of(mine), lanes_of(across[1])
     own_base = pl.multiple_of(half * 2 * LANE, 2 * LANE)
     far_base = pl.multiple_of((1 - half) * 2 * LANE, 2 * LANE)
-    gather = Gather(rows, w_ref.shape[1], wbuf, w_s, w_r, wp_s, wp_r)
+    shard = wbuf.shape[1] // rows
+    gather = Gather(rows, shard, wbuf, w_s, w_r, wp_s, wp_r)
+    first_gather = Gather(rows, shard, wbuf, first_s, first_r, first_ps, first_pr)
 
     def slab(layer, k, lanes):
         low, size = parts[k]
@@ -284,7 +322,7 @@
         return remote(piece, piece, fwd_s.at[layer, k], fwd_r.at[layer, k], partner)
 
     def load(layer):
-        return pltpu.make_async_copy(w_ref.at[layer], wbuf.at[layer], w_s.at[layer, 0])
+        return pltpu.make_async_copy(w_refs[0].at[layer], wbuf.at[layer], w_s.at[layer, 0])
 
     def save(layer, which):
         pairs = [(vbuf, full_out), (zbuf, z_out), (wbuf, w_out)]
@@ -317,29 +355,46 @@
         return yext[low : low + size, spot * LANE : (spot + 1) * LANE]
 
     greet([partner, across] + row_peers(rows))
-    vbuf[0, :, :, own_lanes] = v_ref[...]
+    if inside:
+        own_rows = gather.rows_of(0, gather.low)
+        for layer in range(layers):
+            source = w_refs[layer // (layers // 2)]
+            for block in range(9):
+                lanes = slice(block * LANE, (block + 1) * LANE)
+                wbuf[layer, own_rows, lanes] = source[layer % (layers // 2), 8 - block]
+            if layer == 0:
+                for piece in range(3):
+                    first_gather.start(0, piece)
+    else:
+        load(0).start()
+    split_planes(v_ref, wide, count)
+    for q in range(4):
+        vbuf[0, q, :, own_lanes] = plane(wide, q).astype(BF16)
     for k in range(len(parts)):
         to_far(0, k).start()
         to_core(0, k).start()
-    if inside:
-        gather.start(0, w_ref[0])
-    else:
-        load(0).start()
     yext[:EDGE, :] = jnp.zeros((EDGE, yext.shape[1]), F32)
     yext[EDGE + padded :, :] = jnp.zeros((EDGE, yext.shape[1]), F32)
+    fill_masks(group_ref, here * count, count, padded, switch_ref, mask_ref)
     if inside:
-        for step in range(1, rows // 2):
-            gather.forward(0, step)
+        for piece in range(3):
+            for step in range(1, rows // 2):
+                first_gather.forward(0, step, piece)
+        for piece in range(3):
+            first_gather.wait(0, piece)
 
     def layer_step(layer):
         more = layer + 1 < layers
         if inside:
-            gather.wait(layer)
+            @pl.when(layer > 0)
+            def _():
+                gather.wait(layer)
+
             save(layer, 2).start()
 
             @pl.when(more)
             def _():
-                gather.start(layer + 1, w_ref[layer + 1])
+                gather.start(layer + 1)
         else:
             load(layer).wait()
 
@@ -386,7 +441,7 @@
         far_products(len(parts) - 1)
         save(layer, 0).start()
         if inside:
-            gather_forward(2, 3)
+            gather_forward(2, rows // 2)
 
         @pl.when(here > 0)
         def _():
@@ -438,12 +493,10 @@
             total = total + jnp.sum(z, axis=0, keepdims=True)
             squares = squares + jnp.sum(z * z, axis=0, keepdims=True)
         save(layer, 1).start()
-        both = exchange_sums(
-            rows, jnp.concatenate([total, squares, jnp.zeros((6, LANE), F32)], axis=0),
-            sums.at[layer], sum_s.at[layer], sum_r.at[layer],
-        )
-        if inside:
-            gather_forward(3, rows // 2)
+        own = jnp.concatenate([total, squares, jnp.zeros((6, LANE), F32)], axis=0)
+        channel = (sums.at[layer], sum_s.at[layer], sum_r.at[layer])
+        send_sums(rows, own, *channel)
+        both = add_sums(rows, *channel)
         mean = both[0:1] / pixels
         inverse = lax.rsqrt(both[1:2] / pixels - mean * mean + EPSILON)
         stat_ref[layer] = jnp.concatenate([mean, inverse, jnp.zeros((6, LANE), F32)], axis=0)
@@ -484,7 +537,8 @@
         def _():
             for k, (low, size) in enumerate(parts):
                 for q, block in enumerate(plain(k)):
-                    next_ref[q, low : low + size] = block.astype(BF16)
+                    set_plane(wide, q, low, block)
+            next_ref[...] = wide[: 4 * count].astype(BF16)
 
     each(layers, layer_step)
 
@@ -494,22 +548,32 @@
             to_core(layer, k).wait_send()
             pass_on(layer, k).wait_send()
         if inside:
-            gather.drain(layer)
+
+            @pl.when(layer > 0)
+            def _():
+                gather.drain(layer)
+
         for which in range(3 if inside else 2):
             save(layer, which).wait()
 
     each(layers, drain)
+    if inside:
+        for piece in range(3):
+            first_gather.drain(0, piece)
 
 
 def backward_kernel(inside, layers, rows, count, padded, pixels, *refs):
     refs = list(refs)
     g_ref, stat_ref, gb_ref, mask_ref, z_in, full_in, w_in = refs[:7]
-    grad_ref, gbgrad_ref, wgrad_ref = refs[7:10]
+    del refs[:7]
+    out_ref, gbgrad_ref = refs[:2]
+    wgrad_refs = refs[2 : 3 + inside]
+    del refs[: 3 + inside]
     (
-        zbuf, fbuf, wbuf, dk, gy, gext, above, below, patch, part, keep, core_out, core_in, x_out, x_in,
+        grad_ref, wide, zbuf, fbuf, wbuf, dk, gy, gext, above, below, patch, part, keep, core_out, core_in, x_out, x_in,
         to_next, to_prev, from_prev, from_next, sums,
         core_s, core_r, x_s, x_r, halo_s, halo_r, sum_s, sum_r, load_sem, out_sem,
-    ) = refs[10:40]
+    ) = refs[:32]
     mine, here = lax.axis_index("grp"), lax.axis_index("rows")
     half, core = mine // 2, lax.rem(mine, 2)
     partner, across = grp_peers()
@@ -517,8 +581,9 @@
     own_base = pl.multiple_of(half * 2 * LANE, 2 * LANE)
     far_base = pl.multiple_of((1 - half) * 2 * LANE, 2 * LANE)
     if inside:
-        first, second, third, s1, r1, s2, r2 = refs[40:]
-        scatter = Scatter(rows, dk.shape[1] // rows, dk, first, second, third, wgrad_ref, s1, r1, s2, r2)
+        first, second, third, total_ref, s1, r1, s2, r2 = refs[32:]
+        shard = dk.shape[1] // rows
+        scatter = Scatter(rows, shard, dk, first, second, third, total_ref, wgrad_refs, s1, r1, s2, r2)
 
     def load(turn, which):
         src, dst = ((z_in, zbuf), (w_in, wbuf), (full_in, fbuf))[which]
@@ -526,15 +591,17 @@
         return pltpu.make_async_copy(src.at[layers - 1 - turn], dst.at[side], load_sem.at[side, which])
 
     def save(turn):
-        side = lax.rem(turn, 2)
-        return pltpu.make_async_copy(dk.at[side], wgrad_ref.at[layers - 1 - turn], out_sem.at[side])
+        slot = lax.rem(turn, 3)
+        return pltpu.make_async_copy(dk.at[slot], wgrad_refs[0].at[layers - 1 - turn], out_sem.at[slot])
 
     for turn in range(2):
         for which in range(3):
             load(turn, which).start()
     after = (lax.rem(here + 1, rows), mine)
     before = (lax.rem(here + rows - 1, rows), mine)
-    grad_ref[...] = g_ref[...]
+    split_planes(g_ref, wide, count)
+    for q in range(4):
+        grad_ref[q] = plane(wide, q)
     gext[:EDGE, :] = jnp.zeros((EDGE, 4 * LANE), F32)
     gext[EDGE + padded :, :] = jnp.zeros((EDGE, 4 * LANE), F32)
     greet([partner, across] + row_peers(rows))
@@ -545,7 +612,7 @@
 
     def layer_step(turn):
         layer = layers - 1 - turn
-        side = lax.rem(turn, 2)
+        side, slot = lax.rem(turn, 2), lax.rem(turn, 3)
         last = turn + 1 == layers
         mean, inverse = stat_ref[layer, 0:1], stat_ref[layer, 1:2]
         gain, shift = gb_ref[layer, 0:1], gb_ref[layer, 1:2]
@@ -599,23 +666,17 @@
         def _():
             up.start()
 
+        own = jnp.concatenate([shift_sum, gain_sum, jnp.zeros((6, LANE), F32)], axis=0)
+        channel = (sums.at[side], sum_s.at[side], sum_r.at[side])
+        send_sums(rows, own, *channel)
         if inside:
 
-            @pl.when(turn > 1)
-            def _():
-                scatter.finish(turn - 2, layer + 2)
-                scatter.drain(turn - 2)
-
-        both = exchange_sums(
-            rows, jnp.concatenate([shift_sum, gain_sum, jnp.zeros((6, LANE), F32)], axis=0),
-            sums.at[side], sum_s.at[side], sum_r.at[side],
-        )
+            @pl.when(turn > 0)
+            def _():
+                scatter.start(turn - 1)
+
+        both = add_sums(rows, *channel)
         gbgrad_ref[layer] = both
-        if inside:
-
-            @pl.when(turn > 0)
-            def _():
-                scatter.start(turn - 1)
 
         def conv_grad(grad, normed):
             out = inverse * gain * (grad - both[0:1] / pixels - normed * both[1:2] / pixels)
@@ -678,17 +739,30 @@
                         fbuf[side, q], taps(q, step), (((0,), (0,)), ((), ())), preferred_element_type=F32
                     )
                     total = product if total is None else total + product
-                dk[side, :, step * 3 * LANE : (step + 1) * 3 * LANE] = total.astype(BF16)
+                dk[slot, :, step * 3 * LANE : (step + 1) * 3 * LANE] = total.astype(BF16)
             if not inside:
                 save(turn).start()
 
+        def scatter_forward(step):
+            @pl.when(turn > 0)
+            def _():
+                scatter.forward(turn - 1, step)
+
+        if inside:
+
+            @pl.when(turn > 1)
+            def _():
+                scatter.finish(turn - 2, layer + 2)
+                scatter.drain(turn - 2)
+
+            scatter_forward(1)
         load(turn, 1).wait()
         load(turn, 2).wait()
         if not inside:
 
-            @pl.when(turn > 1)
-            def _():
-                save(turn - 2).wait()
+            @pl.when(turn > 2)
+            def _():
+                save(turn - 3).wait()
 
         @pl.when(last)
         def _():
@@ -727,6 +801,8 @@
             to_core(spot).start()
             if 2 <= spot < 6:
                 send_across(spot - 2)
+            if inside and spot == 5:
+                scatter_forward(2)
 
         @pl.when(jnp.logical_not(last))
         def _():
@@ -738,11 +814,9 @@
                 load(turn + 2, which).start()
 
         if inside:
-
-            @pl.when(turn > 0)
-            def _():
-                for step in scatter.order():
-                    scatter.forward(turn - 1, step, layer + 1)
+            for step in range(3, rows // 2):
+                scatter_forward(step)
+            scatter_forward(0)
         for q in range(4):
             to_core(4 + q).wait_recv()
             to_far(q).wait_recv()
@@ -753,14 +827,17 @@
             to_far(q).wait_send()
 
     each(layers, layer_step)
+    for q in range(4):
+        set_plane(wide, q, 0, grad_ref[q])
+    out_ref[...] = wide[: 4 * count].astype(BF16)
     if inside:
         for step in scatter.order():
-            scatter.forward(layers - 1, step, 0)
+            scatter.forward(layers - 1, step)
         for turn in (layers - 2, layers - 1):
             scatter.finish(turn, layers - 1 - turn)
             scatter.drain(turn)
     else:
-        for turn in (layers - 2, layers - 1):
+        for turn in range(layers - 3, layers):
             save(turn).wait()
 
 
@@ -770,23 +847,25 @@
 DMA = pltpu.SemaphoreType.DMA
 
 
-def forward_block(inside, rows, count, padded, pixels, planes, weight, gain_shift, masks):
-    layers, channels, taps = weight.shape[0], 4 * LANE, weight.shape[2]
+def forward_block(inside, rows, count, padded, pixels, image_group, switches, features, pairs, weights):
+    layers, channels, taps = pairs.shape[0], 4 * LANE, 9 * LANE
     ext = padded + 2 * EDGE
     n_parts = len(row_parts(padded, count))
     far = rows // 2
+    shape = jax.ShapeDtypeStruct
     out = pl.pallas_call(
         functools.partial(forward_kernel, inside, layers, rows, count, padded, pixels),
         name="forward_block",
         out_shape=(
-            jax.ShapeDtypeStruct((4, padded, LANE), BF16),
-            jax.ShapeDtypeStruct((layers, 8, LANE), F32),
-            jax.ShapeDtypeStruct((layers, 4, padded, LANE), F32),
-            jax.ShapeDtypeStruct((layers, 4, padded, channels), BF16),
-            jax.ShapeDtypeStruct((layers, channels, taps) if inside else (1, 16, LANE), BF16),
+            shape((4 * count, LANE), BF16),
+            shape((layers, 8, LANE), F32),
+            shape((ext, LANE), F32),
+            shape((layers, 4, padded, LANE), F32),
+            shape((layers, 4, padded, channels), BF16),
+            shape((layers, channels, taps) if inside else (1, 16, LANE), BF16),
         ),
-        in_specs=[VM, VM if inside else HBM, VM, VM],
-        out_specs=(VM, VM, HBM, HBM, HBM),
+        in_specs=[pl.BlockSpec(memory_space=pltpu.SMEM), VM, VM, VM] + [VM if inside else HBM] * len(weights),
+        out_specs=(VM, VM, VM, HBM, HBM, HBM),
         scratch_shapes=[
             pltpu.VMEM((layers, 4, padded, channels), BF16),
             pltpu.VMEM((layers, channels, taps), BF16),
@@ -794,6 +873,7 @@
             pltpu.VMEM((ext, 16 * LANE), F32),
             pltpu.VMEM((ext, 2 * LANE), F32),
             pltpu.VMEM((ext, 2 * LANE), F32),
+            pltpu.VMEM((4 * padded, LANE), F32),
         ]
         + [pltpu.VMEM((EDGE, 6 * LANE), BF16)] * 4
         + [pltpu.VMEM((layers, rows, 8, LANE), F32)]
@@ -802,24 +882,29 @@
         + [DMA((layers, rows - 1))] * 2
         + [DMA((layers, 3))]
         + [DMA((layers, far - 1))] * 2
-        + [DMA((layers, far))] * 2,
+        + [DMA((layers, far))] * 2
+        + [DMA((3, far - 1))] * 2
+        + [DMA((3, far))] * 2,
         compiler_params=pltpu.CompilerParams(
             collective_id=0, has_side_effects=True, vmem_limit_bytes=LIMIT
         ),
-    )(planes, weight, gain_shift, masks)
-    return out[:4] + ((out[4] if inside else weight),)
-
-
-def backward_block(inside, rows, count, padded, pixels, grad, z, stat, gain_shift, masks, full, weight):
+    )(image_group, switches, features, pairs, *weights)
+    return out[:5] + ((out[5] if inside else weights[0]),)
+
+
+def backward_block(inside, rows, count, padded, pixels, grad, z, stat, pairs, masks, full, weight):
     layers, channels, taps = weight.shape
     ext = padded + 2 * EDGE
     shard = channels // rows
     far = rows // 2
+    shape = jax.ShapeDtypeStruct
     scratch = [
+        pltpu.VMEM((4, padded, LANE), F32),
+        pltpu.VMEM((4 * padded, LANE), F32),
         pltpu.VMEM((2, 4, padded, LANE), F32),
         pltpu.VMEM((2, 4, padded, channels), BF16),
         pltpu.VMEM((2, channels, taps), BF16),
-        pltpu.VMEM((2, channels, taps), BF16),
+        pltpu.VMEM((3, channels, taps), BF16),
         pltpu.VMEM((4, padded, LANE), F32),
         pltpu.VMEM((ext, 4 * LANE), F32),
         pltpu.VMEM((padded + 16, 2 * LANE), F32),
@@ -835,31 +920,28 @@
     scratch += [pltpu.VMEM((EDGE, 6 * LANE), BF16)] * 2 + [pltpu.VMEM((2, EDGE, 6 * LANE), BF16)] * 2
     scratch += [pltpu.VMEM((2, rows, 8, LANE), F32)]
     scratch += [DMA((2, 8))] * 2 + [DMA((2, 4))] * 2 + [DMA((2,)), DMA((2, 2))] + [DMA((2, rows - 1))] * 2
-    scratch += [DMA((2, 3)), DMA((2,))]
+    scratch += [DMA((2, 3)), DMA((3,))]
+    wgrads = [shape((layers, channels, taps), BF16)]
     if inside:
+        wgrads = [shape((layers // 2, 9, shard, LANE), F32)] * 2
         scratch += [
-            pltpu.VMEM((2, far, shard, taps), BF16),
-            pltpu.VMEM((2, far - 1, shard, taps), BF16),
-            pltpu.VMEM((2, far - 1, shard, taps), BF16),
+            pltpu.VMEM((3, far, shard, taps), BF16),
+            pltpu.VMEM((3, far - 1, shard, taps), BF16),
+            pltpu.VMEM((3, far - 1, shard, taps), BF16),
+            pltpu.VMEM((3, shard, taps), F32),
         ]
-        scratch += [DMA((2, far))] * 2 + [DMA((2, far - 1))] * 2
+        scratch += [DMA((3, far))] * 2 + [DMA((3, far - 1))] * 2
     return pl.pallas_call(
         functools.partial(backward_kernel, inside, layers, rows, count, padded, pixels),
         name="backward_block",
-        out_shape=(
-            jax.ShapeDtypeStruct((4, padded, LANE), F32),
-            jax.ShapeDtypeStruct((layers, 8, LANE), F32),
-            jax.ShapeDtypeStruct((layers, shard, taps), F32)
-            if inside
-            else jax.ShapeDtypeStruct((layers, channels, taps), BF16),
-        ),
+        out_shape=[shape((4 * count, LANE), BF16), shape((layers, 8, LANE), F32)] + wgrads,
         in_specs=[VM] * 4 + [HBM] * 3,
-        out_specs=(VM, VM, VM if inside else HBM),
+        out_specs=[VM, VM] + [VM if inside else HBM] * len(wgrads),
         scratch_shapes=scratch,
         compiler_params=pltpu.CompilerParams(
             collective_id=1, has_side_effects=True, vmem_limit_bytes=LIMIT
         ),
-    )(grad, stat, gain_shift, masks, z, full, weight)
+    )(grad, stat, pairs, masks, z, full, weight)
 
 
 def shards(
@@ -870,38 +952,36 @@
     count = features.shape[0] // 4
     padded = ceil_to(count, 16)
     pixels = float(features.shape[0] * rows)
-    shard = enc_weight.shape[2]
+    depth, shard = enc_weight.shape[0], enc_weight.shape[2]
     inside = shard % 16 == 0
     sizes = (rows, count, padded, pixels)
-    masks = window_masks(image_group, switches, lax.axis_index("rows") * count, count, padded)
-
-    both = jnp.concatenate([enc_weight, dec_weight])
-    flat = jnp.transpose(both[:, ::-1], (0, 2, 1, 3)).reshape(both.shape[0], shard, -1)
+    weights = [enc_weight, dec_weight]
     if not inside:
-        flat = lax.all_gather(flat, "rows", axis=1, tiled=True)
+        both = jnp.concatenate(weights)
+        flat = jnp.transpose(both[:, ::-1], (0, 2, 1, 3)).reshape(both.shape[0], shard, -1)
+        weights = [lax.all_gather(flat, "rows", axis=1, tiled=True)]
     pairs = jnp.stack([jnp.concatenate([enc_gain, dec_gain]), jnp.concatenate([enc_bias, dec_bias])], axis=1)
     pairs = jnp.pad(pairs, ((0, 0), (0, 6), (0, 0)))
 
-    planes, stat, z, full, weight = forward_block(
-        inside, *sizes, to_planes(features, count, padded), flat, pairs, masks
+    hits = jnp.pad(switches, (EDGE, padded - count + EDGE), constant_values=-LANE)[:, None]
+    decoded, stat, masks, z, full, weight = forward_block(
+        inside, *sizes, image_group, hits, features, pairs, weights
     )
-    grad = to_planes(d_decoded, count, padded).astype(F32)
-    grad, pair_grads, weight_grads = backward_block(
-        inside, *sizes, grad, z, stat, pairs, masks, full, weight
+    grad, pair_grads, *wgrads = backward_block(
+        inside, *sizes, d_decoded, z, stat, pairs, masks, full, weight
     )
     if not inside:
-        weight_grads = lax.psum_scatter(weight_grads, "rows", scatter_dimension=1, tiled=True).astype(F32)
-    layers = weight_grads.shape[0]
-    weight_grads = jnp.transpose(weight_grads.reshape(layers, shard, 9, -1)[:, :, ::-1], (0, 2, 1, 3))
+        wgrad = lax.psum_scatter(wgrads[0], "rows", scatter_dimension=1, tiled=True).astype(F32)
+        wgrad = jnp.transpose(wgrad.reshape(2 * depth, shard, 9, -1)[:, :, ::-1], (0, 2, 1, 3))
+        wgrads = [wgrad[:depth], wgrad[depth:]]
     return (
-        to_stream(planes, count),
-        to_stream(grad.astype(BF16), count),
-        weight_grads[:3],
-        weight_grads[3:],
-        pair_grads[:3, 1],
-        pair_grads[:3, 0],
-        pair_grads[3:, 1],
-        pair_grads[3:, 0],
+        decoded,
+        grad,
+        *wgrads,
+        pair_grads[:depth, 1],
+        pair_grads[:depth, 0],
+        pair_grads[depth:, 1],
+        pair_grads[depth:, 0],
     )
 
 

time: 395 us -> 346 us (0.88)
  Pallas kernels: 366 us -> 332 us
  local copies, waits for them, and re-layouts: 21.5 us -> 10.6 us
  other arithmetic: 6.07 us -> 2.03 us
    pallas_call x1, Pallas kernels: 204 us -> 169 us  [backward_block(): pl.pallas_call(functools.partial(backward_kernel, inside, layers, rows, c...]
    reshape x8 -> x0, local copies, waits for them, and re-layouts: 6.86 us -> none  [the longest x2 2.13 us: to_stream(): jnp.transpose(planes[:, :count], (1, 0, 2))]
    rev x1 -> x0, local copies, waits for them, and re-layouts: 4.74 us -> none  [shards(): weight_grads.reshape(layers, shard, 9, -1)[:, :, ::-1]]
    unnamed x14 -> x8, local copies, waits for them, and re-layouts: 4.7 us -> 8.14 us
where the time goes in v4:
time: 346 us; the launch traced here: 345 us
  Pallas kernels  332 us (96%)
  local copies, waits for them, and re-layouts  10.6 us (3%)
    pallas_call x1, Pallas kernels, backward_block(): pl.pallas_call(functools.partial(backward_kernel, inside, layers, rows, c...  169 us
    pallas_call x1, Pallas kernels, forward_block(): pl.pallas_call(functools.partial(forward_kernel, inside, layers, rows, co...  163 us
    unnamed x8, local copies, waits for them, and re-layouts  8.14 us

profile of v4, /device:TPU:9, one launch (start us, length us, event | category | flops | bytes accessed | tf_op | source)
XLA Modules:
  0.0 345.2 jit_solution(1637416375049535638)
XLA Ops:
  0.6 0.8 pad.8
  1.4 0.7 pad_maximum_fusion
  2.1 0.7 pad_maximum_fusion.1
  2.8 0.6 select_maximum_fusion.gb_ref.refs_2_
  3.4 0.9 broadcast_in_dim.4.switch_ref
  4.3 162.7 %forward_block.1 = (bf16[1932,128]{1,0:T(8,128)(2,1)}, f32[6,8,128]{2,1,0:T(8,128)}, f32[592,128]{1,0:T(8,128)}, f32[6,4,496,128]{3,2,1,0:T(8,128)}, bf16[6,4,49...) custom-call(s32[6]{0:T(128)} %group_ref.1, s32[592,1]{1,0:T(8,128)} %broadcast_in_dim.4.switch_ref, ...), custom_call_target="tpu_custom_call" | custom-call | tf_op jit(solution)/shard_map/forward_block/pallas_call | solution.py:856
  167.0 0.0 copy-start
  167.0 169.2 %backward_block.1 = (bf16[1932,128]{1,0:T(8,128)(2,1)}, f32[6,8,128]{2,1,0:T(8,128)}, f32[3,9,64,128]{3,2,1,0:T(8,128)}, f32[3,9,64,128]{3,2,1,0:T(8,128)}) custom-call(bf16[1932,128]{1,0:T(8,128)(2,1)} %refs_0_.3, f32[6,8,128]{2,1,0:T(8,128)} %get-tuple-element.19.refs_1_, f32[6,8,128]{2,1,0:T(8,128)} %select_maximum_fusion.gb_ref.refs_2_, ...), custom_call_target="tpu_custom_call" | custom-call | tf_op jit(solution)/shard_map/backward_block/pallas_call | solution.py:934
  336.2 0.8 fusion
  337.0 0.6 copy_bitcast_fusion
  337.6 0.6 copy_bitcast_fusion.2
  338.2 0.0 copy-done
  338.2 0.8 copy.31
  339.0 1.8 copy.32
  340.8 2.2 copy.33
  343.0 2.2 copy.34
  (2 shorter events, 0.0 us)
Async XLA Ops:
  167.0 171.2 %copy-start = (bf16[1932,128]{1,0:T(8,128)(2,1)S(1)}, bf16[1932,128]{1,0:T(8,128)(2,1)}, u32[]{:S(2)}) copy-start(bf16[1932,128]{1,0:T(8,128)(2,1)} %get-tuple-element.44) | copy-start | bytes 1483780

commit v5 on v4

--- a/solution.py
+++ b/solution.py
@@ -144,13 +144,29 @@
 
 def row_parts(padded, count):
     tail = (count - EDGE) // 16 * 16
-    parts = [(0, EDGE), (tail, padded - tail)]
-    start, steps = EDGE, 3
+    inner, start, steps = [], EDGE, 3
     for k in range(steps):
         size = min(ceil_to(-(-(tail - start) // (steps - k)), 16), tail - start)
-        parts.append((start, size))
+        inner.append((start, size))
         start += size
-    return parts
+    return [(0, EDGE), (tail, padded - tail), inner[0], inner[2], inner[1]]
+
+
+REACH = max(WIDTHS) + 1
+
+
+def far_pieces(parts):
+    low, size = parts[4]
+    first, last = (low - REACH) // 8 * 8, ceil_to(low + size + REACH, 8)
+    return [
+        (2, parts[2][0], first - parts[2][0]),
+        (3, last, parts[3][0] + parts[3][1] - last),
+        (0, *parts[0]),
+        (1, *parts[1]),
+        (2, first, parts[2][0] + parts[2][1] - first),
+        (3, parts[3][0], last - parts[3][0]),
+        (4, low, size),
+    ]
 
 
 def lanes_of(block):
@@ -290,14 +306,16 @@
     w_refs, refs = refs[: 1 + inside], refs[1 + inside :]
     (
         next_ref, stat_ref, mask_ref, z_out, full_out, w_out,
-        vbuf, wbuf, zbuf, yext, over, under, wide, to_next, to_prev, from_prev, from_next, sums,
+        vbuf, wbuf, zbuf, raw, coef, yext, over, under, wide, to_next, to_prev, from_prev, from_next, sums,
         core_s, core_r, x_s, x_r, fwd_s, fwd_r, halo_s, halo_r, sum_s, sum_r, out_sem,
-        w_s, w_r, wp_s, wp_r, first_s, first_r, first_ps, first_pr,
+        coef_s, coef_r, w_s, w_r, wp_s, wp_r, first_s, first_r, first_ps, first_pr,
     ) = refs
     mine, here = lax.axis_index("grp"), lax.axis_index("rows")
     half = mine // 2
     partner, across = grp_peers()
+    diagonal = (here, across[1] + partner[1] - mine)
     parts = row_parts(padded, count)
+    pieces = far_pieces(parts)
     own_lanes, far_lanes = lanes_of(mine), lanes_of(across[1])
     own_base = pl.multiple_of(half * 2 * LANE, 2 * LANE)
     far_base = pl.multiple_of((1 - half) * 2 * LANE, 2 * LANE)
@@ -307,19 +325,24 @@
 
     def slab(layer, k, lanes):
         low, size = parts[k]
-        return vbuf.at[layer, :, pl.ds(low, size), lanes]
-
-    def to_core(layer, k):
-        piece = slab(layer, k, own_lanes)
-        return remote(piece, piece, core_s.at[layer, k], core_r.at[layer, k], partner)
+        return raw.at[lax.rem(layer, 2), :, pl.ds(low, size), lanes]
+
+    def to_core(layer):
+        whole = raw.at[lax.rem(layer, 2), :, :, own_lanes]
+        return remote(whole, whole, core_s.at[layer], core_r.at[layer], partner)
 
     def to_far(layer, k):
-        piece = slab(layer, k, own_lanes)
+        _, low, size = pieces[k]
+        piece = raw.at[lax.rem(layer, 2), :, pl.ds(low, size), own_lanes]
         return remote(piece, piece, x_s.at[layer, k], x_r.at[layer, k], across)
 
     def pass_on(layer, k):
         piece = slab(layer, k, far_lanes)
         return remote(piece, piece, fwd_s.at[layer, k], fwd_r.at[layer, k], partner)
+
+    def coef_copy(layer, k):
+        own = coef.at[lax.rem(layer, 2), mine]
+        return remote(own, own, coef_s.at[layer, k], coef_r.at[layer, k], (partner, across, diagonal)[k])
 
     def load(layer):
         return pltpu.make_async_copy(w_refs[0].at[layer], wbuf.at[layer], w_s.at[layer, 0])
@@ -351,10 +374,46 @@
                         yext[where] = block
                         touched.add(spot)
 
+    def fill(layer, k, chip):
+        low, size = parts[k]
+        side = lax.rem(layer, 2)
+        rows_here = slice(low, low + size)
+        lanes = pl.ds(pl.multiple_of(chip * 2 * LANE, 2 * LANE), 2 * LANE)
+
+        def kept(which):
+            return mask_of(mask_ref, which, EDGE + low, size)
+
+        def activation(q):
+            scale, offset = (
+                jnp.concatenate([coef[side, chip * 2, n : n + 1], coef[side, chip * 2 + 1, n : n + 1]], axis=1)
+                for n in range(2)
+            )
+            y = raw[side, q, rows_here, lanes].astype(F32) * scale + offset
+            return y * jax.nn.sigmoid(y)
+
+        @pl.when(layer == 0)
+        def _():
+            for q in range(4):
+                vbuf[layer, q, rows_here, lanes] = raw[side, q, rows_here, lanes]
+
+        @pl.when(jnp.logical_and(layer != 0, layer != POOL + 1))
+        def _():
+            for q in range(4):
+                block = activation(q)
+                if low + size > count:
+                    block = jnp.where(kept(M_VALID), block, 0.0)
+                vbuf[layer, q, rows_here, lanes] = block.astype(BF16)
+
+        @pl.when(layer == POOL + 1)
+        def _():
+            pooled = smooth_max([activation(q) for q in range(4)])
+            for q in range(4):
+                vbuf[layer, q, rows_here, lanes] = jnp.where(kept(M_HIT + q), pooled, 0.0).astype(BF16)
+
     def at(low, size, spot):
         return yext[low : low + size, spot * LANE : (spot + 1) * LANE]
 
-    greet([partner, across] + row_peers(rows))
+    greet([partner, across, diagonal] + row_peers(rows))
     if inside:
         own_rows = gather.rows_of(0, gather.low)
         for layer in range(layers):
@@ -365,14 +424,16 @@
             if layer == 0:
                 for piece in range(3):
                     first_gather.start(0, piece)
+            elif layer <= 2:
+                gather.start(layer)
     else:
         load(0).start()
     split_planes(v_ref, wide, count)
     for q in range(4):
-        vbuf[0, q, :, own_lanes] = plane(wide, q).astype(BF16)
-    for k in range(len(parts)):
+        raw[0, q, :, own_lanes] = plane(wide, q).astype(BF16)
+    to_core(0).start()
+    for k in range(len(pieces)):
         to_far(0, k).start()
-        to_core(0, k).start()
     yext[:EDGE, :] = jnp.zeros((EDGE, yext.shape[1]), F32)
     yext[EDGE + padded :, :] = jnp.zeros((EDGE, yext.shape[1]), F32)
     fill_masks(group_ref, here * count, count, padded, switch_ref, mask_ref)
@@ -385,36 +446,54 @@
 
     def layer_step(layer):
         more = layer + 1 < layers
+        def forward_gathers(condition, which, steps):
+            @pl.when(condition)
+            def _():
+                for step in steps:
+                    gather.forward(which, step)
+
+        far = rows // 2
+        if not inside:
+            load(layer).wait()
+
+            @pl.when(more)
+            def _():
+                load(layer + 1).start()
+
+        to_core(layer).wait_recv()
+
+        @pl.when(layer > 0)
+        def _():
+            coef_copy(layer, 0).wait_recv()
+
+        def take(part):
+            for k, piece in enumerate(pieces):
+                if piece[0] == part:
+                    to_far(layer, k).wait_recv()
+            pass_on(layer, part).start()
+
+        for k in range(len(parts)):
+            fill(layer, k, half)
+        take(0)
+        take(1)
         if inside:
+
             @pl.when(layer > 0)
             def _():
                 gather.wait(layer)
 
             save(layer, 2).start()
-
-            @pl.when(more)
-            def _():
-                gather.start(layer + 1)
-        else:
-            load(layer).wait()
-
-            @pl.when(more)
-            def _():
-                load(layer + 1).start()
-
-        for k in range(len(parts)):
-            to_core(layer, k).wait_recv()
         add_products(layer, 0, padded, own_base, set())
 
-        def gather_forward(first, end):
-            @pl.when(more)
-            def _():
-                for step in range(first, end):
-                    gather.forward(layer + 1, step)
+        @pl.when(layer > 0)
+        def _():
+            for k in range(1, 3):
+                coef_copy(layer, k).wait_recv()
 
         def far_products(k):
             pass_on(layer, k).wait_recv()
             low, size = parts[k]
+            fill(layer, k, 1 - half)
             add_products(layer, low, size, far_base, set(range(16)))
             if k != 1:
                 return
@@ -431,122 +510,165 @@
             def _():
                 up.start()
 
-        for k in range(len(parts)):
-            to_far(layer, k).wait_recv()
-            pass_on(layer, k).start()
-            if k > 0:
-                far_products(k - 1)
-            if inside and k == 2:
-                gather_forward(1, 2)
-        far_products(len(parts) - 1)
-        save(layer, 0).start()
-        if inside:
-            gather_forward(2, rows // 2)
-
-        @pl.when(here > 0)
-        def _():
-            down.wait_recv()
-            up.wait_send()
-            for lane, spot in enumerate((12, 13, 14, 15, 7, 11)):
-                received = from_prev[:, lane * LANE : (lane + 1) * LANE].astype(F32)
-                yext[:EDGE, spot * LANE : (spot + 1) * LANE] = received
-
-        @pl.when(here + 1 < rows)
-        def _():
-            up.wait_recv()
-            down.wait_send()
-            for lane, spot in enumerate((0, 1, 2, 3, 4, 8)):
-                received = from_next[:, lane * LANE : (lane + 1) * LANE].astype(F32)
-                yext[EDGE + count : 2 * EDGE + count, spot * LANE : (spot + 1) * LANE] = received
-
-        low, size = 8, padded + 2 * EDGE - 16
-        go_left = mask_of(mask_ref, M_LEFT, low, size)
-        go_right = mask_of(mask_ref, M_RIGHT, low, size)
-        for kept, first in ((over, 12), (under, 0)):
+        def receive_halos():
+            @pl.when(here > 0)
+            def _():
+                down.wait_recv()
+                up.wait_send()
+                for lane, spot in enumerate((12, 13, 14, 15, 7, 11)):
+                    received = from_prev[:, lane * LANE : (lane + 1) * LANE].astype(F32)
+                    yext[:EDGE, spot * LANE : (spot + 1) * LANE] = received
+
+            @pl.when(here + 1 < rows)
+            def _():
+                up.wait_recv()
+                down.wait_send()
+                for lane, spot in enumerate((0, 1, 2, 3, 4, 8)):
+                    received = from_next[:, lane * LANE : (lane + 1) * LANE].astype(F32)
+                    yext[EDGE + count : 2 * EDGE + count, spot * LANE : (spot + 1) * LANE] = received
+
+        def over_columns(kept, first, begin, end):
+            low, size = EDGE + begin, end - begin
+            go_left = mask_of(mask_ref, M_LEFT, low, size)
+            go_right = mask_of(mask_ref, M_RIGHT, low, size)
             kept[low : low + size, :LANE] = at(low, size, first + 1) + jnp.where(
                 go_left, at(low - 1, size, first + 3), 0.0
             )
             kept[low : low + size, LANE:] = at(low, size, first + 2) + jnp.where(
                 go_right, at(low + 1, size, first), 0.0
             )
-        go_left = mask_of(mask_ref, M_LEFT, EDGE, padded)
-        go_right = mask_of(mask_ref, M_RIGHT, EDGE, padded)
-        valid = mask_of(mask_ref, M_VALID, EDGE, padded)
-        total = jnp.zeros((1, LANE), F32)
-        squares = jnp.zeros((1, LANE), F32)
-        for q in range(4):
-            a, b = q // 2, q % 2
-            lanes = slice(b * LANE, (b + 1) * LANE)
-            kept, sign = (over, -1) if a == 0 else (under, 1)
-            rowwise = by_width(
-                mask_ref, EDGE, padded,
-                lambda w: kept[EDGE + sign * w : EDGE + sign * w + padded, lanes],
-            )
-            z = at(EDGE, padded, (a + 1) * 4 + b + 1)
-            z = z + jnp.where(mask_of(mask_ref, (M_UP, M_DOWN)[a], EDGE, padded), rowwise, 0.0)
-            if b == 0:
-                z = z + jnp.where(go_left, at(EDGE - 1, padded, (a + 1) * 4 + 3), 0.0)
-            else:
-                z = z + jnp.where(go_right, at(EDGE + 1, padded, (a + 1) * 4), 0.0)
-            z = jnp.where(valid, z, 0.0)
-            zbuf[layer, q] = z
-            total = total + jnp.sum(z, axis=0, keepdims=True)
-            squares = squares + jnp.sum(z * z, axis=0, keepdims=True)
+
+        def assemble(begin, end, sums_so_far):
+            low, size = EDGE + begin, end - begin
+            go_left = mask_of(mask_ref, M_LEFT, low, size)
+            go_right = mask_of(mask_ref, M_RIGHT, low, size)
+            total, squares = sums_so_far
+            for q in range(4):
+                a, b = q // 2, q % 2
+                lanes = slice(b * LANE, (b + 1) * LANE)
+                kept, sign = (over, -1) if a == 0 else (under, 1)
+                rowwise = by_width(
+                    mask_ref, low, size, lambda w: kept[low + sign * w : low + sign * w + size, lanes]
+                )
+                z = at(low, size, (a + 1) * 4 + b + 1)
+                z = z + jnp.where(mask_of(mask_ref, (M_UP, M_DOWN)[a], low, size), rowwise, 0.0)
+                if b == 0:
+                    z = z + jnp.where(go_left, at(low - 1, size, (a + 1) * 4 + 3), 0.0)
+                else:
+                    z = z + jnp.where(go_right, at(low + 1, size, (a + 1) * 4), 0.0)
+                if end > count:
+                    z = jnp.where(mask_of(mask_ref, M_VALID, low, size), z, 0.0)
+                zbuf[layer, q, begin:end] = z
+                total = total + jnp.sum(z, axis=0, keepdims=True)
+                squares = squares + jnp.sum(z * z, axis=0, keepdims=True)
+            return total, squares
+
+        def prepare(k):
+            _, low, size = pieces[k]
+            for q in range(4):
+                piece = zbuf[layer, q, low : low + size] - local
+                raw[lax.rem(layer + 1, 2), q, low : low + size, own_lanes] = piece.astype(BF16)
+
+        if inside:
+            forward_gathers(jnp.logical_and(layer < 2, more), layer + 1, range(1, 2))
+            forward_gathers(jnp.logical_and(layer > 1, more), layer + 1, range(2, 3))
+        take(2)
+        far_products(0)
+        far_products(1)
+        take(3)
+        far_products(2)
+        far_products(3)
+        take(4)
+        if inside:
+            forward_gathers(jnp.logical_and(layer < 2, more), layer + 1, range(2, far - 1))
+            forward_gathers(jnp.logical_and(layer > 1, more), layer + 1, range(3, far))
+        near, widest = min(WIDTHS), max(WIDTHS)
+        (_, top, size), (_, bottom, last_size) = pieces[:2]
+        first = (top, top + size)
+        last = (bottom, bottom + last_size)
+        over_ready = [(n - widest, ceil_to(m - near, 8)) for n, m in (first, last)]
+        under_ready = [((n + near) // 8 * 8, m + widest) for n, m in (first, last)]
+        for kept, spot, ready in ((over, 12, over_ready), (under, 0, under_ready)):
+            for begin, end in ready:
+                over_columns(kept, spot, begin, end)
+        none = (jnp.zeros((1, LANE), F32),) * 2
+        inner = assemble(*last, assemble(*first, none))
+        local = inner[0] / (4.0 * (size + last_size))
+
+        @pl.when(more)
+        def _():
+            for k in range(2):
+                prepare(k)
+                to_far(layer + 1, k).start()
+
+        far_products(4)
+        save(layer, 0).start()
+        receive_halos()
+        over_rest = [(8 - EDGE, over_ready[0][0]), (over_ready[0][1], over_ready[1][0]), (over_ready[1][1], padded)]
+        under_rest = [(0, under_ready[0][0]), (under_ready[0][1], under_ready[1][0]), (under_ready[1][1], padded + EDGE - 8)]
+        for kept, spot, rest in ((over, 12, over_rest), (under, 0, under_rest)):
+            for begin, end in rest:
+                over_columns(kept, spot, begin, end)
+        total, squares = assemble(last[1], padded, assemble(first[1], last[0], assemble(0, first[0], inner)))
         save(layer, 1).start()
         own = jnp.concatenate([total, squares, jnp.zeros((6, LANE), F32)], axis=0)
         channel = (sums.at[layer], sum_s.at[layer], sum_r.at[layer])
         send_sums(rows, own, *channel)
+
+        @pl.when(more)
+        def _():
+            for k in range(2, len(pieces)):
+                prepare(k)
+                if k < 4:
+                    to_far(layer + 1, k).start()
+            to_core(layer + 1).start()
+
+        for k in range(len(pieces)):
+            to_far(layer, k).wait_send()
+        for k in range(len(parts)):
+            pass_on(layer, k).wait_send()
+        to_core(layer).wait_send()
+
+        @pl.when(layer > 0)
+        def _():
+            for k in range(3):
+                coef_copy(layer, k).wait_send()
+
+        if inside:
+            forward_gathers(jnp.logical_and(layer < 2, more), layer + 1, range(far - 1, far))
         both = add_sums(rows, *channel)
         mean = both[0:1] / pixels
         inverse = lax.rsqrt(both[1:2] / pixels - mean * mean + EPSILON)
         stat_ref[layer] = jnp.concatenate([mean, inverse, jnp.zeros((6, LANE), F32)], axis=0)
-
-        def activation(k, q):
-            low, size = parts[k]
-            y = gb_ref[layer, 0:1] * ((zbuf[layer, q, low : low + size] - mean) * inverse) + gb_ref[layer, 1:2]
-            return y * jax.nn.sigmoid(y)
-
-        def kept(k, which):
-            low, size = parts[k]
-            return mask_of(mask_ref, which, EDGE + low, size)
-
-        def pass_to_next(of_part):
-            for k, (low, size) in enumerate(parts):
-                blocks = of_part(k)
-                for q in range(4):
-                    vbuf[layer + 1, q, low : low + size, own_lanes] = blocks[q].astype(BF16)
+        scale = gb_ref[layer, 0:1] * inverse
+
+        @pl.when(more)
+        def _():
+            offset = scale * (local - mean) + gb_ref[layer, 1:2]
+            coef[lax.rem(layer + 1, 2), mine] = jnp.concatenate([scale, offset, jnp.zeros((6, LANE), F32)], axis=0)
+            for k in range(3):
+                coef_copy(layer + 1, k).start()
+            for k in range(4, len(pieces)):
                 to_far(layer + 1, k).start()
-                to_core(layer + 1, k).start()
-
-        def plain(k):
-            return [jnp.where(kept(k, M_VALID), activation(k, q), 0.0) for q in range(4)]
-
-        def unpooled(k):
-            pooled = smooth_max([activation(k, q) for q in range(4)])
-            return [jnp.where(kept(k, M_HIT + q), pooled, 0.0) for q in range(4)]
-
-        @pl.when(jnp.logical_and(more, layer != POOL))
-        def _():
-            pass_to_next(plain)
-
-        @pl.when(layer == POOL)
-        def _():
-            pass_to_next(unpooled)
+
+        if inside:
+
+            @pl.when(layer + 3 < layers)
+            def _():
+                gather.start(layer + 3)
+
+            forward_gathers(jnp.logical_and(layer > 0, layer + 2 < layers), layer + 2, range(1, 2))
 
         @pl.when(layer + 1 == layers)
         def _():
-            for k, (low, size) in enumerate(parts):
-                for q, block in enumerate(plain(k)):
-                    set_plane(wide, q, low, block)
+            for q in range(4):
+                y = scale * (zbuf[layer, q] - mean) + gb_ref[layer, 1:2]
+                set_plane(wide, q, 0, y * jax.nn.sigmoid(y))
             next_ref[...] = wide[: 4 * count].astype(BF16)
 
     each(layers, layer_step)
 
     def drain(layer):
-        for k in range(len(parts)):
-            to_far(layer, k).wait_send()
-            to_core(layer, k).wait_send()
-            pass_on(layer, k).wait_send()
         if inside:
 
             @pl.when(layer > 0)
@@ -870,6 +992,8 @@
             pltpu.VMEM((layers, 4, padded, channels), BF16),
             pltpu.VMEM((layers, channels, taps), BF16),
             pltpu.VMEM((layers, 4, padded, LANE), F32),
+            pltpu.VMEM((2, 4, padded, channels), BF16),
+            pltpu.VMEM((2, 4, 8, LANE), F32),
             pltpu.VMEM((ext, 16 * LANE), F32),
             pltpu.VMEM((ext, 2 * LANE), F32),
             pltpu.VMEM((ext, 2 * LANE), F32),
@@ -877,10 +1001,12 @@
         ]
         + [pltpu.VMEM((EDGE, 6 * LANE), BF16)] * 4
         + [pltpu.VMEM((layers, rows, 8, LANE), F32)]
-        + [DMA((layers, n_parts))] * 6
+        + [DMA((layers,))] * 2
+        + [DMA((layers, len(far_pieces(row_parts(padded, count)))))] * 2
+        + [DMA((layers, n_parts))] * 2
         + [DMA((2,))] * 2
         + [DMA((layers, rows - 1))] * 2
-        + [DMA((layers, 3))]
+        + [DMA((layers, 3))] * 3
         + [DMA((layers, far - 1))] * 2
         + [DMA((layers, far))] * 2
         + [DMA((3, far - 1))] * 2

time: 346 us -> 328 us (0.948)
  Pallas kernels: 332 us -> 314 us
    pallas_call x1, Pallas kernels: 163 us -> 145 us  [forward_block(): pl.pallas_call(functools.partial(forward_kernel, inside, layers, rows, co...]
where the time goes in v5:
time: 328 us; the launch traced here: 327 us
  Pallas kernels  314 us (96%)
  local copies, waits for them, and re-layouts  10.6 us (3%)
    pallas_call x1, Pallas kernels, backward_block(): pl.pallas_call(functools.partial(backward_kernel, inside, layers, rows, c...  169 us
    pallas_call x1, Pallas kernels, forward_block(): pl.pallas_call(functools.partial(forward_kernel, inside, layers, rows, co...  145 us
    unnamed x8, local copies, waits for them, and re-layouts  8.14 us

profile of v5, /device:TPU:9, one launch (start us, length us, event | category | flops | bytes accessed | tf_op | source)
XLA Modules:
  0.0 327.4 jit_solution(6258375636058356531)
XLA Ops:
  0.6 0.8 pad.8
  1.4 0.7 pad_maximum_fusion
  2.1 0.7 pad_maximum_fusion.1
  2.8 0.6 select_maximum_fusion.gb_ref.refs_2_
  3.4 0.9 broadcast_in_dim.4.switch_ref
  4.3 144.7 %forward_block.1 = (bf16[1932,128]{1,0:T(8,128)(2,1)}, f32[6,8,128]{2,1,0:T(8,128)}, f32[592,128]{1,0:T(8,128)}, f32[6,4,496,128]{3,2,1,0:T(8,128)}, bf16[6,4,49...) custom-call(s32[6]{0:T(128)} %group_ref.1, s32[592,1]{1,0:T(8,128)} %broadcast_in_dim.4.switch_ref, ...), custom_call_target="tpu_custom_call" | custom-call | tf_op jit(solution)/shard_map/forward_block/pallas_call | solution.py:978
  149.0 0.0 copy-start
  149.0 169.5 %backward_block.1 = (bf16[1932,128]{1,0:T(8,128)(2,1)}, f32[6,8,128]{2,1,0:T(8,128)}, f32[3,9,64,128]{3,2,1,0:T(8,128)}, f32[3,9,64,128]{3,2,1,0:T(8,128)}) custom-call(bf16[1932,128]{1,0:T(8,128)(2,1)} %refs_0_.3, f32[6,8,128]{2,1,0:T(8,128)} %get-tuple-element.19.refs_1_, f32[6,8,128]{2,1,0:T(8,128)} %select_maximum_fusion.gb_ref.refs_2_, ...), custom_call_target="tpu_custom_call" | custom-call | tf_op jit(solution)/shard_map/backward_block/pallas_call | solution.py:1060
  318.5 0.8 fusion
  319.3 0.6 copy_bitcast_fusion
  319.9 0.6 copy_bitcast_fusion.2
  320.5 0.0 copy-done
  320.5 0.8 copy.31
  321.2 1.8 copy.32
  323.1 2.2 copy.33
  325.3 2.2 copy.34
  (2 shorter events, 0.0 us)
Async XLA Ops:
  149.0 171.5 %copy-start = (bf16[1932,128]{1,0:T(8,128)(2,1)S(1)}, bf16[1932,128]{1,0:T(8,128)(2,1)}, u32[]{:S(2)}) copy-start(bf16[1932,128]{1,0:T(8,128)(2,1)} %get-tuple-element.44) | copy-start | bytes 1483780

commit v6 on v5

--- a/solution.py
+++ b/solution.py
@@ -223,12 +223,12 @@
 
 
 class Scatter:
-    def __init__(self, rows, shard, grads, first, second, third, total, outs, send, recv, far_send, far_recv):
+    def __init__(self, rows, shard, grads, first, second, third, total, outs, semaphores):
         self.shard, self.grads, self.first, self.second, self.third = shard, grads, first, second, third
         self.total, self.outs, self.far = total, outs, rows // 2
         here, self.there = lax.axis_index("rows"), lax.axis_index("grp")
         self.high, self.low = here // 2, lax.rem(here, 2)
-        self.send, self.recv, self.far_send, self.far_recv = send, recv, far_send, far_recv
+        self.semaphores = semaphores
 
     def rows_of(self, step, low):
         block = lax.rem(self.high + step, self.far) * 2 + low
@@ -236,26 +236,28 @@
 
     def across(self, turn, step):
         slot = lax.rem(turn, 3)
+        send, recv, _, _ = self.semaphores
         peer = (self.high * 2 + 1 - self.low, self.there)
         return remote(
             self.grads.at[slot, self.rows_of(step, 1 - self.low), :], self.first.at[slot, step],
-            self.send.at[slot, step], self.recv.at[slot, step], peer,
+            send.at[slot, step], recv.at[slot, step], peer,
         )
 
     def spread(self, turn, step):
         slot = lax.rem(turn, 3)
+        _, _, send, recv = self.semaphores
         peer = (lax.rem(self.high + step, self.far) * 2 + self.low, self.there)
         k = step - 1
         return remote(
             self.second.at[slot, k], self.third.at[slot, k],
-            self.far_send.at[slot, k], self.far_recv.at[slot, k], peer,
+            send.at[slot, k], recv.at[slot, k], peer,
         )
 
     def order(self):
         return list(range(1, self.far)) + [0]
 
-    def start(self, turn):
-        for step in self.order():
+    def start(self, turn, steps):
+        for step in steps:
             self.across(turn, step).start()
 
     def forward(self, turn, step):
@@ -271,9 +273,10 @@
 
     def finish(self, turn, layer):
         slot = lax.rem(turn, 3)
+        for step in range(1, self.far):
+            self.spread(turn, step).wait_recv()
         total = self.total[slot]
         for step in range(1, self.far):
-            self.spread(turn, step).wait_recv()
             total = total + self.third[slot, step - 1].astype(F32)
         depth = self.outs[0].shape[0]
 
@@ -298,6 +301,20 @@
 
 def each(count, body):
     lax.fori_loop(0, count, lambda i, carry: (body(i), carry)[1], 0)
+
+
+GATHER_PLAN = {
+    "products": {0: [("pass", 1, 1)]},
+    "parts": {0: [("pass", 1, 2)]},
+    "outer": {},
+    "sums": {0: [("pass", 1, 3)]},
+    "norm": {},
+}
+for turn in range(4):
+    GATHER_PLAN["norm"][turn] = [("out", turn + 2, 1), ("out", turn + 2, 2), ("own", turn + 2, 0)]
+    GATHER_PLAN["parts"][turn + 1] = [("pass", turn + 2, 1)]
+    GATHER_PLAN["outer"][turn + 1] = [("out", turn + 2, 3), ("pass", turn + 2, 2)]
+    GATHER_PLAN["sums"][turn + 1] = [("pass", turn + 2, 3)]
 
 
 def forward_kernel(
@@ -424,7 +441,7 @@
             if layer == 0:
                 for piece in range(3):
                     first_gather.start(0, piece)
-            elif layer <= 2:
+            elif layer <= 1:
                 gather.start(layer)
     else:
         load(0).start()
@@ -446,13 +463,21 @@
 
     def layer_step(layer):
         more = layer + 1 < layers
-        def forward_gathers(condition, which, steps):
-            @pl.when(condition)
-            def _():
-                for step in steps:
-                    gather.forward(which, step)
-
-        far = rows // 2
+        def gather_at(point):
+            if not inside:
+                return
+            for turn, actions in GATHER_PLAN[point].items():
+
+                @pl.when(layer == turn)
+                def _(actions=actions):
+                    for action, which, step in actions:
+                        if action == "pass":
+                            gather.forward(which, step)
+                        elif action == "out":
+                            gather.spread(which, step).start()
+                        else:
+                            gather.across(which, 0).start()
+
         if not inside:
             load(layer).wait()
 
@@ -569,9 +594,7 @@
                 piece = zbuf[layer, q, low : low + size] - local
                 raw[lax.rem(layer + 1, 2), q, low : low + size, own_lanes] = piece.astype(BF16)
 
-        if inside:
-            forward_gathers(jnp.logical_and(layer < 2, more), layer + 1, range(1, 2))
-            forward_gathers(jnp.logical_and(layer > 1, more), layer + 1, range(2, 3))
+        gather_at("products")
         take(2)
         far_products(0)
         far_products(1)
@@ -579,9 +602,7 @@
         far_products(2)
         far_products(3)
         take(4)
-        if inside:
-            forward_gathers(jnp.logical_and(layer < 2, more), layer + 1, range(2, far - 1))
-            forward_gathers(jnp.logical_and(layer > 1, more), layer + 1, range(3, far))
+        gather_at("parts")
         near, widest = min(WIDTHS), max(WIDTHS)
         (_, top, size), (_, bottom, last_size) = pieces[:2]
         first = (top, top + size)
@@ -601,6 +622,7 @@
                 prepare(k)
                 to_far(layer + 1, k).start()
 
+        gather_at("outer")
         far_products(4)
         save(layer, 0).start()
         receive_halos()
@@ -634,8 +656,7 @@
             for k in range(3):
                 coef_copy(layer, k).wait_send()
 
-        if inside:
-            forward_gathers(jnp.logical_and(layer < 2, more), layer + 1, range(far - 1, far))
+        gather_at("sums")
         both = add_sums(rows, *channel)
         mean = both[0:1] / pixels
         inverse = lax.rsqrt(both[1:2] / pixels - mean * mean + EPSILON)
@@ -651,13 +672,7 @@
             for k in range(4, len(pieces)):
                 to_far(layer + 1, k).start()
 
-        if inside:
-
-            @pl.when(layer + 3 < layers)
-            def _():
-                gather.start(layer + 3)
-
-            forward_gathers(jnp.logical_and(layer > 0, layer + 2 < layers), layer + 2, range(1, 2))
+        gather_at("norm")
 
         @pl.when(layer + 1 == layers)
         def _():
@@ -692,10 +707,10 @@
     wgrad_refs = refs[2 : 3 + inside]
     del refs[: 3 + inside]
     (
-        grad_ref, wide, zbuf, fbuf, wbuf, dk, gy, gext, above, below, patch, part, keep, core_out, core_in, x_out, x_in,
+        grad_ref, wide, partial, zbuf, fbuf, wbuf, dk, gy, gext, above, below, patch, part, keep, core_out, core_in, x_out, x_in,
         to_next, to_prev, from_prev, from_next, sums,
         core_s, core_r, x_s, x_r, halo_s, halo_r, sum_s, sum_r, load_sem, out_sem,
-    ) = refs[:32]
+    ) = refs[:33]
     mine, here = lax.axis_index("grp"), lax.axis_index("rows")
     half, core = mine // 2, lax.rem(mine, 2)
     partner, across = grp_peers()
@@ -703,9 +718,9 @@
     own_base = pl.multiple_of(half * 2 * LANE, 2 * LANE)
     far_base = pl.multiple_of((1 - half) * 2 * LANE, 2 * LANE)
     if inside:
-        first, second, third, total_ref, s1, r1, s2, r2 = refs[32:]
+        first, second, third, total_ref = refs[33:37]
         shard = dk.shape[1] // rows
-        scatter = Scatter(rows, shard, dk, first, second, third, total_ref, wgrad_refs, s1, r1, s2, r2)
+        scatter = Scatter(rows, shard, dk, first, second, third, total_ref, wgrad_refs, refs[37:41])
 
     def load(turn, which):
         src, dst = ((z_in, zbuf), (w_in, wbuf), (full_in, fbuf))[which]
@@ -722,11 +737,27 @@
     after = (lax.rem(here + 1, rows), mine)
     before = (lax.rem(here + rows - 1, rows), mine)
     split_planes(g_ref, wide, count)
-    for q in range(4):
-        grad_ref[q] = plane(wide, q)
     gext[:EDGE, :] = jnp.zeros((EDGE, 4 * LANE), F32)
     gext[EDGE + padded :, :] = jnp.zeros((EDGE, 4 * LANE), F32)
     greet([partner, across] + row_peers(rows))
+    load(0, 0).wait()
+    partial[...] = jnp.zeros_like(partial)
+
+    def norm_of(layer):
+        return stat_ref[layer, 0:1], stat_ref[layer, 1:2], gb_ref[layer, 0:1], gb_ref[layer, 1:2]
+
+    def shifted(turn, q):
+        mean, inverse, gain, shift = norm_of(layers - 1 - turn)
+        normed = (zbuf[lax.rem(turn, 2), q] - mean) * inverse
+        return normed, gain * normed + shift
+
+    def begin(turn, q, grad):
+        normed, y = shifted(turn, q)
+        s = jax.nn.sigmoid(y)
+        grad = jnp.where(mask_of(mask_ref, M_VALID, EDGE, padded), grad * s * (1.0 + y * (1.0 - s)), 0.0)
+        gy[q] = grad
+        partial[0:1] += jnp.sum(grad, axis=0, keepdims=True)
+        partial[1:2] += jnp.sum(grad * normed, axis=0, keepdims=True)
 
     def taps(q, step):
         first = (q // 2 + step) * 4 + q % 2
@@ -736,39 +767,24 @@
         layer = layers - 1 - turn
         side, slot = lax.rem(turn, 2), lax.rem(turn, 3)
         last = turn + 1 == layers
-        mean, inverse = stat_ref[layer, 0:1], stat_ref[layer, 1:2]
-        gain, shift = gb_ref[layer, 0:1], gb_ref[layer, 1:2]
-        valid = mask_of(mask_ref, M_VALID, EDGE, padded)
-        load(turn, 0).wait()
         down = remote(to_next, from_prev.at[side], halo_s.at[0], halo_r.at[side, 0], after)
         up = remote(to_prev, from_next.at[side], halo_s.at[1], halo_r.at[side, 1], before)
-
-        def shifted(q):
-            normed = (zbuf[side, q] - mean) * inverse
-            return normed, gain * normed + shift
+        mean, inverse, gain, _ = norm_of(layer)
+        valid = mask_of(mask_ref, M_VALID, EDGE, padded)
 
         @pl.when(layer == POOL)
         def _():
+            load(turn, 0).wait()
             pooled_grad = jnp.zeros((padded, LANE), F32)
             for q in range(4):
                 pooled_grad = jnp.where(mask_of(mask_ref, M_HIT + q, EDGE, padded), grad_ref[q], pooled_grad)
-            blocks = []
             for q in range(4):
-                _, y = shifted(q)
+                _, y = shifted(turn, q)
                 gy[q] = y * jax.nn.sigmoid(y)
             pooled = smooth_max([gy[q] for q in range(4)])
+            partial[...] = jnp.zeros_like(partial)
             for q in range(4):
-                grad_ref[q] = pooled_grad * (jnp.exp(gy[q] - pooled) * 0.25)
-
-        shift_sum = jnp.zeros((1, LANE), F32)
-        gain_sum = jnp.zeros((1, LANE), F32)
-        for q in range(4):
-            normed, y = shifted(q)
-            s = jax.nn.sigmoid(y)
-            grad = jnp.where(valid, grad_ref[q] * s * (1.0 + y * (1.0 - s)), 0.0)
-            gy[q] = grad
-            shift_sum = shift_sum + jnp.sum(grad, axis=0, keepdims=True)
-            gain_sum = gain_sum + jnp.sum(grad * normed, axis=0, keepdims=True)
+                begin(turn, q, pooled_grad * (jnp.exp(gy[q] - pooled) * 0.25))
 
         def spread(buf, low, planes):
             for lane, q in enumerate(planes):
@@ -788,24 +804,26 @@
         def _():
             up.start()
 
-        own = jnp.concatenate([shift_sum, gain_sum, jnp.zeros((6, LANE), F32)], axis=0)
+        own = partial[...]
         channel = (sums.at[side], sum_s.at[side], sum_r.at[side])
         send_sums(rows, own, *channel)
+        both = add_sums(rows, *channel)
+        gbgrad_ref[layer] = both
         if inside:
 
             @pl.when(turn > 0)
             def _():
-                scatter.start(turn - 1)
-
-        both = add_sums(rows, *channel)
-        gbgrad_ref[layer] = both
+                scatter.start(turn - 1, scatter.order()[2:])
+                for step in scatter.order()[:2]:
+                    scatter.forward(turn - 1, step)
+
 
         def conv_grad(grad, normed):
             out = inverse * gain * (grad - both[0:1] / pixels - normed * both[1:2] / pixels)
             return out.astype(BF16).astype(F32)
 
         for q in range(4):
-            normed, _ = shifted(q)
+            normed, _ = shifted(turn, q)
             gext[EDGE : EDGE + padded, q * LANE : (q + 1) * LANE] = jnp.where(
                 valid, conv_grad(gy[q], normed), 0.0
             )
@@ -877,7 +895,6 @@
                 scatter.finish(turn - 2, layer + 2)
                 scatter.drain(turn - 2)
 
-            scatter_forward(1)
         load(turn, 1).wait()
         load(turn, 2).wait()
         if not inside:
@@ -890,7 +907,7 @@
         def _():
             kernel_grad()
             if inside:
-                scatter.start(turn)
+                scatter.start(turn, scatter.order())
 
         def input_grad(q, base):
             total = None
@@ -923,12 +940,15 @@
             to_core(spot).start()
             if 2 <= spot < 6:
                 send_across(spot - 2)
-            if inside and spot == 5:
-                scatter_forward(2)
+            if inside and spot == 3:
+                for step in scatter.order()[2:-1]:
+                    scatter_forward(step)
 
         @pl.when(jnp.logical_not(last))
         def _():
             kernel_grad()
+            if inside:
+                scatter.start(turn, scatter.order()[:2])
 
         @pl.when(turn + 2 < layers)
         def _():
@@ -936,25 +956,49 @@
                 load(turn + 2, which).start()
 
         if inside:
-            for step in range(3, rows // 2):
-                scatter_forward(step)
             scatter_forward(0)
-        for q in range(4):
+        if inside:
+
+            pass
+
+        def arrived(q):
             to_core(4 + q).wait_recv()
             to_far(q).wait_recv()
-            grad_ref[q] = keep[4 + q] + core_in[side, 4 + q].astype(F32) + x_in[side, q].astype(F32)
+            return keep[4 + q] + core_in[side, 4 + q].astype(F32) + x_in[side, q].astype(F32)
+
+        begin_next = jnp.logical_and(jnp.logical_not(last), layer - 1 != POOL)
+
+        @pl.when(begin_next)
+        def _():
+            load(turn + 1, 0).wait()
+            partial[...] = jnp.zeros_like(partial)
+            for q in range(4):
+                begin(turn + 1, q, arrived(q))
+
+        @pl.when(layer - 1 == POOL)
+        def _():
+            for q in range(4):
+                grad_ref[q] = arrived(q)
+
+        @pl.when(last)
+        def _():
+            for q in range(4):
+                if inside:
+                    scatter.forward(turn, scatter.order()[q])
+                grad_ref[q] = arrived(q)
+
         for spot in range(8):
             to_core(spot).wait_send()
         for q in range(4):
             to_far(q).wait_send()
 
+    for q in range(4):
+        begin(0, q, plane(wide, q))
     each(layers, layer_step)
     for q in range(4):
         set_plane(wide, q, 0, grad_ref[q])
     out_ref[...] = wide[: 4 * count].astype(BF16)
     if inside:
-        for step in scatter.order():
-            scatter.forward(layers - 1, step)
         for turn in (layers - 2, layers - 1):
             scatter.finish(turn, layers - 1 - turn)
             scatter.drain(turn)
@@ -1027,6 +1071,7 @@
     scratch = [
         pltpu.VMEM((4, padded, LANE), F32),
         pltpu.VMEM((4 * padded, LANE), F32),
+        pltpu.VMEM((8, LANE), F32),
         pltpu.VMEM((2, 4, padded, LANE), F32),
         pltpu.VMEM((2, 4, padded, channels), BF16),
         pltpu.VMEM((2, channels, taps), BF16),
@@ -1079,7 +1124,7 @@
     padded = ceil_to(count, 16)
     pixels = float(features.shape[0] * rows)
     depth, shard = enc_weight.shape[0], enc_weight.shape[2]
-    inside = shard % 16 == 0
+    inside = shard % 16 == 0 and rows == 8 and 2 * depth == 6
     sizes = (rows, count, padded, pixels)
     weights = [enc_weight, dec_weight]
     if not inside:

time: 328 us -> 316 us (0.963)
  Pallas kernels: 314 us -> 302 us
    pallas_call x1, Pallas kernels: 169 us -> 163 us  [backward_block(): pl.pallas_call(functools.partial(backward_kernel, inside, layers, rows, c...]
    pallas_call x1, Pallas kernels: 145 us -> 139 us  [forward_block(): pl.pallas_call(functools.partial(forward_kernel, inside, layers, rows, co...]
where the time goes in v6:
time: 316 us
  Pallas kernels  302 us (96%)
  local copies, waits for them, and re-layouts  10.6 us (3%)
    pallas_call x1, Pallas kernels, backward_block(): pl.pallas_call(functools.partial(backward_kernel, inside, layers, rows, c...  163 us
    pallas_call x1, Pallas kernels, forward_block(): pl.pallas_call(functools.partial(forward_kernel, inside, layers, rows, co...  139 us
    unnamed x8, local copies, waits for them, and re-layouts  8.14 us

profile of v6, /device:TPU:9, one launch (start us, length us, event | category | flops | bytes accessed | tf_op | source)
XLA Modules:
  0.0 315.7 jit_solution(17407521610609712369)
XLA Ops:
  0.6 0.8 pad.8
  1.4 0.7 pad_maximum_fusion
  2.1 0.7 pad_maximum_fusion.1
  2.8 0.6 select_maximum_fusion.gb_ref.refs_2_
  3.4 0.9 broadcast_in_dim.4.switch_ref
  4.3 139.1 %forward_block.1 = (bf16[1932,128]{1,0:T(8,128)(2,1)}, f32[6,8,128]{2,1,0:T(8,128)}, f32[592,128]{1,0:T(8,128)}, f32[6,4,496,128]{3,2,1,0:T(8,128)}, bf16[6,4,49...) custom-call(s32[6]{0:T(128)} %group_ref.1, s32[592,1]{1,0:T(8,128)} %broadcast_in_dim.4.switch_ref, ...), custom_call_target="tpu_custom_call" | custom-call | tf_op jit(solution)/shard_map/forward_block/pallas_call | solution.py:1022
  143.4 0.0 copy-start
  143.4 163.3 %backward_block.1 = (bf16[1932,128]{1,0:T(8,128)(2,1)}, f32[6,8,128]{2,1,0:T(8,128)}, f32[3,9,64,128]{3,2,1,0:T(8,128)}, f32[3,9,64,128]{3,2,1,0:T(8,128)}) custom-call(bf16[1932,128]{1,0:T(8,128)(2,1)} %refs_0_.3, f32[6,8,128]{2,1,0:T(8,128)} %get-tuple-element.19.refs_1_, f32[6,8,128]{2,1,0:T(8,128)} %select_maximum_fusion.gb_ref.refs_2_, ...), custom_call_target="tpu_custom_call" | custom-call | tf_op jit(solution)/shard_map/backward_block/pallas_call | solution.py:1105
  306.7 0.8 fusion
  307.5 0.6 copy_bitcast_fusion
  308.1 0.6 copy_bitcast_fusion.2
  308.7 0.0 copy-done
  308.7 0.8 copy.31
  309.5 1.8 copy.32
  311.3 2.2 copy.33
  313.5 2.2 copy.34
  (2 shorter events, 0.0 us)
Async XLA Ops:
  143.4 165.3 %copy-start = (bf16[1932,128]{1,0:T(8,128)(2,1)S(1)}, bf16[1932,128]{1,0:T(8,128)(2,1)}, u32[]{:S(2)}) copy-start(bf16[1932,128]{1,0:T(8,128)(2,1)} %get-tuple-element.44) | copy-start | bytes 1483780

commit v7 on v6

--- a/solution.py
+++ b/solution.py
@@ -920,8 +920,9 @@
             part[...] = total
 
         def to_core(spot):
+            which = spot if spot < 4 else pl.ds(4, 4)
             return remote(
-                core_out.at[side, spot], core_in.at[side, spot],
+                core_out.at[side, which], core_in.at[side, which],
                 core_s.at[side, spot], core_r.at[side, spot], partner,
             )
 
@@ -937,13 +938,16 @@
             input_grad(spot % 4, far_base if spot < 4 else own_base)
             core_out[side, spot] = part[:, other_lanes].astype(BF16)
             keep[spot] = part[:, own_lanes]
-            to_core(spot).start()
+            if spot < 4:
+                to_core(spot).start()
             if 2 <= spot < 6:
                 send_across(spot - 2)
             if inside and spot == 3:
                 for step in scatter.order()[2:-1]:
                     scatter_forward(step)
 
+        to_core(4).start()
+
         @pl.when(jnp.logical_not(last))
         def _():
             kernel_grad()
@@ -962,7 +966,8 @@
             pass
 
         def arrived(q):
-            to_core(4 + q).wait_recv()
+            if q == 0:
+                to_core(4).wait_recv()
             to_far(q).wait_recv()
             return keep[4 + q] + core_in[side, 4 + q].astype(F32) + x_in[side, q].astype(F32)
 
@@ -987,7 +992,7 @@
                     scatter.forward(turn, scatter.order()[q])
                 grad_ref[q] = arrived(q)
 
-        for spot in range(8):
+        for spot in range(5):
             to_core(spot).wait_send()
         for q in range(4):
             to_far(q).wait_send()

time: 316 us -> 313 us (level)
  Pallas kernels: 302 us -> 298 us
    pallas_call x1, Pallas kernels: 163 us -> 159 us  [backward_block(): pl.pallas_call(functools.partial(backward_kernel, inside, layers, rows, c...]
where the time goes in v7:
time: 313 us; the launch traced here: 311 us
  Pallas kernels  298 us (95%)
  local copies, waits for them, and re-layouts  10.6 us (3%)
    pallas_call x1, Pallas kernels, backward_block(): pl.pallas_call(functools.partial(backward_kernel, inside, layers, rows, c...  159 us
    pallas_call x1, Pallas kernels, forward_block(): pl.pallas_call(functools.partial(forward_kernel, inside, layers, rows, co...  139 us
    unnamed x8, local copies, waits for them, and re-layouts  8.14 us

profile of v7, /device:TPU:9, one launch (start us, length us, event | category | flops | bytes accessed | tf_op | source)
XLA Modules:
  0.0 311.4 jit_solution(4648067059295915145)
XLA Ops:
  0.6 0.8 pad.8
  1.4 0.7 pad_maximum_fusion
  2.1 0.7 pad_maximum_fusion.1
  2.8 0.6 select_maximum_fusion.gb_ref.refs_2_
  3.4 0.9 broadcast_in_dim.4.switch_ref
  4.3 139.1 %forward_block.1 = (bf16[1932,128]{1,0:T(8,128)(2,1)}, f32[6,8,128]{2,1,0:T(8,128)}, f32[592,128]{1,0:T(8,128)}, f32[6,4,496,128]{3,2,1,0:T(8,128)}, bf16[6,4,49...) custom-call(s32[6]{0:T(128)} %group_ref.1, s32[592,1]{1,0:T(8,128)} %broadcast_in_dim.4.switch_ref, ...), custom_call_target="tpu_custom_call" | custom-call | tf_op jit(solution)/shard_map/forward_block/pallas_call | solution.py:1027
  143.4 0.0 copy-start
  143.4 159.0 %backward_block.1 = (bf16[1932,128]{1,0:T(8,128)(2,1)}, f32[6,8,128]{2,1,0:T(8,128)}, f32[3,9,64,128]{3,2,1,0:T(8,128)}, f32[3,9,64,128]{3,2,1,0:T(8,128)}) custom-call(bf16[1932,128]{1,0:T(8,128)(2,1)} %refs_0_.3, f32[6,8,128]{2,1,0:T(8,128)} %get-tuple-element.19.refs_1_, f32[6,8,128]{2,1,0:T(8,128)} %select_maximum_fusion.gb_ref.refs_2_, ...), custom_call_target="tpu_custom_call" | custom-call | tf_op jit(solution)/shard_map/backward_block/pallas_call | solution.py:1110
  302.5 0.8 fusion
  303.2 0.6 copy_bitcast_fusion
  303.8 0.6 copy_bitcast_fusion.2
  304.4 0.0 copy-done
  304.4 0.8 copy.31
  305.2 1.8 copy.32
  307.0 2.2 copy.33
  309.2 2.2 copy.34
  (2 shorter events, 0.0 us)
Async XLA Ops:
  143.4 161.0 %copy-start = (bf16[1932,128]{1,0:T(8,128)(2,1)S(1)}, bf16[1932,128]{1,0:T(8,128)(2,1)}, u32[]{:S(2)}) copy-start(bf16[1932,128]{1,0:T(8,128)(2,1)} %get-tuple-element.44) | copy-start | bytes 1483780

commit v8 on v7

--- a/solution.py
+++ b/solution.py
@@ -109,10 +109,12 @@
 
 
 def greet(peers):
-    barrier = pltpu.get_barrier_semaphore()
     for peer in peers:
-        pl.semaphore_signal(barrier, inc=1, device_id=peer, device_id_type=MESH)
-    pl.semaphore_wait(barrier, len(peers))
+        pl.semaphore_signal(pltpu.get_barrier_semaphore(), inc=1, device_id=peer, device_id_type=MESH)
+
+
+def meet(peers):
+    pl.semaphore_wait(pltpu.get_barrier_semaphore(), len(peers))
 
 
 def remote(src, dst, send, recv, peer):
@@ -430,7 +432,12 @@
     def at(low, size, spot):
         return yext[low : low + size, spot * LANE : (spot + 1) * LANE]
 
-    greet([partner, across, diagonal] + row_peers(rows))
+    everyone = [partner, across, diagonal] + row_peers(rows)
+    greet(everyone)
+    split_planes(v_ref, wide, count)
+    for q in range(4):
+        raw[0, q, :, own_lanes] = plane(wide, q).astype(BF16)
+    meet(everyone)
     if inside:
         own_rows = gather.rows_of(0, gather.low)
         for layer in range(layers):
@@ -445,9 +452,6 @@
                 gather.start(layer)
     else:
         load(0).start()
-    split_planes(v_ref, wide, count)
-    for q in range(4):
-        raw[0, q, :, own_lanes] = plane(wide, q).astype(BF16)
     to_core(0).start()
     for k in range(len(pieces)):
         to_far(0, k).start()
@@ -731,6 +735,8 @@
         slot = lax.rem(turn, 3)
         return pltpu.make_async_copy(dk.at[slot], wgrad_refs[0].at[layers - 1 - turn], out_sem.at[slot])
 
+    everyone = [partner, across] + row_peers(rows)
+    greet(everyone)
     for turn in range(2):
         for which in range(3):
             load(turn, which).start()
@@ -739,7 +745,6 @@
     split_planes(g_ref, wide, count)
     gext[:EDGE, :] = jnp.zeros((EDGE, 4 * LANE), F32)
     gext[EDGE + padded :, :] = jnp.zeros((EDGE, 4 * LANE), F32)
-    greet([partner, across] + row_peers(rows))
     load(0, 0).wait()
     partial[...] = jnp.zeros_like(partial)
 
@@ -999,6 +1004,7 @@
 
     for q in range(4):
         begin(0, q, plane(wide, q))
+    meet(everyone)
     each(layers, layer_step)
     for q in range(4):
         set_plane(wide, q, 0, grad_ref[q])

time: 313 us -> 311 us (level)
  no operation moved by 1% of the time
where the time goes in v8:
time: 311 us
  Pallas kernels  298 us (96%)
  local copies, waits for them, and re-layouts  10.6 us (3%)
    pallas_call x1, Pallas kernels, backward_block(): pl.pallas_call(functools.partial(backward_kernel, inside, layers, rows, c...  159 us
    pallas_call x1, Pallas kernels, forward_block(): pl.pallas_call(functools.partial(forward_kernel, inside, layers, rows, co...  139 us
    unnamed x8, local copies, waits for them, and re-layouts  8.14 us

profile of v8, /device:TPU:9, one launch (start us, length us, event | category | flops | bytes accessed | tf_op | source)
XLA Modules:
  0.0 310.8 jit_solution(11362732724856425238)
XLA Ops:
  0.6 0.8 pad.8
  1.4 0.7 pad_maximum_fusion
  2.1 0.7 pad_maximum_fusion.1
  2.8 0.6 select_maximum_fusion.gb_ref.refs_2_
  3.4 0.9 broadcast_in_dim.4.switch_ref
  4.3 139.1 %forward_block.1 = (bf16[1932,128]{1,0:T(8,128)(2,1)}, f32[6,8,128]{2,1,0:T(8,128)}, f32[592,128]{1,0:T(8,128)}, f32[6,4,496,128]{3,2,1,0:T(8,128)}, bf16[6,4,49...) custom-call(s32[6]{0:T(128)} %group_ref.1, s32[592,1]{1,0:T(8,128)} %broadcast_in_dim.4.switch_ref, ...), custom_call_target="tpu_custom_call" | custom-call | tf_op jit(solution)/shard_map/forward_block/pallas_call | solution.py:1033
  143.4 0.0 copy-start
  143.4 158.5 %backward_block.1 = (bf16[1932,128]{1,0:T(8,128)(2,1)}, f32[6,8,128]{2,1,0:T(8,128)}, f32[3,9,64,128]{3,2,1,0:T(8,128)}, f32[3,9,64,128]{3,2,1,0:T(8,128)}) custom-call(bf16[1932,128]{1,0:T(8,128)(2,1)} %refs_0_.3, f32[6,8,128]{2,1,0:T(8,128)} %get-tuple-element.19.refs_1_, f32[6,8,128]{2,1,0:T(8,128)} %select_maximum_fusion.gb_ref.refs_2_, ...), custom_call_target="tpu_custom_call" | custom-call | tf_op jit(solution)/shard_map/backward_block/pallas_call | solution.py:1116
  301.9 0.8 fusion
  302.7 0.6 copy_bitcast_fusion
  303.3 0.6 copy_bitcast_fusion.2
  303.9 0.0 copy-done
  303.9 0.8 copy.31
  304.7 1.8 copy.32
  306.5 2.2 copy.33
  308.7 2.2 copy.34
  (2 shorter events, 0.0 us)
Async XLA Ops:
  143.4 160.5 %copy-start = (bf16[1932,128]{1,0:T(8,128)(2,1)S(1)}, bf16[1932,128]{1,0:T(8,128)(2,1)}, u32[]{:S(2)}) copy-start(bf16[1932,128]{1,0:T(8,128)(2,1)} %get-tuple-element.44) | copy-start | bytes 1483780
